TPU v7x, 256 devices: a whole 4x4x8 slice. The times are simulated.
256 devices in a mesh: lat: 32 (over z, x_hi, core), lon: 8 (over x_lo, y).
Axes of the slice: x: 4 (x_hi: 2, x_lo: 2; x = x_hi * 2 + x_lo), y: 4, z: 8, core: 2. Of those that a mesh axis runs over, the one named last changes fastest.
Arguments:
- row_signs: int32 [4, 4, 512], P(None, None, 'lat'), may hold values from 0 to 1
- col_signs: int32 [4, 4, 3600], P(None, None, 'lon'), may hold values from 0 to 1
- spread: float32 [4, 4, 512, 3600], P(None, None, 'lat', 'lon'), may hold values from 0.5 to 2
- east_wind: float32 [4, 512, 3600], P(None, 'lat', 'lon'), may hold values from -4 to 4
- north_wind: float32 [4, 512, 3600], P(None, 'lat', 'lon'), may hold values from -4 to 4
- cutoffs: int32 [512], P('lat'), may hold values from 1 to 256, as said below
Outputs:
- tangent: float32 [4, 4, 512, 3600], P(None, None, 'lat', 'lon')
- probe_diag: float32 [4, 4, 512, 3600], P(None, None, 'lat', 'lon')
Inputs may be any that keep to these rules, and one draw needn't show every extreme that they name: Rows within 32 rows of either pole have cutoffs from 1 to 128, the row next to each pole exactly 1; all other rows have 256, where the filter leaves them unchanged.
All inputs are finite; a program needn't handle non-finite values.
Results may differ from a plain program's by a relative error of at most 0.000082.
Values sent between devices are 32-bit elements; how exact they have to be, the bound alone decides.
A program may use at most 128 MiB of HBM per device.

v0:
```python
import jax
import jax.numpy as jnp
from jax import lax
from jax.sharding import PartitionSpec as P

KTOP = 256


time_step = 0.5
coupling = 0.5
mixing = 0.2
metric_cap = 4.0


def partner_2(value, axis, apart):
    return lax.ppermute(value, axis, [(i, i ^ 1 << apart) for i in range(lax.axis_size(axis))])


def extended(cells, sides, width):
    for axis, dim in sides:
        count = lax.axis_size(axis)
        head = lax.slice_in_dim(cells, 0, width, axis=dim)
        tail = lax.slice_in_dim(cells, cells.shape[dim] - width, cells.shape[dim], axis=dim)
        cells = jnp.concatenate(
            [
                lax.ppermute(tail, axis, [(i, (i + 1) % count) for i in range(count)]),
                cells,
                lax.ppermute(head, axis, [((i + 1) % count, i) for i in range(count)]),
            ],
            axis=dim,
        )
    return cells


def metric_rows(first_row, count, total_rows):
    rows = first_row + jnp.arange(count, dtype=jnp.int32)
    latitude = jnp.pi * ((rows.astype(jnp.float32) + 0.5) / total_rows - 0.5)
    return jnp.minimum(1.0 / jnp.cos(latitude), metric_cap)


def tendency(padded, east_wind, north_wind, metric):
    center = padded[:, :, 1:-1, 1:-1]
    along_x = 0.5 * (padded[:, :, 1:-1, 2:] - padded[:, :, 1:-1, :-2]) * metric[:, None]
    along_y = 0.5 * (padded[:, :, 2:, 1:-1] - padded[:, :, :-2, 1:-1])
    advect = east_wind * along_x + north_wind * along_y
    linked = jnp.stack([along_x[2], along_y[2], along_x[0] + along_y[1], jnp.zeros_like(center[3])])
    above = jnp.concatenate([center[:, :1], center[:, :-1]], axis=1)
    below = jnp.concatenate([center[:, 1:], center[:, -1:]], axis=1)
    return -advect - coupling * linked + mixing * (above - 2.0 * center + below)


def mode_table(first_col, count, total_cols, modes):
    cols = first_col + jnp.arange(count, dtype=jnp.int32)
    waves = jnp.arange(1, modes + 1, dtype=jnp.int32)
    phase = cols[:, None] * waves[None, :] % total_cols
    angle = 2.0 * jnp.pi / total_cols * phase.astype(jnp.float32)
    return jnp.concatenate([jnp.cos(angle), jnp.sin(angle)], axis=1)


def removal_mask(cutoffs, modes):
    waves = jnp.arange(1, modes + 1, dtype=jnp.int32)
    high = (waves[None, :] > cutoffs[:, None]).astype(jnp.float32)
    return jnp.concatenate([high, high], axis=1)


def across_pole(pair, lanes):
    return partner_2(pair, "lon", lanes.bit_length() - 2)


def per_device(row_signs, col_signs, spread, east_wind, north_wind, cutoffs):
    lanes = lax.axis_size("lon")
    bands = lax.axis_size("lat")
    rows = spread.shape[2]
    cols = spread.shape[3]
    total_rows = rows * bands
    total_cols = cols * lanes
    modes = KTOP
    band = lax.axis_index("lat")
    lane = lax.axis_index("lon")
    is_north = band == 0
    is_south = band == bands - 1
    row_part = (2 * row_signs - 1).astype(jnp.float32)
    col_part = (2 * col_signs - 1).astype(jnp.float32)
    signs = row_part[:, :, :, None] * col_part[:, :, None, :]
    probe = spread * signs
    metric = metric_rows(band * rows, rows, total_rows)
    flip = jnp.array([-1.0, -1.0, 1.0, 1.0], jnp.float32)[:, None, None]
    scaled_mask = removal_mask(cutoffs, modes) * (2.0 / total_cols)
    local_table = mode_table(lane * cols, cols, total_cols, modes)

    def filtered(field):
        full_table = mode_table(0, total_cols, total_cols, modes)
        coef = jnp.einsum(
            "flrj,jk->flrk",
            lax.all_gather(field, "lon", axis=3, tiled=True),
            full_table,
            precision=lax.Precision.HIGHEST,
        )
        return field - jnp.einsum(
            "flrk,jk->flrj", coef * scaled_mask, local_table, precision=lax.Precision.HIGHEST
        )

    padded = extended(probe, (("lat", 2), ("lon", 3)), 1)
    ends = jnp.concatenate([probe[:, :, :1], probe[:, :, -1:]], axis=2)
    partner = across_pole(ends, lanes)
    north_row = jnp.where(is_north, flip * partner[:, :, 0], padded[:, :, 0, 1:-1])
    south_row = jnp.where(is_south, flip * partner[:, :, 1], padded[:, :, -1, 1:-1])
    padded = padded.at[:, :, 0, 1:-1].set(north_row).at[:, :, -1, 1:-1].set(south_row)
    tangent = probe + time_step * filtered(tendency(padded, east_wind, north_wind, metric))
    adjoint_in = filtered(tangent)
    zero_grid = jnp.zeros(padded.shape, jnp.float32)
    unused, pullback = jax.vjp(
        lambda grid: tendency(grid, east_wind, north_wind, metric), zero_grid
    )
    spread_back = pullback(adjoint_in)[0]
    inner = spread_back[:, :, 1:-1, 1:-1]
    north_back = spread_back[:, :, 0, 1:-1]
    south_back = spread_back[:, :, -1, 1:-1]
    west_back = spread_back[:, :, 1:-1, 0]
    east_back = spread_back[:, :, 1:-1, -1]
    blank = jnp.zeros_like(inner)
    lat_part = blank.at[:, :, 0].set(north_back).at[:, :, -1].set(south_back)
    lon_part = blank.at[:, :, :, 0].set(west_back).at[:, :, :, -1].set(east_back)
    returned = extended(jnp.stack([lat_part, lon_part]), (("lat", 3), ("lon", 4)), 1)
    from_above = returned[0, :, :, 0, 1:-1]
    from_below = returned[0, :, :, -1, 1:-1]
    from_west = returned[1, :, :, 1:-1, 0]
    from_east = returned[1, :, :, 1:-1, -1]
    pole_back = across_pole(jnp.stack([north_back, south_back], axis=2), lanes)
    first_add = jnp.where(is_north, flip * pole_back[:, :, 0], from_above)
    last_add = jnp.where(is_south, flip * pole_back[:, :, 1], from_below)
    total_back = inner.at[:, :, 0].add(first_add).at[:, :, -1].add(last_add)
    total_back = total_back.at[:, :, :, 0].add(from_west).at[:, :, :, -1].add(from_east)
    back = tangent + time_step * total_back
    return (tangent, signs * spread * (back - probe))


def solution(mesh):
    return jax.shard_map(
        per_device,
        mesh=mesh,
        in_specs=(
            P(None, None, "lat"),
            P(None, None, "lon"),
            P(None, None, "lat", "lon"),
            P(None, "lat", "lon"),
            P(None, "lat", "lon"),
            P("lat"),
        ),
        out_specs=(P(None, None, "lat", "lon"), P(None, None, "lat", "lon")),
        check_vma=False,
    )
```

profile of v0, /device:TPU:1, one launch (start us, length us, event | category | flops | bytes accessed | tf_op | source)
XLA Modules:
  0.0 798.1 jit_solution(15129534466694210374)
XLA Ops:
  7.2 0.7 add_convert_fusion.1
  7.9 0.8 add_convert_fusion
  8.7 1.2 multiply_multiply_fusion.1
  9.9 0.1 fusion.47
  9.9 4.2 collective-permute-start
  14.2 0.1 pad_maximum_fusion.10
  14.2 0.4 collective-permute-start.4
  14.6 0.9 broadcast_multiply_fusion.2
  15.6 0.6 fusion.48
  16.2 3.5 collective-permute-done.1
  19.6 0.2 pad_maximum_fusion.7
  19.8 1.4 collective-permute-start.2
  21.2 2.3 collective-permute-start.3
  23.5 0.1 pad.99.clone
  23.6 4.2 collective-permute-done.2
  27.7 0.5 pad_maximum_fusion
  28.3 0.1 broadcast_select_fusion.1
  28.4 4.2 scatter.20
  32.6 2.9 scatter.21
  35.5 0.1 fusion.43
  35.7 0.3 fusion.42
  36.0 0.5 fusion.23
  36.5 0.6 fusion.22
  37.1 3.1 copy.89
  40.2 0.1 broadcast_compare_fusion
  40.3 2.0 fusion.30
  42.3 16.9 %fusion.9 = (f32[3600,256]{1,0:T(8,128)}, f32[3600,256]{1,0:T(8,128)}) fusion(s32[256]{0:T(256)S(1)} %iota_add_fusion.1), kind=kLoop, calls=%fused_computation.12 | loop fusion | flops 8294400 | bytes 7373824 | tf_op jit(solution)/shard_map/cos | solution.py:57
  59.2 275.7 %all-gather.3.cloned.1.call-done = f32[4,4,16,3600]{2,1,0,3:T(4,128)} async-done(((f32[4,4,16,450]{2,1,0,3:T(4,128)}), f32[4,4,16,3600]{2,1,0,3:T(4,128)}) %all-gather.3.cloned.1.call-update) | async-done | bytes 3686416 | tf_op jit(solution)/shard_map/all_gather | solution.py:95
  334.8 60.0 %fusion.13 = f32[4,4,16,512]{3,2,1,0:T(8,128)S(1)} fusion(f32[3600,256]{1,0:T(8,128)} %get-tuple-element.162, f32[3600,256]{1,0:T(8,128)} %get-tuple-element.161, f32[4,4,16,3600]{2,1,0,3:T(4,128)} %all-gather.3.cloned.1.call-done, f32[16,512]{1,0:T(8,128)S(1)} %add_select_fusion.2), kind=kOutput, calls=%fused_computation.18 | convolution fusion | flops 5664284672 | bytes 11616256 | tf_op jit(solution)/shard_map/flrj,jk->flrk/dot_general | solution.py:93
  394.9 1.1 fusion.12
  395.9 3.1 copy.91
  399.0 291.3 %all-gather.5.cloned.1.call-done = f32[4,4,16,3600]{2,1,0,3:T(4,128)} async-done(((f32[4,4,16,450]{2,1,0,3:T(4,128)}), f32[4,4,16,3600]{2,1,0,3:T(4,128)}) %all-gather.5.cloned.1.call-update) | async-done | bytes 3686416 | tf_op jit(solution)/shard_map/all_gather | solution.py:95
  690.3 60.2 %fusion.16 = f32[4,4,16,512]{3,2,1,0:T(8,128)S(1)} fusion(f32[3600,256]{1,0:T(8,128)} %get-tuple-element.162, f32[3600,256]{1,0:T(8,128)} %get-tuple-element.161, f32[4,4,16,3600]{2,1,0,3:T(4,128)} %all-gather.5.cloned.1.call-done, f32[16,512]{1,0:T(8,128)S(1)} %add_select_fusion.2), kind=kOutput, calls=%fused_computation.19 | convolution fusion | flops 5664284672 | bytes 11616256 | tf_op jit(solution)/shard_map/flrj,jk->flrk/dot_general | solution.py:93
  750.5 1.1 negate_multiply_fusion
  751.6 0.1 fusion.45
  751.8 0.4 fusion.40
  752.2 0.1 pad_add_fusion.2
  752.3 0.4 add_bitcast_fusion
  752.6 1.9 pad_add_fusion
  754.5 0.8 pad_bitcast_fusion.1
  755.4 0.9 pad_bitcast_fusion
  756.2 1.8 scatter.25
  758.0 2.7 scatter.29
  760.7 1.3 pad_maximum_fusion.8
  762.0 0.8 collective-permute-start.7
  762.8 2.8 collective-permute-start.6
  765.5 0.1 pad_maximum_fusion.11
  765.6 0.4 collective-permute-start.5
  766.0 2.1 slice.439
  768.1 0.5 collective-permute-done.6
  768.6 0.1 copy-done.4
  768.7 2.1 pad_maximum_fusion.1
  770.8 0.6 copy-done.5
  771.4 0.8 fusion.34
  772.2 1.8 scatter-add.14
  774.0 1.1 fusion.35
  775.1 1.8 scatter-add.15
  776.9 3.6 collective-permute-start.9
  780.4 1.0 fusion.33
  781.5 1.6 scatter-add.16
  783.1 2.1 collective-permute-done.9
  785.2 1.0 fusion.32
  786.2 2.7 scatter-add.19
  788.9 2.1 subtract_multiply_fusion
  (36 shorter events, 0.3 us)
Async XLA Ops:
  7.2 21.1 %copy-start.6 = (f32[4]{0:T(128)S(1)}, f32[4]{0:T(128)}, u32[]{:S(2)}) copy-start(f32[4]{0:T(128)} %constant.326.clone) | copy-start | bytes 52
  7.2 327.6 %all-gather.3.cloned.1.call-start = ((), (), s32[]{:S(2)}) async-start(), calls=%async_computation | async-start | bytes 33177600 | tf_op jit(solution)/shard_map/all_gather | solution.py:95
  8.7 5.5 copy-start.3
  9.9 6.2 collective-permute-start
  14.2 5.5 collective-permute-start.1
  14.2 14.0 %collective-permute-start.4 = (f32[4,4,2,450]{3,2,1,0:T(2,128)S(1)}, f32[4,4,2,450]{3,2,1,0:T(2,128)S(1)}, u32[]{:S(2)}, u32[]{:S(2)}) collective-permute-start(f32[4,4,2,450]{3,2,1,0:T(2,128)S(1)} %pad_maximum_fusion.10), channel_id=1, source_target_pairs={{0,4},{1,5},{2,6},{3,7},{4,0},{5,1},{6,2},{7,3},{8,12},{9,13},{10,... | collective-permute-start | bytes 172808 | tf_op jit(solution)/shard_map/ppermute | solution.py:16
  19.8 8.0 collective-permute-start.2
  21.2 6.6 collective-permute-start.3
  28.2 8.3 %copy-start.1 = (f32[4,16,450]{2,1,0:T(8,128)S(1)}, f32[4,16,450]{2,1,0:T(8,128)}, u32[]{:S(2)}) copy-start(f32[4,16,450]{2,1,0:T(8,128)} %param.30) | copy-start | bytes 345604
  37.1 3.2 copy-start.8
  40.2 650.1 %all-gather.5.cloned.1.call-start = ((), (), s32[]{:S(2)}) async-start(), calls=%async_computation.1 | async-start | bytes 33177600 | tf_op jit(solution)/shard_map/all_gather | solution.py:95
  395.9 393.0 %copy-start = (f32[4,4,16,450]{3,2,1,0:T(8,128)}, f32[4,4,16,450]{3,2,1,0:T(8,128)S(1)}, u32[]{:S(2)}) copy-start(f32[4,4,16,450]{3,2,1,0:T(8,128)S(1)} %fusion.12) | copy-start | bytes 1382404
  750.5 1.3 copy-start.2
  750.5 1.3 copy-start.7
  762.0 6.1 collective-permute-start.7
  762.8 5.8 collective-permute-start.6
  765.6 5.2 collective-permute-start.5
  768.1 0.6 copy-start.4
  770.8 9.6 %collective-permute-start.8 = (f32[2,4,4,18,1]{4,3,2,1,0:T(8,128)}, f32[2,4,4,18,1]{4,3,2,1,0:T(8,128)}, u32[]{:S(2)}, u32[]{:S(2)}) collective-permute-start(f32[2,4,4,18,1]{4,3,2,1,0:T(8,128)} %get-tuple-element.131), channel_id=1, source_target_pairs={{0,1},{1,2},{2,3},{3,4},{4,5},{5,6},{6,7},{7,0},{8,9},{9,10},{10,1... | collective-permute-start | bytes 6920 | tf_op jit(solution)/shard_map/ppermute | solution.py:26
  770.8 0.6 copy-start.5
  776.9 8.3 %collective-permute-start.9 = (f32[2,4,4,18,1]{4,3,2,1,0:T(8,128)S(1)}, f32[2,4,4,18,1]{4,3,2,1,0:T(8,128)S(1)}, u32[]{:S(2)}, u32[]{:S(2)}) collective-permute-start(f32[2,4,4,18,1]{4,3,2,1,0:T(8,128)S(1)} %get-tuple-element.130), channel_id=1, source_target_pairs={{1,0},{2,1},{3,2},{4,3},{5,4},{6,5},{7,6},{0,7},{9,8},{10,9},{11,1... | collective-permute-start | bytes 6920 | tf_op jit(solution)/shard_map/ppermute | solution.py:28
Sparse Core Ops, SparseCore 0:
  40.3 294.5 all-gather.2
  399.1 291.0 all-gather.4
where the time goes:
time: 812 us; the launch traced here: 798 us
  waiting for transfers between devices  577 us (71%)
  matrix products  122 us (15%)
  other arithmetic  36.7 us (5%)
  local copies, waits for them, and re-layouts  31.4 us (4%)
  starting transfers between devices  15.8 us (2%)
  between operations  14.6 us (2%)
    all_gather x2, waiting for transfers between devices, filtered(): lax.all_gather(field, 'lon', axis=3, tiled=True)  567 us
    dot_general x2, matrix products, filtered(): jnp.einsum('flrj,jk->flrk', lax.all_gather(field, 'lon', axis=3, tiled=Tr...  120 us
    cos x2, other arithmetic, mode_table(): return jnp.concatenate([jnp.cos(angle), jnp.sin(angle)], axis=1)  18.8 us
  transfers between devices with their start and end apart: 12, of which 6 were waited for; matrix products, arithmetic and copies ran while one was open for 4% of the time, Pallas kernels for 0%

commit v1 on v0

v1 whole, which is shorter than its diff:
```python
import functools

import jax
import jax.numpy as jnp
import ml_dtypes
import numpy as np
from jax import lax
from jax.experimental import pallas as pl
from jax.experimental.pallas import tpu as pltpu
from jax.sharding import PartitionSpec as P

KTOP = 256
POLAR = 32
RANK = 128
ROWS = 16
COLS = 450
WIDE = 512
LANES = 8
FIELDS = 4
LEV = 4
PAIRS = FIELDS * LEV

time_step = 0.5
coupling = 0.5
mixing = 0.2
metric_cap = 4.0

MESH = pl.DeviceIdType.MESH
F32 = jnp.float32
BF16 = jnp.bfloat16


def split_table(table):
    high = table.astype(ml_dtypes.bfloat16)
    low = (table - high.astype(np.float64)).astype(ml_dtypes.bfloat16)
    return high, low


@functools.lru_cache(None)
def mode_factors():
    total = COLS * LANES
    size = COLS + 2
    place = np.arange(size, dtype=np.float64)
    width = (KTOP + 0.5) / total
    diag = ((size - 1 - 2 * place) / 2) ** 2 * np.cos(2 * np.pi * width)
    side = place[1:] * (size - place[1:]) / 2
    vectors = np.linalg.eigh(np.diag(diag) + np.diag(side, 1) + np.diag(side, -1))[1]
    basis = vectors[:, ::-1][:, :RANK]
    basis = basis * np.where(basis[size // 2] < 0, -1.0, 1.0)
    waves = np.arange(1, KTOP + 1)
    factors = []
    for lane in range(LANES):
        cols = lane * COLS - 1 + np.arange(size)
        angle = 2 * np.pi / total * (cols[:, None] * waves[None, :] % total)
        factors.append(basis.T @ np.concatenate([np.cos(angle), np.sin(angle)], axis=1))
    factors = np.round(np.concatenate(factors, axis=0) * 2.0**22) / 2.0**22
    wide = np.zeros((RANK, WIDE))
    wide[:, : COLS + 1] = basis[1:].T
    wide[:, WIDE - 1] = basis[0]
    wide = np.round(wide * 2.0**26) / 2.0**26
    return split_table(wide) + split_table(factors)


@functools.lru_cache(None)
def half_metric(bands):
    total = bands * ROWS
    rows = np.clip(np.arange(bands)[:, None] * ROWS - 8 + np.arange(32)[None, :], 0, total - 1)
    metric = np.minimum(1.0 / np.cos(np.pi * ((rows + 0.5) / total - 0.5)), metric_cap)
    return np.broadcast_to((0.5 * metric).astype(np.float32)[:, :, None], (bands, 32, 128)).copy()


def dot_rows(a, b):
    return lax.dot_general(a, b, (((1,), (1,)), ((), ())), preferred_element_type=F32)


def dot_cols(a, b):
    return lax.dot_general(a, b, (((1,), (0,)), ((), ())), preferred_element_type=F32)


def dot3(dot, x, high, low):
    xh = x.astype(BF16)
    xl = (x - xh.astype(F32)).astype(BF16)
    return dot(xh, high) + dot(xl, high) + dot(xh, low)


def roll(x, shift, axis):
    return pltpu.roll(x, shift % x.shape[axis], axis)


def roll_blocks(x, shift):
    return roll(x.reshape(x.shape[0] * x.shape[1], x.shape[2]), shift, 1).reshape(x.shape)


def fold(x):
    while x.shape[0] > 1:
        half = x.shape[0] // 2
        x = x[:half] + roll_blocks(x[half:], 2 * half)
    return x


def kernel(
    bands, spread, east, north, rs, cs, cut, metric, qh_in, ql_in, rh_in, rl_in, tan_out, diag_out,
    spread_v, east_v, north_v, rs_v, cs_v, cut_s, hm, qh, ql, rh, rl,
    grid, er, hr, hc, cp, hcol, ybuf, yr, zbuf, zr, bz,
    tend, proj_p, proj_t, edge_t, edge_proj, adj, gy, tan_v, diag_v,
    in_sem, row_send, row_recv, cor_send, cor_recv, col_send, col_recv,
    y_send, y_recv, z_send, z_recv, b_send, b_recv, out_sem,
):
    b = lax.axis_index("lat")
    i = lax.axis_index("lon")
    caps = POLAR // ROWS
    is_north = b == 0
    is_south = b == bands - 1
    polar = jnp.logical_or(b < caps, b >= bands - caps)
    above_polar = jnp.logical_or(b <= caps, is_south)
    below_polar = jnp.logical_or(b >= bands - caps - 1, is_north)
    across = lax.rem(i + LANES // 2, LANES)
    west = lax.rem(i + LANES - 1, LANES)
    east_lane = lax.rem(i + 1, LANES)
    nb = jnp.where(is_north, 0, b - 1)
    nl = jnp.where(is_north, across, i)
    sb = jnp.where(is_south, bands - 1, b + 1)
    sl = jnp.where(is_south, across, i)
    slot_n = jnp.where(is_north, 0, 1)
    slot_s = jnp.where(is_south, 1, 0)
    first, last = 0, LANES - 1

    def plus(lane, d):
        return lax.rem(lane + d, LANES)

    loads = [
        pltpu.make_async_copy(spread, spread_v, in_sem.at[0]),
        pltpu.make_async_copy(rs, rs_v, in_sem.at[1]),
        pltpu.make_async_copy(cs, cs_v, in_sem.at[2]),
        pltpu.make_async_copy(east, east_v, in_sem.at[3]),
        pltpu.make_async_copy(north, north_v, in_sem.at[4]),
        pltpu.make_async_copy(metric.at[b], hm, in_sem.at[5]),
        pltpu.make_async_copy(cut, cut_s, in_sem.at[6]),
        pltpu.make_async_copy(qh_in, qh, in_sem.at[7]),
        pltpu.make_async_copy(ql_in, ql, in_sem.at[8]),
    ]
    table_loads = [
        pltpu.make_async_copy(rh_in, rh, in_sem.at[9]),
        pltpu.make_async_copy(rl_in, rl, in_sem.at[10]),
    ]
    for load in loads:
        load.start()

    @pl.when(polar)
    def _():
        for load in table_loads:
            load.start()

    barrier = pltpu.get_barrier_semaphore()

    def greet(lat, lon):
        pl.semaphore_signal(barrier, inc=1, device_id=(lat, lon), device_id_type=MESH)

    greet(nb, nl)
    greet(sb, sl)
    greet(b, west)
    greet(b, east_lane)
    greet(nb, plus(nl, 1))
    greet(nb, plus(nl, LANES - 1))
    greet(sb, plus(sl, 1))
    greet(sb, plus(sl, LANES - 1))

    @pl.when(polar)
    def _():
        @pl.loop(1, LANES)
        def _(d):
            greet(b, plus(i, d))

    @pl.when(jnp.logical_and(above_polar, jnp.logical_not(is_north)))
    def _():
        greet(nb, last)

    @pl.when(jnp.logical_and(below_polar, jnp.logical_not(is_south)))
    def _():
        greet(sb, first)

    for load in loads[:5]:
        load.wait()
    grid[:, 8:24, 384:512] = jnp.zeros((PAIRS + 2 * LEV, ROWS, 128), F32)
    row_part = jnp.concatenate([rs_v[f] for f in range(FIELDS)], axis=0)
    row_part = (2 * row_part - 1).astype(F32).T
    for f in range(FIELDS):
        col_part = (2 * cs_v[f] - 1).astype(F32)
        for l in range(LEV):
            n = f * LEV + l
            grid[n, 8:24, 0:COLS] = spread_v[f, l] * (row_part[:, n : n + 1] * col_part[l : l + 1, :])
    for l in range(LEV):
        grid[PAIRS + l, 8:24, 0:COLS] = east_v[l]
        grid[PAIRS + LEV + l, 8:24, 0:COLS] = north_v[l]

    for s, (near, far) in enumerate(((8, 9), (23, 22))):
        for f in range(FIELDS + 2):
            er[s, f if f < FIELDS else f + FIELDS] = grid[f * LEV : (f + 1) * LEV, near, :]
        for f in range(FIELDS):
            er[s, FIELDS + f] = grid[f * LEV : (f + 1) * LEV, far, :]
    lane128 = lax.broadcasted_iota(jnp.int32, (1, 1, 128), 2)
    for s, (start, shift) in enumerate(((0, 0), (384, COLS - 2 - 384))):
        tile = grid[:, 8:24, start : start + 128]
        tile = jnp.where(jnp.logical_and(lane128 >= shift, lane128 < shift + 2), tile, 0.0)
        packed = fold(tile[:PAIRS]) + roll_blocks(fold(tile[PAIRS:]), 2 * PAIRS)
        cp[s] = roll_blocks(packed, -shift)[0]

    pl.semaphore_wait(
        barrier,
        8
        + jnp.where(polar, LANES - 1, 0)
        + jnp.where(jnp.logical_and(polar, jnp.logical_and(i == first, jnp.logical_not(is_north))), LANES, 0)
        + jnp.where(jnp.logical_and(polar, jnp.logical_and(i == last, jnp.logical_not(is_south))), LANES, 0),
    )

    def remote(src, dst, send, recv, lat, lon):
        return pltpu.make_async_remote_copy(
            src_ref=src, dst_ref=dst, send_sem=send, recv_sem=recv, device_id=(lat, lon), device_id_type=MESH
        )

    halo_sends = [
        remote(er.at[0], hr.at[slot_n], row_send.at[0], row_recv.at[slot_n], nb, nl),
        remote(er.at[1], hr.at[slot_s], row_send.at[1], row_recv.at[slot_s], sb, sl),
        remote(cp.at[0], hcol.at[1], col_send.at[0], col_recv.at[1], b, west),
        remote(cp.at[1], hcol.at[0], col_send.at[1], col_recv.at[0], b, east_lane),
    ]
    for s, (slot, lat, lon) in enumerate(((slot_n, nb, nl), (slot_s, sb, sl))):
        halo_sends.append(
            remote(
                er.at[s, 0:FIELDS, :, 384:512], hc.at[slot, 0], cor_send.at[s, 0], cor_recv.at[slot, 0],
                lat, plus(lon, 1),
            )
        )
        halo_sends.append(
            remote(
                er.at[s, 0:FIELDS, :, 0:128], hc.at[slot, 1], cor_send.at[s, 1], cor_recv.at[slot, 1],
                lat, plus(lon, LANES - 1),
            )
        )
    for send in halo_sends:
        send.start()

    lane512 = lax.broadcasted_iota(jnp.int32, (1, WIDE), 1)
    own_cols = lane512 < COLS

    def y_copy(q, o):
        return remote(ybuf.at[q, o], yr.at[q, i], y_send.at[q, o], y_recv.at[q, i], b, o)

    def y_arrival(q, j):
        return remote(ybuf.at[q, j], yr.at[q, j], y_send.at[q, j], y_recv.at[q, j], b, j)

    def send_row_values(q, x):
        y = dot3(dot_rows, jnp.where(own_cols, x, 0.0), qh[...], ql[...])
        y = jnp.swapaxes(y.reshape(PAIRS, ROWS, RANK), 0, 1)
        ybuf[q] = y.reshape(LANES, 2 * PAIRS, RANK)

        @pl.loop(1, LANES)
        def _(d):
            y_copy(q, plus(i, d)).start()

        yr[q, i] = ybuf[q, i]

    def z_copy(q, j):
        return remote(zbuf.at[q, j], zr.at[q, i], z_send.at[q, j], z_recv.at[q, i], b, j)

    def z_arrival(q, j):
        return remote(zbuf.at[q, j], zr.at[q, j], z_send.at[q, j], z_recv.at[q, j], b, j)

    def edge_copy(q, j, s):
        slot, lat = ((slot_n, nb), (slot_s, sb))[s]
        over = (is_north, is_south)[s]
        lon = jnp.where(over, plus(j, LANES // 2), j)
        part = zbuf.at[q, j, PAIRS * s : PAIRS * (s + 1)]
        here = jnp.logical_and(over, lon == i)

        def away():
            return remote(part, bz.at[slot, q], b_send.at[q, j], b_recv.at[slot, q], lat, lon)

        def local():
            return pltpu.make_async_copy(part, bz.at[s, q], b_recv.at[s, q])

        return here, away, local

    def edge_sends(q, act):
        for s, owner in ((0, first), (1, last)):
            @pl.when(i == owner)
            def _():
                @pl.loop(0, LANES)
                def _(j):
                    here, away, local = edge_copy(q, j, s)

                    @pl.when(jnp.logical_not(here))
                    def _():
                        act(away())

                    if act is start_copy:
                        @pl.when(here)
                        def _():
                            local().start()

    def start_copy(copy):
        copy.start()

    def end_copy(copy):
        copy.wait_send()

    def own_rows(q):
        @pl.loop(1, LANES)
        def _(d):
            y_arrival(q, plus(i, d)).wait_recv()

        y = jnp.concatenate([yr[q, j] for j in range(LANES)], axis=1)
        coef = dot3(dot_cols, y, rh[...], rl[...])
        wave = lax.rem(lax.broadcasted_iota(jnp.int32, (PAIRS, 2 * KTOP), 1), KTOP) + 1
        keep = jnp.concatenate(
            [jnp.where(wave > cut_s[2 * i + part], 2.0 / (COLS * LANES), 0.0) for part in range(2)], axis=0
        )
        z = dot3(dot_rows, coef * keep, rh[...], rl[...])
        for j in range(LANES):
            zbuf[q, j] = z[:, j * RANK : (j + 1) * RANK]

        @pl.loop(1, LANES)
        def _(d):
            z_copy(q, plus(i, d)).start()

        edge_sends(q, start_copy)
        zr[q, i] = zbuf[q, i]

    def project(q, out):
        @pl.loop(1, LANES)
        def _(d):
            z_arrival(q, plus(i, d)).wait_recv()

        z = jnp.swapaxes(zr[q].reshape(ROWS, PAIRS, RANK), 0, 1).reshape(PAIRS * ROWS, RANK)
        out[...] = dot3(dot_cols, z, qh[...], ql[...]).reshape(PAIRS, ROWS, WIDE)

    for load in loads[5:]:
        load.wait()

    @pl.when(polar)
    def _():
        send_row_values(0, grid[0:PAIRS, 8:24, :].reshape(PAIRS * ROWS, WIDE))

    for s in range(2):
        remote(er.at[s], hr.at[s], row_send.at[s], row_recv.at[s], nb, nl).wait_recv()
        remote(cp.at[s], hcol.at[s], col_send.at[s], col_recv.at[s], b, west).wait_recv()
        for side in range(2):
            remote(
                er.at[s, 0:FIELDS, :, 0:128], hc.at[s, side], cor_send.at[s, side], cor_recv.at[s, side], nb, nl
            ).wait_recv()

    from_west = roll(hcol[0], 126, 1)
    from_east = roll(hcol[1], COLS - 384, 1)
    lane2 = lax.broadcasted_iota(jnp.int32, (1, 128), 1)
    both = jnp.where(jnp.logical_and(lane2 >= 66, lane2 < 114), from_east, from_west)[None]
    for width in (2, 4, 8):
        both = jnp.concatenate([both, roll_blocks(both, -width)], axis=0)
    both = jnp.concatenate([both, roll_blocks(both, -16), roll_blocks(both, -32)], axis=0)
    in_halo = jnp.logical_or(
        jnp.logical_and(lane128 >= 66, lane128 < 68), lane128 >= 126
    )
    grid[:, 8:24, 384:512] = jnp.where(in_halo, both, grid[:, 8:24, 384:512])

    flips = (-1.0, -1.0, 1.0, 1.0)
    over_pole = (is_north, is_south)
    edge_row = (7, 24)
    inward = (1.0, -1.0)

    def edge_center(s, f):
        tile = hr[s, f][:, 384:512]
        tile = jnp.where(lane2 == 66, roll(hc[s, 1, f], 66, 1), tile)
        tile = jnp.where(lane2 == 127, roll(hc[s, 0, f], 62, 1), tile)
        return jnp.concatenate([hr[s, f][:, 0:384], tile], axis=1)

    edge_probe = []
    for s in range(2):
        centers = [edge_center(s, f) for f in range(FIELDS)]
        edge_probe.append(centers)
        half = jnp.concatenate([hm[edge_row[s] : edge_row[s] + 1, :]] * 4, axis=1)
        turn = jnp.where(over_pole[s], -inward[s], inward[s])
        along_x, along_y = [], []
        for f in range(FIELDS):
            flip = jnp.where(over_pole[s], flips[f], 1.0)
            grid[f * LEV : (f + 1) * LEV, edge_row[s], :] = flip * centers[f]
            along_x.append(half * (roll(centers[f], -1, 1) - roll(centers[f], 1, 1)))
            along_y.append((0.5 * turn) * (flip * er[s, f] - hr[s, FIELDS + f]))
        linked = (along_x[2], along_y[2], along_x[0] + along_y[1], None)
        for f in range(FIELDS):
            mid = centers[f]
            up = jnp.concatenate([mid[0:1], mid[0:3]], axis=0)
            down = jnp.concatenate([mid[1:4], mid[3:4]], axis=0)
            t = -(hr[s, 8] * along_x[f] + hr[s, 9] * along_y[f]) + mixing * (up + down - 2.0 * mid)
            if linked[f] is not None:
                t = t - coupling * linked[f]
            edge_t[s, f] = t

    @pl.loop(0, LEV)
    def _(l):
        lo = jnp.maximum(l - 1, 0)
        hi = jnp.minimum(l + 1, LEV - 1)
        for h in (8, 16):
            half = jnp.concatenate([hm[h : h + 8, :]] * 4, axis=1)
            ew = grid[PAIRS + l, h : h + 8, :]
            nw = grid[PAIRS + LEV + l, h : h + 8, :]
            along_x, along_y = [], []
            for f in range(FIELDS):
                mid = grid[f * LEV + l, h : h + 8, :]
                along_x.append(half * (roll(mid, -1, 1) - roll(mid, 1, 1)))
                along_y.append(0.5 * (grid[f * LEV + l, h + 1 : h + 9, :] - grid[f * LEV + l, h - 1 : h + 7, :]))
            linked = (along_x[2], along_y[2], along_x[0] + along_y[1], None)
            for f in range(FIELDS):
                mid = grid[f * LEV + l, h : h + 8, :]
                mixed = grid[f * LEV + lo, h : h + 8, :] + grid[f * LEV + hi, h : h + 8, :] - 2.0 * mid
                t = -(ew * along_x[f] + nw * along_y[f]) + mixing * mixed
                if linked[f] is not None:
                    t = t - coupling * linked[f]
                tend[f * LEV + l, h - 8 : h, :] = t

    @pl.when(polar)
    def _():
        send_row_values(1, tend[...].reshape(PAIRS * ROWS, WIDE))
        for load in table_loads:
            load.wait()
        own_rows(0)
        own_rows(1)
        project(0, proj_p)
        project(1, proj_t)

    @pl.when(jnp.logical_not(polar))
    def _():
        proj_p[...] = jnp.zeros(proj_p.shape, F32)
        proj_t[...] = jnp.zeros(proj_t.shape, F32)

    for s, wanted in enumerate((above_polar, below_polar)):
        @pl.when(wanted)
        def _():
            for q in range(2):
                remote(
                    zbuf.at[q, 0, 0:PAIRS], bz.at[s, q], b_send.at[q, 0], b_recv.at[s, q], nb, nl
                ).wait_recv()
            z = bz[s].reshape(2 * PAIRS, RANK)
            edge_proj[s] = dot3(dot_cols, z, qh[...], ql[...]).reshape(2, PAIRS, WIDE)

        @pl.when(jnp.logical_not(wanted))
        def _():
            edge_proj[s] = jnp.zeros((2, PAIRS, WIDE), F32)

    def row_weights(a, nw):
        return (
            -nw * a[0],
            -nw * a[1] - coupling * a[2],
            -nw * a[2] - coupling * a[1],
            -nw * a[3],
        )

    for s in range(2):
        a = []
        for f in range(FIELDS):
            rows = slice(f * LEV, (f + 1) * LEV)
            a.append(
                edge_probe[s][f]
                + time_step * (edge_t[s, f] - edge_proj[s, 1, rows, :])
                - edge_proj[s, 0, rows, :]
            )
        for f, weight in enumerate(row_weights(a, hr[s, 9])):
            flip = jnp.where(over_pole[s], -flips[f], 1.0)
            gy[f * LEV : (f + 1) * LEV, edge_row[s], :] = flip * weight

    @pl.loop(0, LEV)
    def _(l):
        for h in (8, 16):
            nw = grid[PAIRS + LEV + l, h : h + 8, :]
            a = []
            for f in range(FIELDS):
                n = f * LEV + l
                change = time_step * (tend[n, h - 8 : h, :] - proj_t[n, h - 8 : h, :])
                tend[n, h - 8 : h, :] = change
                tangent = grid[n, h : h + 8, :] + change
                tan_v[f, l, h - 8 : h, :] = tangent[:, :COLS]
                a.append(tangent - proj_p[n, h - 8 : h, :])
                adj[n, h - 8 : h, :] = a[f]
            for f, weight in enumerate(row_weights(a, nw)):
                gy[f * LEV + l, h : h + 8, :] = weight

    tan_copy = pltpu.make_async_copy(tan_v, tan_out, out_sem.at[0])
    tan_copy.start()

    @pl.loop(0, LEV)
    def _(l):
        lo = jnp.maximum(l - 1, 0)
        hi = jnp.minimum(l + 1, LEV - 1)
        for h in (8, 16):
            rows = slice(h - 8, h)
            half = jnp.concatenate([hm[h : h + 8, :]] * 4, axis=1)
            ew = grid[PAIRS + l, h : h + 8, :]
            a = [adj[f * LEV + l, rows, :] for f in range(FIELDS)]
            col_weights = (
                -ew * a[0] - coupling * a[2],
                -ew * a[1],
                -ew * a[2] - coupling * a[0],
                -ew * a[3],
            )
            for f in range(FIELDS):
                n = f * LEV + l
                back = half * (roll(col_weights[f], 1, 1) - roll(col_weights[f], -1, 1))
                back = back + 0.5 * (gy[n, h - 1 : h + 7, :] - gy[n, h + 1 : h + 9, :])
                back = back + mixing * (adj[f * LEV + lo, rows, :] + adj[f * LEV + hi, rows, :] - 2.0 * a[f])
                diag = grid[n, h : h + 8, :] * (tend[n, rows, :] + time_step * back)
                diag_v[f, l, rows, :] = diag[:, :COLS]

    diag_copy = pltpu.make_async_copy(diag_v, diag_out, out_sem.at[1])
    diag_copy.start()

    for send in halo_sends:
        send.wait_send()

    @pl.when(polar)
    def _():
        for q in range(2):
            @pl.loop(1, LANES)
            def _(d):
                y_copy(q, plus(i, d)).wait_send()
                z_copy(q, plus(i, d)).wait_send()

            edge_sends(q, end_copy)

    tan_copy.wait()
    diag_copy.wait()


def per_device(bands, row_signs, col_signs, spread, east_wind, north_wind, cutoffs):
    any_spec = pl.BlockSpec(memory_space=pl.ANY)
    out = jax.ShapeDtypeStruct((FIELDS, LEV, ROWS, COLS), F32)
    tables = [jnp.asarray(table) for table in (half_metric(bands),) + mode_factors()]
    vmem = pltpu.VMEM
    dma = pltpu.SemaphoreType.DMA
    return pl.pallas_call(
        functools.partial(kernel, bands),
        out_shape=(out, out),
        in_specs=[any_spec] * 11,
        out_specs=(any_spec, any_spec),
        scratch_shapes=[
            vmem((FIELDS, LEV, ROWS, COLS), F32),
            vmem((LEV, ROWS, COLS), F32),
            vmem((LEV, ROWS, COLS), F32),
            vmem((FIELDS, LEV, ROWS), jnp.int32),
            vmem((FIELDS, LEV, COLS), jnp.int32),
            pltpu.SMEM((ROWS,), jnp.int32),
            vmem((32, 128), F32),
            vmem((RANK, WIDE), BF16),
            vmem((RANK, WIDE), BF16),
            vmem((LANES * RANK, 2 * KTOP), BF16),
            vmem((LANES * RANK, 2 * KTOP), BF16),
            vmem((PAIRS + 2 * LEV, 32, WIDE), F32),
            vmem((2, 10, LEV, WIDE), F32),
            vmem((2, 10, LEV, WIDE), F32),
            vmem((2, 2, FIELDS, LEV, 128), F32),
            vmem((2, ROWS, 128), F32),
            vmem((2, ROWS, 128), F32),
            vmem((2, LANES, 2 * PAIRS, RANK), F32),
            vmem((2, LANES, 2 * PAIRS, RANK), F32),
            vmem((2, LANES, 2 * PAIRS, RANK), F32),
            vmem((2, LANES, 2 * PAIRS, RANK), F32),
            vmem((2, 2, PAIRS, RANK), F32),
            vmem((PAIRS, ROWS, WIDE), F32),
            vmem((PAIRS, ROWS, WIDE), F32),
            vmem((PAIRS, ROWS, WIDE), F32),
            vmem((2, FIELDS, LEV, WIDE), F32),
            vmem((2, 2, PAIRS, WIDE), F32),
            vmem((PAIRS, ROWS, WIDE), F32),
            vmem((PAIRS, 32, WIDE), F32),
            vmem((FIELDS, LEV, ROWS, COLS), F32),
            vmem((FIELDS, LEV, ROWS, COLS), F32),
            dma((11,)),
            dma((2,)),
            dma((2,)),
            dma((2, 2)),
            dma((2, 2)),
            dma((2,)),
            dma((2,)),
            dma((2, LANES)),
            dma((2, LANES)),
            dma((2, LANES)),
            dma((2, LANES)),
            dma((2, LANES)),
            dma((2, 2)),
            dma((2,)),
        ],
        compiler_params=pltpu.CompilerParams(
            collective_id=0, has_side_effects=True, vmem_limit_bytes=48 * 2**20
        ),
        cost_estimate=pl.CostEstimate(flops=10**9, bytes_accessed=4 * 10**6, transcendentals=0),
    )(spread, east_wind, north_wind, row_signs, col_signs, cutoffs, *tables)


def solution(mesh):
    return jax.shard_map(
        functools.partial(per_device, mesh.shape["lat"]),
        mesh=mesh,
        in_specs=(
            P(None, None, "lat"),
            P(None, None, "lon"),
            P(None, None, "lat", "lon"),
            P(None, "lat", "lon"),
            P(None, "lat", "lon"),
            P("lat"),
        ),
        out_specs=(P(None, None, "lat", "lon"), P(None, None, "lat", "lon")),
        check_vma=False,
    )
```

time: 812 us -> 40.4 us (0.05); the launches traced: 798 us -> 39.9 us
  waiting for transfers between devices: 577 us -> 0 us
  matrix products: 122 us -> 0 us
  other arithmetic: 36.7 us -> 0 us
  Pallas kernels: 0 us -> 27.5 us
  local copies, waits for them, and re-layouts: 31.4 us -> 11.8 us
  starting transfers between devices: 15.8 us -> 0 us
  between operations: 14.6 us -> 0.66 us
    all_gather x2 -> x0, waiting for transfers between devices: 567 us -> none  [filtered(): lax.all_gather(field, 'lon', axis=3, tiled=True)]
    dot_general x4 -> x0, matrix products: 122 us -> none  [the longest x2 120 us: filtered(): jnp.einsum('flrj,jk->flrk', lax.all_gather(field, 'lon', axis=3, tiled=Tr...]
    pallas_call x0 -> x1, Pallas kernels: none -> 27.5 us  [per_device(): pl.pallas_call(functools.partial(kernel, bands), out_shape=(out, out), in...]
    cos x2 -> x0, other arithmetic: 18.8 us -> none  [mode_table(): return jnp.concatenate([jnp.cos(angle), jnp.sin(angle)], axis=1)]
    ppermute x10 -> x0, starting transfers between devices: 15.7 us -> none  [the longest x4 8.36 us: extended(): lax.ppermute(tail, axis, [(i, (i + 1) % count) for i in range(count)])]
    scatter x4 -> x0, local copies, waits for them, and re-layouts: 11.6 us -> none  [the longest x2 7.12 us: per_device(): padded.at[:, :, 0, 1:-1].set(north_row).at[:, :, -1, 1:-1].set(south_row)]
    unnamed x18 -> x24, local copies, waits for them, and re-layouts: 0.8 us -> 11.8 us
    ppermute x10 -> x0, waiting for transfers between devices: 10.2 us -> none  [the longest x4 5.58 us: extended(): lax.ppermute(head, axis, [((i + 1) % count, i) for i in range(count)])]
  transfers between devices with their start and end apart: 12 -> 0, of which waited for: 6 -> 0; matrix products, arithmetic and copies ran while one was open for 4% -> 0% of each run, Pallas kernels for 0% -> 0%
where the time goes in v1:
time: 40.4 us; the launch traced here: 39.9 us
  Pallas kernels  27.5 us (68%)
  local copies, waits for them, and re-layouts  11.8 us (29%)
  between operations  0.66 us (2%)
    pallas_call x1, Pallas kernels, per_device(): pl.pallas_call(functools.partial(kernel, bands), out_shape=(out, out), in...  27.5 us
    unnamed x24, local copies, waits for them, and re-layouts  11.8 us

profile of v1, /device:TPU:1, one launch (start us, length us, event | category | flops | bytes accessed | tf_op | source)
XLA Modules:
  0.0 39.9 jit_solution(1836291387426253308)
XLA Ops:
  0.6 0.0 copy-start
  0.6 1.2 %copy-done = bf16[1024,512]{1,0:T(8,128)(2,1)S(1)} copy-done((bf16[1024,512]{1,0:T(8,128)(2,1)S(1)}, bf16[1024,512]{1,0:T(8,128)(2,1)}, u32[]{:S(2)}) %copy-start) | copy-done | bytes 1048600
  1.9 0.0 copy-start.1
  1.9 1.2 %copy-done.1 = bf16[1024,512]{1,0:T(8,128)(2,1)S(1)} copy-done((bf16[1024,512]{1,0:T(8,128)(2,1)S(1)}, bf16[1024,512]{1,0:T(8,128)(2,1)}, u32[]{:S(2)}) %copy-start.1) | copy-done | bytes 1048600
  3.1 0.0 copy-start.2
  3.1 1.0 %copy-done.2 = f32[4,4,16,450]{3,2,1,0:T(8,128)S(1)} copy-done((f32[4,4,16,450]{3,2,1,0:T(8,128)S(1)}, f32[4,4,16,450]{3,2,1,0:T(8,128)}, u32[]{:S(2)}) %copy-start.2) | copy-done | bytes 460824
  4.1 0.0 copy-start.3
  4.1 1.0 %copy-done.3 = f32[32,32,128]{2,1,0:T(8,128)S(1)} copy-done((f32[32,32,128]{2,1,0:T(8,128)S(1)}, f32[32,32,128]{2,1,0:T(8,128)}, u32[]{:S(2)}) %copy-start.3) | copy-done | bytes 524312
  5.2 0.0 copy-start.4
  5.2 0.9 %copy-done.4 = f32[4,16,450]{2,1,0:T(8,128)S(1)} copy-done((f32[4,16,450]{2,1,0:T(8,128)S(1)}, f32[4,16,450]{2,1,0:T(8,128)}, u32[]{:S(2)}) %copy-start.4) | copy-done | bytes 115224
  6.1 0.0 copy-start.5
  6.1 0.9 %copy-done.5 = f32[4,16,450]{2,1,0:T(8,128)S(1)} copy-done((f32[4,16,450]{2,1,0:T(8,128)S(1)}, f32[4,16,450]{2,1,0:T(8,128)}, u32[]{:S(2)}) %copy-start.5) | copy-done | bytes 115224
  7.0 0.0 copy-start.6
  7.0 0.9 %copy-done.6 = bf16[128,512]{1,0:T(8,128)(2,1)S(1)} copy-done((bf16[128,512]{1,0:T(8,128)(2,1)S(1)}, bf16[128,512]{1,0:T(8,128)(2,1)}, u32[]{:S(2)}) %copy-start.6) | copy-done | bytes 131096
  7.9 0.0 copy-start.7
  7.9 0.9 %copy-done.7 = bf16[128,512]{1,0:T(8,128)(2,1)S(1)} copy-done((bf16[128,512]{1,0:T(8,128)(2,1)S(1)}, bf16[128,512]{1,0:T(8,128)(2,1)}, u32[]{:S(2)}) %copy-start.7) | copy-done | bytes 131096
  8.8 0.0 copy-start.8
  8.8 0.8 %copy-done.8 = s32[4,4,450]{2,1,0:T(4,128)S(1)} copy-done((s32[4,4,450]{2,1,0:T(4,128)S(1)}, s32[4,4,450]{2,1,0:T(4,128)}, u32[]{:S(2)}) %copy-start.8) | copy-done | bytes 28824
  9.5 0.0 copy-start.9
  9.5 0.7 %copy-done.9 = s32[4,4,16]{2,1,0:T(4,128)S(1)} copy-done((s32[4,4,16]{2,1,0:T(4,128)S(1)}, s32[4,4,16]{2,1,0:T(4,128)}, u32[]{:S(2)}) %copy-start.9) | copy-done | bytes 1048
  10.2 0.0 copy-start.10
  10.2 0.7 %copy-done.10 = s32[16]{0:T(128)S(1)} copy-done((s32[16]{0:T(128)S(1)}, s32[16]{0:T(128)}, u32[]{:S(2)}) %copy-start.10) | copy-done | bytes 88
  10.9 27.5 %shard_map.122 = (f32[4,4,16,450]{3,2,1,0:T(8,128)S(1)}, f32[4,4,16,450]{3,2,1,0:T(8,128)S(1)}) custom-call(f32[4,4,16,450]{3,2,1,0:T(8,128)S(1)} %copy-done.2, f32[4,16,450]{2,1,0:T(8,128)S(1)} %copy-done.4, f32[4,16,450]{2,1,0:T(8,128)S(1)} %copy-done.5, s32[4,4,16]{2,1,0:T(4,128)S(1)} %copy-done.9, s32[4,4,450]{2,1,0:T(4,128)S(1)} %copy-done.8, ...), custom_call_target="tpu_custom_call" | custom-call | flops 1000000000 | bytes 4000000 | tf_op jit(solution)/shard_map/pallas_call | solution.py:537
  38.4 0.8 %copy.15 = f32[4,4,16,450]{3,2,1,0:T(8,128)} copy(f32[4,4,16,450]{3,2,1,0:T(8,128)S(1)} %get-tuple-element.4) | data formatting | bytes 921600
  39.2 0.8 %copy.16 = f32[4,4,16,450]{3,2,1,0:T(8,128)} copy(f32[4,4,16,450]{3,2,1,0:T(8,128)S(1)} %get-tuple-element.5) | data formatting | bytes 921600
Async XLA Ops:
  0.6 1.2 %copy-start = (bf16[1024,512]{1,0:T(8,128)(2,1)S(1)}, bf16[1024,512]{1,0:T(8,128)(2,1)}, u32[]{:S(2)}) copy-start(bf16[1024,512]{1,0:T(8,128)(2,1)} %constant.14.clone.rl_in) | copy-start | bytes 3145732
  1.9 1.2 %copy-start.1 = (bf16[1024,512]{1,0:T(8,128)(2,1)S(1)}, bf16[1024,512]{1,0:T(8,128)(2,1)}, u32[]{:S(2)}) copy-start(bf16[1024,512]{1,0:T(8,128)(2,1)} %constant.13.clone.rh_in) | copy-start | bytes 3145732
  3.1 1.0 %copy-start.2 = (f32[4,4,16,450]{3,2,1,0:T(8,128)S(1)}, f32[4,4,16,450]{3,2,1,0:T(8,128)}, u32[]{:S(2)}) copy-start(f32[4,4,16,450]{3,2,1,0:T(8,128)} %spread.1) | copy-start | bytes 1382404
  4.1 1.0 %copy-start.3 = (f32[32,32,128]{2,1,0:T(8,128)S(1)}, f32[32,32,128]{2,1,0:T(8,128)}, u32[]{:S(2)}) copy-start(f32[32,32,128]{2,1,0:T(8,128)} %constant.10.clone.metric) | copy-start | bytes 1572868
  5.2 0.9 %copy-start.4 = (f32[4,16,450]{2,1,0:T(8,128)S(1)}, f32[4,16,450]{2,1,0:T(8,128)}, u32[]{:S(2)}) copy-start(f32[4,16,450]{2,1,0:T(8,128)} %east.1) | copy-start | bytes 345604
  6.1 0.9 %copy-start.5 = (f32[4,16,450]{2,1,0:T(8,128)S(1)}, f32[4,16,450]{2,1,0:T(8,128)}, u32[]{:S(2)}) copy-start(f32[4,16,450]{2,1,0:T(8,128)} %north.1) | copy-start | bytes 345604
  7.0 0.9 %copy-start.6 = (bf16[128,512]{1,0:T(8,128)(2,1)S(1)}, bf16[128,512]{1,0:T(8,128)(2,1)}, u32[]{:S(2)}) copy-start(bf16[128,512]{1,0:T(8,128)(2,1)} %constant.12.clone.ql_in) | copy-start | bytes 393220
  7.9 0.9 %copy-start.7 = (bf16[128,512]{1,0:T(8,128)(2,1)S(1)}, bf16[128,512]{1,0:T(8,128)(2,1)}, u32[]{:S(2)}) copy-start(bf16[128,512]{1,0:T(8,128)(2,1)} %constant.11.clone.qh_in) | copy-start | bytes 393220
  8.8 0.8 %copy-start.8 = (s32[4,4,450]{2,1,0:T(4,128)S(1)}, s32[4,4,450]{2,1,0:T(4,128)}, u32[]{:S(2)}) copy-start(s32[4,4,450]{2,1,0:T(4,128)} %cs.1) | copy-start | bytes 86404
  9.5 0.7 %copy-start.9 = (s32[4,4,16]{2,1,0:T(4,128)S(1)}, s32[4,4,16]{2,1,0:T(4,128)}, u32[]{:S(2)}) copy-start(s32[4,4,16]{2,1,0:T(4,128)} %rs.1) | copy-start | bytes 3076
  10.2 0.7 %copy-start.10 = (s32[16]{0:T(128)S(1)}, s32[16]{0:T(128)}, u32[]{:S(2)}) copy-start(s32[16]{0:T(128)} %cut.1) | copy-start | bytes 196

commit v2 on v1

--- a/solution.py
+++ b/solution.py
@@ -34,6 +34,14 @@
     high = table.astype(ml_dtypes.bfloat16)
     low = (table - high.astype(np.float64)).astype(ml_dtypes.bfloat16)
     return high, low
+
+
+def waves_of(group, lane_index):
+    place = lane_index % 64
+    second = place // 32
+    other = (8 - group) if group else 4
+    residue = group + second * (other - group)
+    return 8 * (place % 32) + residue + (8 * (1 - second) if group == 0 else 0)
 
 
 @functools.lru_cache(None)
@@ -47,18 +55,49 @@
     vectors = np.linalg.eigh(np.diag(diag) + np.diag(side, 1) + np.diag(side, -1))[1]
     basis = vectors[:, ::-1][:, :RANK]
     basis = basis * np.where(basis[size // 2] < 0, -1.0, 1.0)
-    waves = np.arange(1, KTOP + 1)
-    factors = []
-    for lane in range(LANES):
-        cols = lane * COLS - 1 + np.arange(size)
-        angle = 2 * np.pi / total * (cols[:, None] * waves[None, :] % total)
-        factors.append(basis.T @ np.concatenate([np.cos(angle), np.sin(angle)], axis=1))
-    factors = np.round(np.concatenate(factors, axis=0) * 2.0**22) / 2.0**22
+    weights = []
+    for group in range(4):
+        waves = waves_of(group, np.arange(64))
+        angle = 2 * np.pi / total * ((np.arange(size)[:, None] - 1) * waves[None, :] % total)
+        alpha, beta = basis.T @ np.cos(angle), basis.T @ np.sin(angle)
+        if group:
+            sign = np.where(np.arange(64) < 32, 1.0, -1.0)
+            top, low = (alpha, beta), (sign * beta, -sign * alpha)
+        else:
+            use = np.where(np.arange(64) < 32, 1.0, 0.0)
+            top, low = (use * alpha, use * beta), ((1 - use) * alpha, (1 - use) * beta)
+        weights.append(np.concatenate([np.concatenate(top, axis=1), np.concatenate(low, axis=1)], axis=0))
+    weights = np.round(np.stack(weights) * 2.0**22) / 2.0**22
     wide = np.zeros((RANK, WIDE))
     wide[:, : COLS + 1] = basis[1:].T
     wide[:, WIDE - 1] = basis[0]
     wide = np.round(wide * 2.0**26) / 2.0**26
-    return split_table(wide) + split_table(factors)
+    return split_table(wide) + split_table(weights)
+
+
+ROOT = float(np.sqrt(0.5))
+
+
+def over_lanes(y):
+    s = [y[j] + y[j + 4] for j in range(4)]
+    d = [y[j] - y[j + 4] for j in range(4)]
+    even, odd = s[0] + s[2], s[1] + s[3]
+    minus, plus = ROOT * (d[1] - d[3]), ROOT * (d[1] + d[3])
+    return [
+        (even + odd, even - odd),
+        (d[0] + minus, -(d[2] + plus)),
+        (s[0] - s[2], s[3] - s[1]),
+        (d[0] - minus, d[2] - plus),
+    ]
+
+
+def to_lanes(pairs):
+    (y0, y4), (u1, v1), (u2, v2), (u3, v3) = pairs
+    even, odd = y0 + y4, y0 - y4
+    s = [even + u2, odd - v2, even - u2, odd + v2]
+    du, sv = ROOT * (u1 - u3), ROOT * (v1 + v3)
+    d = [u1 + u3, du - sv, v3 - v1, -du - sv]
+    return [s[j] + d[j] for j in range(4)] + [s[j] - d[j] for j in range(4)]
 
 
 @functools.lru_cache(None)
@@ -80,7 +119,9 @@
 def dot3(dot, x, high, low):
     xh = x.astype(BF16)
     xl = (x - xh.astype(F32)).astype(BF16)
-    return dot(xh, high) + dot(xl, high) + dot(xh, low)
+    rows = x.shape[0]
+    both = dot(jnp.concatenate([xh, xl], axis=0), high)
+    return both[:rows] + both[rows:] + dot(xh, low)
 
 
 def roll(x, shift, axis):
@@ -99,8 +140,8 @@
 
 
 def kernel(
-    bands, spread, east, north, rs, cs, cut, metric, qh_in, ql_in, rh_in, rl_in, tan_out, diag_out,
-    spread_v, east_v, north_v, rs_v, cs_v, cut_s, hm, qh, ql, rh, rl,
+    bands, spread, east, north, rs, cs, cut, metric, qh_in, ql_in, wh_in, wl_in, tan_out, diag_out,
+    spread_v, east_v, north_v, rs_v, cs_v, cut_s, hm, qh, ql, wh, wl,
     grid, er, hr, hc, cp, hcol, ybuf, yr, zbuf, zr, bz,
     tend, proj_p, proj_t, edge_t, edge_proj, adj, gy, tan_v, diag_v,
     in_sem, row_send, row_recv, cor_send, cor_recv, col_send, col_recv,
@@ -140,8 +181,8 @@
         pltpu.make_async_copy(ql_in, ql, in_sem.at[8]),
     ]
     table_loads = [
-        pltpu.make_async_copy(rh_in, rh, in_sem.at[9]),
-        pltpu.make_async_copy(rl_in, rl, in_sem.at[10]),
+        pltpu.make_async_copy(wh_in, wh, in_sem.at[9]),
+        pltpu.make_async_copy(wl_in, wl, in_sem.at[10]),
     ]
     for load in loads:
         load.start()
@@ -309,15 +350,17 @@
         def _(d):
             y_arrival(q, plus(i, d)).wait_recv()
 
-        y = jnp.concatenate([yr[q, j] for j in range(LANES)], axis=1)
-        coef = dot3(dot_cols, y, rh[...], rl[...])
-        wave = lax.rem(lax.broadcasted_iota(jnp.int32, (PAIRS, 2 * KTOP), 1), KTOP) + 1
-        keep = jnp.concatenate(
-            [jnp.where(wave > cut_s[2 * i + part], 2.0 / (COLS * LANES), 0.0) for part in range(2)], axis=0
-        )
-        z = dot3(dot_rows, coef * keep, rh[...], rl[...])
-        for j in range(LANES):
-            zbuf[q, j] = z[:, j * RANK : (j + 1) * RANK]
+        pairs = []
+        for group, pair in enumerate(over_lanes([yr[q, j] for j in range(LANES)])):
+            coef = dot3(dot_cols, jnp.concatenate(pair, axis=1), wh[group], wl[group])
+            wave = waves_of(group, lax.broadcasted_iota(jnp.int32, (PAIRS, 2 * 64), 1))
+            keep = jnp.concatenate(
+                [jnp.where(wave > cut_s[2 * i + part], 2.0 / (COLS * LANES), 0.0) for part in range(2)], axis=0
+            )
+            back = dot3(dot_rows, coef * keep, wh[group], wl[group])
+            pairs.append((back[:, :RANK], back[:, RANK:]))
+        for j, z in enumerate(to_lanes(pairs)):
+            zbuf[q, j] = z
 
         @pl.loop(1, LANES)
         def _(d):
@@ -372,27 +415,11 @@
         tile = jnp.where(lane2 == 127, roll(hc[s, 0, f], 62, 1), tile)
         return jnp.concatenate([hr[s, f][:, 0:384], tile], axis=1)
 
-    edge_probe = []
+    edge_probe = [[edge_center(s, f) for f in range(FIELDS)] for s in range(2)]
     for s in range(2):
-        centers = [edge_center(s, f) for f in range(FIELDS)]
-        edge_probe.append(centers)
-        half = jnp.concatenate([hm[edge_row[s] : edge_row[s] + 1, :]] * 4, axis=1)
-        turn = jnp.where(over_pole[s], -inward[s], inward[s])
-        along_x, along_y = [], []
         for f in range(FIELDS):
             flip = jnp.where(over_pole[s], flips[f], 1.0)
-            grid[f * LEV : (f + 1) * LEV, edge_row[s], :] = flip * centers[f]
-            along_x.append(half * (roll(centers[f], -1, 1) - roll(centers[f], 1, 1)))
-            along_y.append((0.5 * turn) * (flip * er[s, f] - hr[s, FIELDS + f]))
-        linked = (along_x[2], along_y[2], along_x[0] + along_y[1], None)
-        for f in range(FIELDS):
-            mid = centers[f]
-            up = jnp.concatenate([mid[0:1], mid[0:3]], axis=0)
-            down = jnp.concatenate([mid[1:4], mid[3:4]], axis=0)
-            t = -(hr[s, 8] * along_x[f] + hr[s, 9] * along_y[f]) + mixing * (up + down - 2.0 * mid)
-            if linked[f] is not None:
-                t = t - coupling * linked[f]
-            edge_t[s, f] = t
+            grid[f * LEV : (f + 1) * LEV, edge_row[s], :] = flip * edge_probe[s][f]
 
     @pl.loop(0, LEV)
     def _(l):
@@ -419,6 +446,28 @@
     @pl.when(polar)
     def _():
         send_row_values(1, tend[...].reshape(PAIRS * ROWS, WIDE))
+
+    for s in range(2):
+        centers = edge_probe[s]
+        half = jnp.concatenate([hm[edge_row[s] : edge_row[s] + 1, :]] * 4, axis=1)
+        turn = jnp.where(over_pole[s], -inward[s], inward[s])
+        along_x, along_y = [], []
+        for f in range(FIELDS):
+            flip = jnp.where(over_pole[s], flips[f], 1.0)
+            along_x.append(half * (roll(centers[f], -1, 1) - roll(centers[f], 1, 1)))
+            along_y.append((0.5 * turn) * (flip * er[s, f] - hr[s, FIELDS + f]))
+        linked = (along_x[2], along_y[2], along_x[0] + along_y[1], None)
+        for f in range(FIELDS):
+            mid = centers[f]
+            up = jnp.concatenate([mid[0:1], mid[0:3]], axis=0)
+            down = jnp.concatenate([mid[1:4], mid[3:4]], axis=0)
+            t = -(hr[s, 8] * along_x[f] + hr[s, 9] * along_y[f]) + mixing * (up + down - 2.0 * mid)
+            if linked[f] is not None:
+                t = t - coupling * linked[f]
+            edge_t[s, f] = t
+
+    @pl.when(polar)
+    def _():
         for load in table_loads:
             load.wait()
         own_rows(0)
@@ -549,8 +598,8 @@
             vmem((32, 128), F32),
             vmem((RANK, WIDE), BF16),
             vmem((RANK, WIDE), BF16),
-            vmem((LANES * RANK, 2 * KTOP), BF16),
-            vmem((LANES * RANK, 2 * KTOP), BF16),
+            vmem((4, 2 * RANK, 2 * 64), BF16),
+            vmem((4, 2 * RANK, 2 * 64), BF16),
             vmem((PAIRS + 2 * LEV, 32, WIDE), F32),
             vmem((2, 10, LEV, WIDE), F32),
             vmem((2, 10, LEV, WIDE), F32),
@@ -587,7 +636,7 @@
             dma((2,)),
         ],
         compiler_params=pltpu.CompilerParams(
-            collective_id=0, has_side_effects=True, vmem_limit_bytes=48 * 2**20
+            collective_id=0, has_side_effects=True, vmem_limit_bytes=64 * 2**20
         ),
         cost_estimate=pl.CostEstimate(flops=10**9, bytes_accessed=4 * 10**6, transcendentals=0),
     )(spread, east_wind, north_wind, row_signs, col_signs, cutoffs, *tables)

time: 40.4 us -> 29.3 us (0.73)
  local copies, waits for them, and re-layouts: 11.8 us -> 2.74 us
  Pallas kernels: 27.5 us -> 25.8 us
    unnamed x24 -> x4, local copies, waits for them, and re-layouts: 11.8 us -> 2.74 us
    pallas_call x1, Pallas kernels: 27.5 us -> 25.8 us  [per_device(): pl.pallas_call(functools.partial(kernel, bands), out_shape=(out, out), in...]
where the time goes in v2:
time: 29.3 us; the launch traced here: 29.2 us
  Pallas kernels  25.8 us (88%)
  local copies, waits for them, and re-layouts  2.74 us (9%)
  between operations  0.65 us (2%)
    pallas_call x1, Pallas kernels, per_device(): pl.pallas_call(functools.partial(kernel, bands), out_shape=(out, out), in...  25.8 us
    unnamed x4, local copies, waits for them, and re-layouts  2.74 us

profile of v2, /device:TPU:1, one launch (start us, length us, event | category | flops | bytes accessed | tf_op | source)
XLA Modules:
  0.0 29.2 jit_solution(14573413410618044229)
XLA Ops:
  0.6 25.8 %shard_map.122 = (f32[4,4,16,450]{3,2,1,0:T(8,128)}, f32[4,4,16,450]{3,2,1,0:T(8,128)}) custom-call(f32[4,4,16,450]{3,2,1,0:T(8,128)} %spread.1, f32[4,16,450]{2,1,0:T(8,128)} %east.1, f32[4,16,450]{2,1,0:T(8,128)} %north.1, s32[4,4,16]{2,1,0:T(4,128)} %rs.1, s32[4,4,450]{2,1,0:T(4,128)} %cs.1, s32[16]{0:T(128)} %cut.1, ...), custom_call_target="tpu_custom_call" | custom-call | flops 1000000000 | bytes 4000000 | tf_op jit(solution)/shard_map/pallas_call | solution.py:586
  26.5 0.0 copy-start
  26.5 1.9 %copy.15 = f32[4,4,16,450]{3,2,1,0:T(8,128)} copy(f32[4,4,16,450]{3,2,1,0:T(8,128)} %get-tuple-element.4) | data formatting | bytes 921600
  28.4 0.0 copy-done
  28.4 0.8 %copy.16 = f32[4,4,16,450]{3,2,1,0:T(8,128)} copy(f32[4,4,16,450]{3,2,1,0:T(8,128)S(1)} %copy-done) | data formatting | bytes 921600
Async XLA Ops:
  26.5 2.0 %copy-start = (f32[4,4,16,450]{3,2,1,0:T(8,128)S(1)}, f32[4,4,16,450]{3,2,1,0:T(8,128)}, u32[]{:S(2)}) copy-start(f32[4,4,16,450]{3,2,1,0:T(8,128)} %get-tuple-element.5) | copy-start | bytes 1382404

commit v3 on v2

--- a/solution.py
+++ b/solution.py
@@ -72,7 +72,8 @@
     wide[:, : COLS + 1] = basis[1:].T
     wide[:, WIDE - 1] = basis[0]
     wide = np.round(wide * 2.0**26) / 2.0**26
-    return split_table(wide) + split_table(weights)
+    wide_h, wide_l = split_table(wide)
+    return np.concatenate([wide_h, wide_l, wide_h], axis=0), np.concatenate(split_table(weights), axis=2)
 
 
 ROOT = float(np.sqrt(0.5))
@@ -116,12 +117,21 @@
     return lax.dot_general(a, b, (((1,), (0,)), ((), ())), preferred_element_type=F32)
 
 
-def dot3(dot, x, high, low):
-    xh = x.astype(BF16)
-    xl = (x - xh.astype(F32)).astype(BF16)
-    rows = x.shape[0]
-    both = dot(jnp.concatenate([xh, xl], axis=0), high)
-    return both[:rows] + both[rows:] + dot(xh, low)
+def split(x):
+    high = x.astype(BF16)
+    return high, (x - high.astype(F32)).astype(BF16)
+
+
+def to_modes(dot, x, both, high):
+    xh, xl = split(x)
+    wide = dot(xh, both)
+    half = wide.shape[1] // 2
+    return wide[:, :half] + wide[:, half:] + dot(xl, high)
+
+
+def evaluate(z, table):
+    zh, zl = split(z)
+    return dot_cols(jnp.concatenate([zh, zh, zl], axis=1), table[...])
 
 
 def roll(x, shift, axis):
@@ -140,8 +150,8 @@
 
 
 def kernel(
-    bands, spread, east, north, rs, cs, cut, metric, qh_in, ql_in, wh_in, wl_in, tan_out, diag_out,
-    spread_v, east_v, north_v, rs_v, cs_v, cut_s, hm, qh, ql, wh, wl,
+    bands, spread, east, north, rs, cs, cut, metric, q3_in, w2_in, tan_out, diag_out,
+    spread_v, east_v, north_v, rs_v, cs_v, cut_s, hm, q3, w2,
     grid, er, hr, hc, cp, hcol, ybuf, yr, zbuf, zr, bz,
     tend, proj_p, proj_t, edge_t, edge_proj, adj, gy, tan_v, diag_v,
     in_sem, row_send, row_recv, cor_send, cor_recv, col_send, col_recv,
@@ -177,20 +187,15 @@
         pltpu.make_async_copy(north, north_v, in_sem.at[4]),
         pltpu.make_async_copy(metric.at[b], hm, in_sem.at[5]),
         pltpu.make_async_copy(cut, cut_s, in_sem.at[6]),
-        pltpu.make_async_copy(qh_in, qh, in_sem.at[7]),
-        pltpu.make_async_copy(ql_in, ql, in_sem.at[8]),
+        pltpu.make_async_copy(q3_in, q3, in_sem.at[7]),
     ]
-    table_loads = [
-        pltpu.make_async_copy(wh_in, wh, in_sem.at[9]),
-        pltpu.make_async_copy(wl_in, wl, in_sem.at[10]),
-    ]
+    table_load = pltpu.make_async_copy(w2_in, w2, in_sem.at[8])
     for load in loads:
         load.start()
 
     @pl.when(polar)
     def _():
-        for load in table_loads:
-            load.start()
+        table_load.start()
 
     barrier = pltpu.get_barrier_semaphore()
 
@@ -211,14 +216,6 @@
         @pl.loop(1, LANES)
         def _(d):
             greet(b, plus(i, d))
-
-    @pl.when(jnp.logical_and(above_polar, jnp.logical_not(is_north)))
-    def _():
-        greet(nb, last)
-
-    @pl.when(jnp.logical_and(below_polar, jnp.logical_not(is_south)))
-    def _():
-        greet(sb, first)
 
     for load in loads[:5]:
         load.wait()
@@ -246,13 +243,7 @@
         packed = fold(tile[:PAIRS]) + roll_blocks(fold(tile[PAIRS:]), 2 * PAIRS)
         cp[s] = roll_blocks(packed, -shift)[0]
 
-    pl.semaphore_wait(
-        barrier,
-        8
-        + jnp.where(polar, LANES - 1, 0)
-        + jnp.where(jnp.logical_and(polar, jnp.logical_and(i == first, jnp.logical_not(is_north))), LANES, 0)
-        + jnp.where(jnp.logical_and(polar, jnp.logical_and(i == last, jnp.logical_not(is_south))), LANES, 0),
-    )
+    pl.semaphore_wait(barrier, 8 + jnp.where(polar, LANES - 1, 0))
 
     def remote(src, dst, send, recv, lat, lon):
         return pltpu.make_async_remote_copy(
@@ -291,7 +282,7 @@
         return remote(ybuf.at[q, j], yr.at[q, j], y_send.at[q, j], y_recv.at[q, j], b, j)
 
     def send_row_values(q, x):
-        y = dot3(dot_rows, jnp.where(own_cols, x, 0.0), qh[...], ql[...])
+        y = to_modes(dot_rows, jnp.where(own_cols, x, 0.0), q3[0 : 2 * RANK, :], q3[0:RANK, :])
         y = jnp.swapaxes(y.reshape(PAIRS, ROWS, RANK), 0, 1)
         ybuf[q] = y.reshape(LANES, 2 * PAIRS, RANK)
 
@@ -301,81 +292,62 @@
 
         yr[q, i] = ybuf[q, i]
 
-    def z_copy(q, j):
-        return remote(zbuf.at[q, j], zr.at[q, i], z_send.at[q, j], z_recv.at[q, i], b, j)
-
-    def z_arrival(q, j):
-        return remote(zbuf.at[q, j], zr.at[q, j], z_send.at[q, j], z_recv.at[q, j], b, j)
-
-    def edge_copy(q, j, s):
-        slot, lat = ((slot_n, nb), (slot_s, sb))[s]
-        over = (is_north, is_south)[s]
-        lon = jnp.where(over, plus(j, LANES // 2), j)
-        part = zbuf.at[q, j, PAIRS * s : PAIRS * (s + 1)]
-        here = jnp.logical_and(over, lon == i)
-
-        def away():
-            return remote(part, bz.at[slot, q], b_send.at[q, j], b_recv.at[slot, q], lat, lon)
-
-        def local():
-            return pltpu.make_async_copy(part, bz.at[s, q], b_recv.at[s, q])
-
-        return here, away, local
-
-    def edge_sends(q, act):
-        for s, owner in ((0, first), (1, last)):
-            @pl.when(i == owner)
-            def _():
-                @pl.loop(0, LANES)
-                def _(j):
-                    here, away, local = edge_copy(q, j, s)
-
-                    @pl.when(jnp.logical_not(here))
-                    def _():
-                        act(away())
-
-                    if act is start_copy:
-                        @pl.when(here)
-                        def _():
-                            local().start()
-
-    def start_copy(copy):
-        copy.start()
-
-    def end_copy(copy):
-        copy.wait_send()
-
-    def own_rows(q):
+    def z_copy(j):
+        return remote(zbuf.at[j], zr.at[i], z_send.at[j], z_recv.at[i], b, j)
+
+    def z_arrival(j):
+        return remote(zbuf.at[j], zr.at[j], z_send.at[j], z_recv.at[j], b, j)
+
+    def own_rows():
+        for q in range(2):
+            @pl.loop(1, LANES)
+            def _(d):
+                y_arrival(q, plus(i, d)).wait_recv()
+
+        pairs = []
+        over = over_lanes([yr[:, j].reshape(4 * PAIRS, RANK) for j in range(LANES)])
+        for group, pair in enumerate(over):
+            coef = to_modes(dot_cols, jnp.concatenate(pair, axis=1), w2[group], w2[group, :, 0:128])
+            wave = waves_of(group, lax.broadcasted_iota(jnp.int32, (PAIRS, 128), 1))
+            keep = [jnp.where(wave > cut_s[2 * i + part], 2.0 / (COLS * LANES), 0.0) for part in range(2)]
+            high, low = split(coef * jnp.concatenate(keep + keep, axis=0))
+            back = dot_rows(jnp.concatenate([high, high], axis=1), w2[group])
+            back = back + dot_rows(low, w2[group, :, 0:128])
+            pairs.append((back[:, :RANK], back[:, RANK:]))
+        for j, z in enumerate(to_lanes(pairs)):
+            zbuf[j] = z.reshape(2, 2 * PAIRS, RANK)
+
         @pl.loop(1, LANES)
         def _(d):
-            y_arrival(q, plus(i, d)).wait_recv()
-
-        pairs = []
-        for group, pair in enumerate(over_lanes([yr[q, j] for j in range(LANES)])):
-            coef = dot3(dot_cols, jnp.concatenate(pair, axis=1), wh[group], wl[group])
-            wave = waves_of(group, lax.broadcasted_iota(jnp.int32, (PAIRS, 2 * 64), 1))
-            keep = jnp.concatenate(
-                [jnp.where(wave > cut_s[2 * i + part], 2.0 / (COLS * LANES), 0.0) for part in range(2)], axis=0
-            )
-            back = dot3(dot_rows, coef * keep, wh[group], wl[group])
-            pairs.append((back[:, :RANK], back[:, RANK:]))
-        for j, z in enumerate(to_lanes(pairs)):
-            zbuf[q, j] = z
+            z_copy(plus(i, d)).start()
+
+        zr[i] = zbuf[i]
+
+    def edge_sends():
+        return (
+            remote(zr.at[first, :, 0:PAIRS], bz.at[slot_n], b_send.at[0], b_recv.at[slot_n], nb, nl),
+            remote(zr.at[last, :, PAIRS : 2 * PAIRS], bz.at[slot_s], b_send.at[1], b_recv.at[slot_s], sb, sl),
+        )
+
+    def project():
+        for owner, send in zip((first, last), edge_sends()):
+            @pl.when(i != owner)
+            def _():
+                z_arrival(owner).wait_recv()
+
+            send.start()
 
         @pl.loop(1, LANES)
         def _(d):
-            z_copy(q, plus(i, d)).start()
-
-        edge_sends(q, start_copy)
-        zr[q, i] = zbuf[q, i]
-
-    def project(q, out):
-        @pl.loop(1, LANES)
-        def _(d):
-            z_arrival(q, plus(i, d)).wait_recv()
-
-        z = jnp.swapaxes(zr[q].reshape(ROWS, PAIRS, RANK), 0, 1).reshape(PAIRS * ROWS, RANK)
-        out[...] = dot3(dot_cols, z, qh[...], ql[...]).reshape(PAIRS, ROWS, WIDE)
+            j = plus(i, d)
+
+            @pl.when(jnp.logical_and(j != first, j != last))
+            def _():
+                z_arrival(j).wait_recv()
+
+        for q, out in enumerate((proj_p, proj_t)):
+            z = jnp.swapaxes(zr[:, q].reshape(ROWS, PAIRS, RANK), 0, 1).reshape(PAIRS * ROWS, RANK)
+            out[...] = evaluate(z, q3).reshape(PAIRS, ROWS, WIDE)
 
     for load in loads[5:]:
         load.wait()
@@ -468,31 +440,14 @@
 
     @pl.when(polar)
     def _():
-        for load in table_loads:
-            load.wait()
-        own_rows(0)
-        own_rows(1)
-        project(0, proj_p)
-        project(1, proj_t)
+        table_load.wait()
+        own_rows()
+        project()
 
     @pl.when(jnp.logical_not(polar))
     def _():
         proj_p[...] = jnp.zeros(proj_p.shape, F32)
         proj_t[...] = jnp.zeros(proj_t.shape, F32)
-
-    for s, wanted in enumerate((above_polar, below_polar)):
-        @pl.when(wanted)
-        def _():
-            for q in range(2):
-                remote(
-                    zbuf.at[q, 0, 0:PAIRS], bz.at[s, q], b_send.at[q, 0], b_recv.at[s, q], nb, nl
-                ).wait_recv()
-            z = bz[s].reshape(2 * PAIRS, RANK)
-            edge_proj[s] = dot3(dot_cols, z, qh[...], ql[...]).reshape(2, PAIRS, WIDE)
-
-        @pl.when(jnp.logical_not(wanted))
-        def _():
-            edge_proj[s] = jnp.zeros((2, PAIRS, WIDE), F32)
 
     def row_weights(a, nw):
         return (
@@ -501,19 +456,6 @@
             -nw * a[2] - coupling * a[1],
             -nw * a[3],
         )
-
-    for s in range(2):
-        a = []
-        for f in range(FIELDS):
-            rows = slice(f * LEV, (f + 1) * LEV)
-            a.append(
-                edge_probe[s][f]
-                + time_step * (edge_t[s, f] - edge_proj[s, 1, rows, :])
-                - edge_proj[s, 0, rows, :]
-            )
-        for f, weight in enumerate(row_weights(a, hr[s, 9])):
-            flip = jnp.where(over_pole[s], -flips[f], 1.0)
-            gy[f * LEV : (f + 1) * LEV, edge_row[s], :] = flip * weight
 
     @pl.loop(0, LEV)
     def _(l):
@@ -533,6 +475,29 @@
 
     tan_copy = pltpu.make_async_copy(tan_v, tan_out, out_sem.at[0])
     tan_copy.start()
+
+    for s, wanted in enumerate((above_polar, below_polar)):
+        @pl.when(wanted)
+        def _():
+            remote(zr.at[first, :, 0:PAIRS], bz.at[s], b_send.at[0], b_recv.at[s], nb, nl).wait_recv()
+            edge_proj[s] = evaluate(bz[s].reshape(2 * PAIRS, RANK), q3).reshape(2, PAIRS, WIDE)
+
+        @pl.when(jnp.logical_not(wanted))
+        def _():
+            edge_proj[s] = jnp.zeros((2, PAIRS, WIDE), F32)
+
+    for s in range(2):
+        a = []
+        for f in range(FIELDS):
+            rows = slice(f * LEV, (f + 1) * LEV)
+            a.append(
+                edge_probe[s][f]
+                + time_step * (edge_t[s, f] - edge_proj[s, 1, rows, :])
+                - edge_proj[s, 0, rows, :]
+            )
+        for f, weight in enumerate(row_weights(a, hr[s, 9])):
+            flip = jnp.where(over_pole[s], -flips[f], 1.0)
+            gy[f * LEV : (f + 1) * LEV, edge_row[s], :] = flip * weight
 
     @pl.loop(0, LEV)
     def _(l):
@@ -565,16 +530,30 @@
 
     @pl.when(polar)
     def _():
-        for q in range(2):
-            @pl.loop(1, LANES)
-            def _(d):
-                y_copy(q, plus(i, d)).wait_send()
-                z_copy(q, plus(i, d)).wait_send()
-
-            edge_sends(q, end_copy)
+        @pl.loop(1, LANES)
+        def _(d):
+            j = plus(i, d)
+            y_copy(0, j).wait_send()
+            y_copy(1, j).wait_send()
+            z_copy(j).wait_send()
+
+        for send in edge_sends():
+            send.wait_send()
 
     tan_copy.wait()
     diag_copy.wait()
+
+
+def hand_out(tan_in, diag_in, tan_out, diag_out, sem):
+    copies = [
+        pltpu.make_async_copy(src.at[f], dst.at[f], sem.at[n, f])
+        for n, (src, dst) in enumerate(((tan_in, tan_out), (diag_in, diag_out)))
+        for f in range(FIELDS)
+    ]
+    for copy in copies:
+        copy.start()
+    for copy in copies:
+        copy.wait()
 
 
 def per_device(bands, row_signs, col_signs, spread, east_wind, north_wind, cutoffs):
@@ -583,10 +562,10 @@
     tables = [jnp.asarray(table) for table in (half_metric(bands),) + mode_factors()]
     vmem = pltpu.VMEM
     dma = pltpu.SemaphoreType.DMA
-    return pl.pallas_call(
+    results = pl.pallas_call(
         functools.partial(kernel, bands),
         out_shape=(out, out),
-        in_specs=[any_spec] * 11,
+        in_specs=[any_spec] * 9,
         out_specs=(any_spec, any_spec),
         scratch_shapes=[
             vmem((FIELDS, LEV, ROWS, COLS), F32),
@@ -596,10 +575,8 @@
             vmem((FIELDS, LEV, COLS), jnp.int32),
             pltpu.SMEM((ROWS,), jnp.int32),
             vmem((32, 128), F32),
-            vmem((RANK, WIDE), BF16),
-            vmem((RANK, WIDE), BF16),
-            vmem((4, 2 * RANK, 2 * 64), BF16),
-            vmem((4, 2 * RANK, 2 * 64), BF16),
+            vmem((3 * RANK, WIDE), BF16),
+            vmem((4, 2 * RANK, 4 * 64), BF16),
             vmem((PAIRS + 2 * LEV, 32, WIDE), F32),
             vmem((2, 10, LEV, WIDE), F32),
             vmem((2, 10, LEV, WIDE), F32),
@@ -608,8 +585,8 @@
             vmem((2, ROWS, 128), F32),
             vmem((2, LANES, 2 * PAIRS, RANK), F32),
             vmem((2, LANES, 2 * PAIRS, RANK), F32),
-            vmem((2, LANES, 2 * PAIRS, RANK), F32),
-            vmem((2, LANES, 2 * PAIRS, RANK), F32),
+            vmem((LANES, 2, 2 * PAIRS, RANK), F32),
+            vmem((LANES, 2, 2 * PAIRS, RANK), F32),
             vmem((2, 2, PAIRS, RANK), F32),
             vmem((PAIRS, ROWS, WIDE), F32),
             vmem((PAIRS, ROWS, WIDE), F32),
@@ -620,7 +597,7 @@
             vmem((PAIRS, 32, WIDE), F32),
             vmem((FIELDS, LEV, ROWS, COLS), F32),
             vmem((FIELDS, LEV, ROWS, COLS), F32),
-            dma((11,)),
+            dma((9,)),
             dma((2,)),
             dma((2,)),
             dma((2, 2)),
@@ -629,10 +606,10 @@
             dma((2,)),
             dma((2, LANES)),
             dma((2, LANES)),
-            dma((2, LANES)),
-            dma((2, LANES)),
-            dma((2, LANES)),
-            dma((2, 2)),
+            dma((LANES,)),
+            dma((LANES,)),
+            dma((2,)),
+            dma((2,)),
             dma((2,)),
         ],
         compiler_params=pltpu.CompilerParams(
@@ -640,6 +617,14 @@
         ),
         cost_estimate=pl.CostEstimate(flops=10**9, bytes_accessed=4 * 10**6, transcendentals=0),
     )(spread, east_wind, north_wind, row_signs, col_signs, cutoffs, *tables)
+    return pl.pallas_call(
+        hand_out,
+        out_shape=(out, out),
+        in_specs=[any_spec] * 2,
+        out_specs=(any_spec, any_spec),
+        scratch_shapes=[dma((2, FIELDS))],
+        compiler_params=pltpu.CompilerParams(vmem_limit_bytes=64 * 2**20),
+    )(*results)
 
 
 def solution(mesh):

time: 29.3 us -> 60.1 us (2.05)
  Pallas kernels: 25.8 us -> 59.4 us
  local copies, waits for them, and re-layouts: 2.74 us -> 0 us
    pallas_call x0 -> x1, Pallas kernels: none -> 32.9 us  [per_device(): pl.pallas_call(hand_out, out_shape=(out, out), in_specs=[any_spec] * 2, o...]
    unnamed x4 -> x0, local copies, waits for them, and re-layouts: 2.74 us -> none
where the time goes in v3:
time: 60.1 us; the launch traced here: 60 us
  Pallas kernels  59.4 us (99%)
  between operations  0.64 us (1%)
    pallas_call x1, Pallas kernels, per_device(): pl.pallas_call(hand_out, out_shape=(out, out), in_specs=[any_spec] * 2, o...  32.9 us
    pallas_call x1, Pallas kernels, per_device(): pl.pallas_call(functools.partial(kernel, bands), out_shape=(out, out), in...  26.4 us

profile of v3, /device:TPU:1, one launch (start us, length us, event | category | flops | bytes accessed | tf_op | source)
XLA Modules:
  0.0 60.0 jit_solution(16540104196547158781)
XLA Ops:
  0.6 26.4 %shard_map.104 = (f32[4,4,16,450]{3,2,1,0:T(8,128)}, f32[4,4,16,450]{3,2,1,0:T(8,128)}) custom-call(f32[4,4,16,450]{3,2,1,0:T(8,128)} %spread.1, f32[4,16,450]{2,1,0:T(8,128)} %east.1, f32[4,16,450]{2,1,0:T(8,128)} %north.1, s32[4,4,16]{2,1,0:T(4,128)} %rs.1, s32[4,4,450]{2,1,0:T(4,128)} %cs.1, s32[16]{0:T(128)} %cut.1, ...), custom_call_target="tpu_custom_call" | custom-call | flops 1000000000 | bytes 4000000 | tf_op jit(solution)/shard_map/pallas_call | solution.py:565
  27.1 32.9 %shard_map.105 = (f32[4,4,16,450]{3,2,1,0:T(8,128)}, f32[4,4,16,450]{3,2,1,0:T(8,128)}) custom-call(f32[4,4,16,450]{3,2,1,0:T(8,128)} %get-tuple-element.4.tan_in, f32[4,4,16,450]{3,2,1,0:T(8,128)} %get-tuple-element.5.diag_in), custom_call_target="tpu_custom_call" | custom-call | tf_op jit(solution)/shard_map/pallas_call | solution.py:620

commit v4 on v3

--- a/solution.py
+++ b/solution.py
@@ -152,7 +152,7 @@
 def kernel(
     bands, spread, east, north, rs, cs, cut, metric, q3_in, w2_in, tan_out, diag_out,
     spread_v, east_v, north_v, rs_v, cs_v, cut_s, hm, q3, w2,
-    grid, er, hr, hc, cp, hcol, ybuf, yr, zbuf, zr, bz,
+    grid, er, hr, hc, cp, hcol, ybuf, yr, zbuf, zr, eb, bz,
     tend, proj_p, proj_t, edge_t, edge_proj, adj, gy, tan_v, diag_v,
     in_sem, row_send, row_recv, cor_send, cor_recv, col_send, col_recv,
     y_send, y_recv, z_send, z_recv, b_send, b_recv, out_sem,
@@ -174,7 +174,6 @@
     sl = jnp.where(is_south, across, i)
     slot_n = jnp.where(is_north, 0, 1)
     slot_s = jnp.where(is_south, 1, 0)
-    first, last = 0, LANES - 1
 
     def plus(lane, d):
         return lax.rem(lane + d, LANES)
@@ -281,80 +280,98 @@
     def y_arrival(q, j):
         return remote(ybuf.at[q, j], yr.at[q, j], y_send.at[q, j], y_recv.at[q, j], b, j)
 
-    def send_row_values(q, x):
-        y = to_modes(dot_rows, jnp.where(own_cols, x, 0.0), q3[0 : 2 * RANK, :], q3[0:RANK, :])
-        y = jnp.swapaxes(y.reshape(PAIRS, ROWS, RANK), 0, 1)
-        ybuf[q] = y.reshape(LANES, 2 * PAIRS, RANK)
+    def row_values(x):
+        return to_modes(dot_rows, jnp.where(own_cols, x, 0.0), q3[0 : 2 * RANK, :], q3[0:RANK, :])
+
+    def send_probe_values():
+        y = row_values(grid[0:PAIRS, 8:24, :].reshape(PAIRS * ROWS, WIDE)).reshape(FIELDS, LEV, 2, 8, RANK)
+        for f in range(FIELDS):
+            for h in range(2):
+                for l in range(LEV):
+                    ybuf[0, 2 * f + h, l] = y[f, l, h]
 
         @pl.loop(1, LANES)
         def _(d):
-            y_copy(q, plus(i, d)).start()
-
-        yr[q, i] = ybuf[q, i]
-
-    def z_copy(j):
-        return remote(zbuf.at[j], zr.at[i], z_send.at[j], z_recv.at[i], b, j)
-
-    def z_arrival(j):
-        return remote(zbuf.at[j], zr.at[j], z_send.at[j], z_recv.at[j], b, j)
-
-    def own_rows():
-        for q in range(2):
-            @pl.loop(1, LANES)
-            def _(d):
-                y_arrival(q, plus(i, d)).wait_recv()
+            y_copy(0, plus(i, d)).start()
+
+        yr[0, i] = ybuf[0, i]
+
+    def send_tendency_values(h):
+        y = row_values(tend[:, 8 * h : 8 * h + 8, :].reshape(PAIRS * 8, WIDE)).reshape(FIELDS, LEV, 8, RANK)
+        for f in range(FIELDS):
+            ybuf[1, 2 * f + h] = y[f]
+
+        @pl.loop(0, FIELDS)
+        def _(d):
+            o = 2 * lax.rem(i // 2 + d, FIELDS) + h
+
+            @pl.when(o != i)
+            def _():
+                y_copy(1, o).start()
+
+            @pl.when(o == i)
+            def _():
+                yr[1, i] = ybuf[1, i]
+
+    def z_copy(q, j):
+        return remote(zbuf.at[q, j], zr.at[q, i], z_send.at[q, j], z_recv.at[q, i], b, j)
+
+    def z_arrival(q, j):
+        return remote(zbuf.at[q, j], zr.at[q, j], z_send.at[q, j], z_recv.at[q, j], b, j)
+
+    def own_rows(q):
+        row = lax.broadcasted_iota(jnp.int32, (8, 128), 0)
+        cutoff = jnp.zeros((8, 128), jnp.int32)
+        for r in range(8):
+            cutoff = jnp.where(row == r, cut_s[8 * lax.rem(i, 2) + r], cutoff)
+
+        @pl.loop(1, LANES)
+        def _(d):
+            y_arrival(q, plus(i, d)).wait_recv()
 
         pairs = []
-        over = over_lanes([yr[:, j].reshape(4 * PAIRS, RANK) for j in range(LANES)])
+        over = over_lanes([yr[q, j].reshape(LEV * 8, RANK) for j in range(LANES)])
         for group, pair in enumerate(over):
             coef = to_modes(dot_cols, jnp.concatenate(pair, axis=1), w2[group], w2[group, :, 0:128])
-            wave = waves_of(group, lax.broadcasted_iota(jnp.int32, (PAIRS, 128), 1))
-            keep = [jnp.where(wave > cut_s[2 * i + part], 2.0 / (COLS * LANES), 0.0) for part in range(2)]
-            high, low = split(coef * jnp.concatenate(keep + keep, axis=0))
+            wave = waves_of(group, lax.broadcasted_iota(jnp.int32, (8, 128), 1))
+            keep = jnp.where(wave > cutoff, 2.0 / (COLS * LANES), 0.0)
+            high, low = split(coef * jnp.concatenate([keep] * LEV, axis=0))
             back = dot_rows(jnp.concatenate([high, high], axis=1), w2[group])
             back = back + dot_rows(low, w2[group, :, 0:128])
             pairs.append((back[:, :RANK], back[:, RANK:]))
         for j, z in enumerate(to_lanes(pairs)):
-            zbuf[j] = z.reshape(2, 2 * PAIRS, RANK)
+            zbuf[q, j] = z.reshape(LEV, 8, RANK)
 
         @pl.loop(1, LANES)
         def _(d):
-            z_copy(plus(i, d)).start()
-
-        zr[i] = zbuf[i]
-
-    def edge_sends():
-        return (
-            remote(zr.at[first, :, 0:PAIRS], bz.at[slot_n], b_send.at[0], b_recv.at[slot_n], nb, nl),
-            remote(zr.at[last, :, PAIRS : 2 * PAIRS], bz.at[slot_s], b_send.at[1], b_recv.at[slot_s], sb, sl),
-        )
-
-    def project():
-        for owner, send in zip((first, last), edge_sends()):
-            @pl.when(i != owner)
-            def _():
-                z_arrival(owner).wait_recv()
-
-            send.start()
-
+            z_copy(q, plus(i, d)).start()
+
+        zr[q, i] = zbuf[q, i]
+
+    def edge_send(q, s):
+        slot, lat, lon = ((slot_n, nb, nl), (slot_s, sb, sl))[s]
+        return remote(eb.at[s, q], bz.at[slot, q], b_send.at[s, q], b_recv.at[slot, q], lat, lon)
+
+    def project(q, out):
         @pl.loop(1, LANES)
         def _(d):
-            j = plus(i, d)
-
-            @pl.when(jnp.logical_and(j != first, j != last))
-            def _():
-                z_arrival(j).wait_recv()
-
-        for q, out in enumerate((proj_p, proj_t)):
-            z = jnp.swapaxes(zr[:, q].reshape(ROWS, PAIRS, RANK), 0, 1).reshape(PAIRS * ROWS, RANK)
-            out[...] = evaluate(z, q3).reshape(PAIRS, ROWS, WIDE)
+            z_arrival(q, plus(i, d)).wait_recv()
+
+        for s, row in ((0, 0), (1, 7)):
+            for f in range(FIELDS):
+                eb[s, q, f * LEV : (f + 1) * LEV, :] = zr[q, 2 * f + s, :, row, :]
+            edge_send(q, s).start()
+        z = jnp.concatenate(
+            [zr[q, 2 * f + h, l] for f in range(FIELDS) for l in range(LEV) for h in range(2)], axis=0
+        )
+        out[...] = evaluate(z, q3).reshape(PAIRS, ROWS, WIDE)
 
     for load in loads[5:]:
         load.wait()
 
     @pl.when(polar)
     def _():
-        send_row_values(0, grid[0:PAIRS, 8:24, :].reshape(PAIRS * ROWS, WIDE))
+        send_probe_values()
 
     for s in range(2):
         remote(er.at[s], hr.at[s], row_send.at[s], row_recv.at[s], nb, nl).wait_recv()
@@ -393,11 +410,11 @@
             flip = jnp.where(over_pole[s], flips[f], 1.0)
             grid[f * LEV : (f + 1) * LEV, edge_row[s], :] = flip * edge_probe[s][f]
 
-    @pl.loop(0, LEV)
-    def _(l):
-        lo = jnp.maximum(l - 1, 0)
-        hi = jnp.minimum(l + 1, LEV - 1)
-        for h in (8, 16):
+    def tendency_rows(h):
+        @pl.loop(0, LEV)
+        def _(l):
+            lo = jnp.maximum(l - 1, 0)
+            hi = jnp.minimum(l + 1, LEV - 1)
             half = jnp.concatenate([hm[h : h + 8, :]] * 4, axis=1)
             ew = grid[PAIRS + l, h : h + 8, :]
             nw = grid[PAIRS + LEV + l, h : h + 8, :]
@@ -415,9 +432,17 @@
                     t = t - coupling * linked[f]
                 tend[f * LEV + l, h - 8 : h, :] = t
 
+    for part in range(2):
+        tendency_rows(8 + 8 * part)
+
+        @pl.when(polar)
+        def _():
+            send_tendency_values(part)
+
     @pl.when(polar)
     def _():
-        send_row_values(1, tend[...].reshape(PAIRS * ROWS, WIDE))
+        table_load.wait()
+        own_rows(0)
 
     for s in range(2):
         centers = edge_probe[s]
@@ -440,9 +465,9 @@
 
     @pl.when(polar)
     def _():
-        table_load.wait()
-        own_rows()
-        project()
+        own_rows(1)
+        project(0, proj_p)
+        project(1, proj_t)
 
     @pl.when(jnp.logical_not(polar))
     def _():
@@ -479,7 +504,8 @@
     for s, wanted in enumerate((above_polar, below_polar)):
         @pl.when(wanted)
         def _():
-            remote(zr.at[first, :, 0:PAIRS], bz.at[s], b_send.at[0], b_recv.at[s], nb, nl).wait_recv()
+            for q in range(2):
+                remote(eb.at[s, q], bz.at[s, q], b_send.at[s, q], b_recv.at[s, q], nb, nl).wait_recv()
             edge_proj[s] = evaluate(bz[s].reshape(2 * PAIRS, RANK), q3).reshape(2, PAIRS, WIDE)
 
         @pl.when(jnp.logical_not(wanted))
@@ -533,27 +559,34 @@
         @pl.loop(1, LANES)
         def _(d):
             j = plus(i, d)
-            y_copy(0, j).wait_send()
-            y_copy(1, j).wait_send()
-            z_copy(j).wait_send()
-
-        for send in edge_sends():
-            send.wait_send()
+            for q in range(2):
+                y_copy(q, j).wait_send()
+                z_copy(q, j).wait_send()
+
+        for q in range(2):
+            for s in range(2):
+                edge_send(q, s).wait_send()
 
     tan_copy.wait()
     diag_copy.wait()
 
 
-def hand_out(tan_in, diag_in, tan_out, diag_out, sem):
-    copies = [
-        pltpu.make_async_copy(src.at[f], dst.at[f], sem.at[n, f])
+def hand_out(tan_in, diag_in, tan_out, diag_out, held, in_sem, out_sem):
+    ways = [
+        (
+            pltpu.make_async_copy(src.at[f], held.at[n, f], in_sem.at[n, f]),
+            pltpu.make_async_copy(held.at[n, f], dst.at[f], out_sem.at[n, f]),
+        )
         for n, (src, dst) in enumerate(((tan_in, tan_out), (diag_in, diag_out)))
         for f in range(FIELDS)
     ]
-    for copy in copies:
-        copy.start()
-    for copy in copies:
-        copy.wait()
+    for arrive, leave in ways:
+        arrive.start()
+    for arrive, leave in ways:
+        arrive.wait()
+        leave.start()
+    for arrive, leave in ways:
+        leave.wait()
 
 
 def per_device(bands, row_signs, col_signs, spread, east_wind, north_wind, cutoffs):
@@ -583,10 +616,11 @@
             vmem((2, 2, FIELDS, LEV, 128), F32),
             vmem((2, ROWS, 128), F32),
             vmem((2, ROWS, 128), F32),
-            vmem((2, LANES, 2 * PAIRS, RANK), F32),
-            vmem((2, LANES, 2 * PAIRS, RANK), F32),
-            vmem((LANES, 2, 2 * PAIRS, RANK), F32),
-            vmem((LANES, 2, 2 * PAIRS, RANK), F32),
+            vmem((2, LANES, LEV, 8, RANK), F32),
+            vmem((2, LANES, LEV, 8, RANK), F32),
+            vmem((2, LANES, LEV, 8, RANK), F32),
+            vmem((2, LANES, LEV, 8, RANK), F32),
+            vmem((2, 2, PAIRS, RANK), F32),
             vmem((2, 2, PAIRS, RANK), F32),
             vmem((PAIRS, ROWS, WIDE), F32),
             vmem((PAIRS, ROWS, WIDE), F32),
@@ -606,10 +640,10 @@
             dma((2,)),
             dma((2, LANES)),
             dma((2, LANES)),
-            dma((LANES,)),
-            dma((LANES,)),
-            dma((2,)),
-            dma((2,)),
+            dma((2, LANES)),
+            dma((2, LANES)),
+            dma((2, 2)),
+            dma((2, 2)),
             dma((2,)),
         ],
         compiler_params=pltpu.CompilerParams(
@@ -622,7 +656,7 @@
         out_shape=(out, out),
         in_specs=[any_spec] * 2,
         out_specs=(any_spec, any_spec),
-        scratch_shapes=[dma((2, FIELDS))],
+        scratch_shapes=[vmem((2, FIELDS, LEV, ROWS, COLS), F32), dma((2, FIELDS)), dma((2, FIELDS))],
         compiler_params=pltpu.CompilerParams(vmem_limit_bytes=64 * 2**20),
     )(*results)
 

time: 60.1 us -> 30.3 us (0.50)
  the two profiles are of different devices: /device:TPU:1 before, /device:TPU:225 now
where the time goes in v4:
time: 30.3 us; the launch traced here: 30.2 us
  Pallas kernels  29.6 us (98%)
  between operations  0.64 us (2%)
    pallas_call x1, Pallas kernels, per_device(): pl.pallas_call(functools.partial(kernel, bands), out_shape=(out, out), in...  27.5 us
    pallas_call x1, Pallas kernels, per_device(): pl.pallas_call(hand_out, out_shape=(out, out), in_specs=[any_spec] * 2, o...  2.09 us

profile of v4, /device:TPU:225, one launch (start us, length us, event | category | flops | bytes accessed | tf_op | source)
XLA Modules:
  0.0 30.2 jit_solution(11203557470374348671)
XLA Ops:
  0.6 27.5 %shard_map.104 = (f32[4,4,16,450]{3,2,1,0:T(8,128)}, f32[4,4,16,450]{3,2,1,0:T(8,128)}) custom-call(f32[4,4,16,450]{3,2,1,0:T(8,128)} %spread.1, f32[4,16,450]{2,1,0:T(8,128)} %east.1, f32[4,16,450]{2,1,0:T(8,128)} %north.1, s32[4,4,16]{2,1,0:T(4,128)} %rs.1, s32[4,4,450]{2,1,0:T(4,128)} %cs.1, s32[16]{0:T(128)} %cut.1, ...), custom_call_target="tpu_custom_call" | custom-call | flops 1000000000 | bytes 4000000 | tf_op jit(solution)/shard_map/pallas_call | solution.py:598
  28.1 2.1 %shard_map.105 = (f32[4,4,16,450]{3,2,1,0:T(8,128)}, f32[4,4,16,450]{3,2,1,0:T(8,128)}) custom-call(f32[4,4,16,450]{3,2,1,0:T(8,128)} %get-tuple-element.4.tan_in, f32[4,4,16,450]{3,2,1,0:T(8,128)} %get-tuple-element.5.diag_in), custom_call_target="tpu_custom_call" | custom-call | tf_op jit(solution)/shard_map/pallas_call | solution.py:654

commit v5 on v4

--- a/solution.py
+++ b/solution.py
@@ -73,7 +73,15 @@
     wide[:, WIDE - 1] = basis[0]
     wide = np.round(wide * 2.0**26) / 2.0**26
     wide_h, wide_l = split_table(wide)
-    return np.concatenate([wide_h, wide_l, wide_h], axis=0), np.concatenate(split_table(weights), axis=2)
+    own = np.where(np.arange(WIDE)[:, None] < COLS, 1, 0).astype(ml_dtypes.bfloat16)
+    high, low = split_table(weights)
+    back = [np.swapaxes(part, 1, 2) for part in (high, low, high)]
+    return (
+        np.concatenate([wide_h.T * own, wide_l.T * own], axis=1),
+        np.concatenate([wide_h, wide_l, wide_h], axis=0),
+        np.concatenate([high, low], axis=2),
+        np.concatenate(back, axis=1),
+    )
 
 
 ROOT = float(np.sqrt(0.5))
@@ -109,10 +117,6 @@
     return np.broadcast_to((0.5 * metric).astype(np.float32)[:, :, None], (bands, 32, 128)).copy()
 
 
-def dot_rows(a, b):
-    return lax.dot_general(a, b, (((1,), (1,)), ((), ())), preferred_element_type=F32)
-
-
 def dot_cols(a, b):
     return lax.dot_general(a, b, (((1,), (0,)), ((), ())), preferred_element_type=F32)
 
@@ -122,14 +126,14 @@
     return high, (x - high.astype(F32)).astype(BF16)
 
 
-def to_modes(dot, x, both, high):
+def to_modes(x, table):
     xh, xl = split(x)
-    wide = dot(xh, both)
-    half = wide.shape[1] // 2
-    return wide[:, :half] + wide[:, half:] + dot(xl, high)
-
-
-def evaluate(z, table):
+    half = table.shape[1] // 2
+    wide = dot_cols(xh, table[...])
+    return wide[:, :half] + wide[:, half:] + dot_cols(xl, table[:, 0:half])
+
+
+def from_modes(z, table):
     zh, zl = split(z)
     return dot_cols(jnp.concatenate([zh, zh, zl], axis=1), table[...])
 
@@ -150,8 +154,8 @@
 
 
 def kernel(
-    bands, spread, east, north, rs, cs, cut, metric, q3_in, w2_in, tan_out, diag_out,
-    spread_v, east_v, north_v, rs_v, cs_v, cut_s, hm, q3, w2,
+    bands, spread, east, north, rs, cs, cut, metric, qf_in, qe_in, wf_in, wb_in, tan_out, diag_out,
+    spread_v, east_v, north_v, rs_v, cs_v, cut_s, hm, qf, qe, wf, wb,
     grid, er, hr, hc, cp, hcol, ybuf, yr, zbuf, zr, eb, bz,
     tend, proj_p, proj_t, edge_t, edge_proj, adj, gy, tan_v, diag_v,
     in_sem, row_send, row_recv, cor_send, cor_recv, col_send, col_recv,
@@ -186,15 +190,20 @@
         pltpu.make_async_copy(north, north_v, in_sem.at[4]),
         pltpu.make_async_copy(metric.at[b], hm, in_sem.at[5]),
         pltpu.make_async_copy(cut, cut_s, in_sem.at[6]),
-        pltpu.make_async_copy(q3_in, q3, in_sem.at[7]),
+        pltpu.make_async_copy(qe_in, qe, in_sem.at[7]),
     ]
-    table_load = pltpu.make_async_copy(w2_in, w2, in_sem.at[8])
+    table_loads = [
+        pltpu.make_async_copy(qf_in, qf, in_sem.at[8]),
+        pltpu.make_async_copy(wf_in, wf, in_sem.at[9]),
+        pltpu.make_async_copy(wb_in, wb, in_sem.at[10]),
+    ]
     for load in loads:
         load.start()
 
     @pl.when(polar)
     def _():
-        table_load.start()
+        for load in table_loads:
+            load.start()
 
     barrier = pltpu.get_barrier_semaphore()
 
@@ -215,6 +224,16 @@
         @pl.loop(1, LANES)
         def _(d):
             greet(b, plus(i, d))
+
+    @pl.when(jnp.logical_and(above_polar, jnp.logical_not(is_north)))
+    def _():
+        for f in range(FIELDS):
+            greet(nb, 2 * f + 1)
+
+    @pl.when(jnp.logical_and(below_polar, jnp.logical_not(is_south)))
+    def _():
+        for f in range(FIELDS):
+            greet(sb, 2 * f)
 
     for load in loads[:5]:
         load.wait()
@@ -242,7 +261,14 @@
         packed = fold(tile[:PAIRS]) + roll_blocks(fold(tile[PAIRS:]), 2 * PAIRS)
         cp[s] = roll_blocks(packed, -shift)[0]
 
-    pl.semaphore_wait(barrier, 8 + jnp.where(polar, LANES - 1, 0))
+    own_half = lax.rem(i, 2)
+    edge_over = jnp.where(own_half == 0, is_north, is_south)
+    pl.semaphore_wait(
+        barrier,
+        8
+        + jnp.where(polar, LANES - 1, 0)
+        + jnp.where(jnp.logical_and(polar, jnp.logical_not(edge_over)), LANES, 0),
+    )
 
     def remote(src, dst, send, recv, lat, lon):
         return pltpu.make_async_remote_copy(
@@ -250,8 +276,12 @@
         )
 
     halo_sends = [
-        remote(er.at[0], hr.at[slot_n], row_send.at[0], row_recv.at[slot_n], nb, nl),
-        remote(er.at[1], hr.at[slot_s], row_send.at[1], row_recv.at[slot_s], sb, sl),
+        remote(
+            er.at[0, 0:FIELDS], hr.at[slot_n, 0:FIELDS], row_send.at[0, 0], row_recv.at[slot_n, 0], nb, nl
+        ),
+        remote(
+            er.at[1, 0:FIELDS], hr.at[slot_s, 0:FIELDS], row_send.at[1, 0], row_recv.at[slot_s, 0], sb, sl
+        ),
         remote(cp.at[0], hcol.at[1], col_send.at[0], col_recv.at[1], b, west),
         remote(cp.at[1], hcol.at[0], col_send.at[1], col_recv.at[0], b, east_lane),
     ]
@@ -268,23 +298,21 @@
                 lat, plus(lon, LANES - 1),
             )
         )
+    halo_sends += [
+        remote(er.at[0, FIELDS:10], hr.at[slot_n, FIELDS:10], row_send.at[0, 1], row_recv.at[slot_n, 1], nb, nl),
+        remote(er.at[1, FIELDS:10], hr.at[slot_s, FIELDS:10], row_send.at[1, 1], row_recv.at[slot_s, 1], sb, sl),
+    ]
     for send in halo_sends:
         send.start()
 
-    lane512 = lax.broadcasted_iota(jnp.int32, (1, WIDE), 1)
-    own_cols = lane512 < COLS
-
     def y_copy(q, o):
         return remote(ybuf.at[q, o], yr.at[q, i], y_send.at[q, o], y_recv.at[q, i], b, o)
 
     def y_arrival(q, j):
         return remote(ybuf.at[q, j], yr.at[q, j], y_send.at[q, j], y_recv.at[q, j], b, j)
 
-    def row_values(x):
-        return to_modes(dot_rows, jnp.where(own_cols, x, 0.0), q3[0 : 2 * RANK, :], q3[0:RANK, :])
-
     def send_probe_values():
-        y = row_values(grid[0:PAIRS, 8:24, :].reshape(PAIRS * ROWS, WIDE)).reshape(FIELDS, LEV, 2, 8, RANK)
+        y = to_modes(grid[0:PAIRS, 8:24, :].reshape(PAIRS * ROWS, WIDE), qf).reshape(FIELDS, LEV, 2, 8, RANK)
         for f in range(FIELDS):
             for h in range(2):
                 for l in range(LEV):
@@ -297,7 +325,7 @@
         yr[0, i] = ybuf[0, i]
 
     def send_tendency_values(h):
-        y = row_values(tend[:, 8 * h : 8 * h + 8, :].reshape(PAIRS * 8, WIDE)).reshape(FIELDS, LEV, 8, RANK)
+        y = to_modes(tend[:, 8 * h : 8 * h + 8, :].reshape(PAIRS * 8, WIDE), qf).reshape(FIELDS, LEV, 8, RANK)
         for f in range(FIELDS):
             ybuf[1, 2 * f + h] = y[f]
 
@@ -323,7 +351,7 @@
         row = lax.broadcasted_iota(jnp.int32, (8, 128), 0)
         cutoff = jnp.zeros((8, 128), jnp.int32)
         for r in range(8):
-            cutoff = jnp.where(row == r, cut_s[8 * lax.rem(i, 2) + r], cutoff)
+            cutoff = jnp.where(row == r, cut_s[8 * own_half + r], cutoff)
 
         @pl.loop(1, LANES)
         def _(d):
@@ -332,15 +360,15 @@
         pairs = []
         over = over_lanes([yr[q, j].reshape(LEV * 8, RANK) for j in range(LANES)])
         for group, pair in enumerate(over):
-            coef = to_modes(dot_cols, jnp.concatenate(pair, axis=1), w2[group], w2[group, :, 0:128])
+            coef = to_modes(jnp.concatenate(pair, axis=1), wf.at[group])
             wave = waves_of(group, lax.broadcasted_iota(jnp.int32, (8, 128), 1))
             keep = jnp.where(wave > cutoff, 2.0 / (COLS * LANES), 0.0)
-            high, low = split(coef * jnp.concatenate([keep] * LEV, axis=0))
-            back = dot_rows(jnp.concatenate([high, high], axis=1), w2[group])
-            back = back + dot_rows(low, w2[group, :, 0:128])
+            back = from_modes(coef * jnp.concatenate([keep] * LEV, axis=0), wb.at[group])
             pairs.append((back[:, :RANK], back[:, RANK:]))
         for j, z in enumerate(to_lanes(pairs)):
-            zbuf[q, j] = z.reshape(LEV, 8, RANK)
+            z = z.reshape(LEV, 8, RANK)
+            zbuf[q, j] = z
+            eb[j, LEV * q : LEV * (q + 1), :] = jnp.where(own_half == 0, z[:, 0, :], z[:, 7, :])
 
         @pl.loop(1, LANES)
         def _(d):
@@ -348,33 +376,58 @@
 
         zr[q, i] = zbuf[q, i]
 
-    def edge_send(q, s):
-        slot, lat, lon = ((slot_n, nb, nl), (slot_s, sb, sl))[s]
-        return remote(eb.at[s, q], bz.at[slot, q], b_send.at[s, q], b_recv.at[slot, q], lat, lon)
+    def edge_sends(act):
+        slot = jnp.where(own_half == 0, slot_n, slot_s)
+        lat = jnp.where(own_half == 0, nb, sb)
+
+        @pl.loop(0, LANES)
+        def _(d):
+            j = plus(i, d)
+            lon = jnp.where(edge_over, plus(j, LANES // 2), j)
+            here = jnp.logical_and(edge_over, lon == i)
+
+            @pl.when(jnp.logical_not(here))
+            def _():
+                act(
+                    remote(
+                        eb.at[j], bz.at[slot, i // 2], b_send.at[j], b_recv.at[slot, i // 2], lat, lon
+                    )
+                )
+
+            if act is start_copy:
+                @pl.when(here)
+                def _():
+                    pltpu.make_async_copy(eb.at[j], bz.at[slot, i // 2], b_recv.at[slot, i // 2]).start()
+
+    def start_copy(copy):
+        copy.start()
+
+    def end_copy(copy):
+        copy.wait_send()
 
     def project(q, out):
         @pl.loop(1, LANES)
         def _(d):
             z_arrival(q, plus(i, d)).wait_recv()
 
-        for s, row in ((0, 0), (1, 7)):
-            for f in range(FIELDS):
-                eb[s, q, f * LEV : (f + 1) * LEV, :] = zr[q, 2 * f + s, :, row, :]
-            edge_send(q, s).start()
         z = jnp.concatenate(
             [zr[q, 2 * f + h, l] for f in range(FIELDS) for l in range(LEV) for h in range(2)], axis=0
         )
-        out[...] = evaluate(z, q3).reshape(PAIRS, ROWS, WIDE)
+        out[...] = from_modes(z, qe).reshape(PAIRS, ROWS, WIDE)
 
     for load in loads[5:]:
         load.wait()
 
     @pl.when(polar)
     def _():
+        for load in table_loads:
+            load.wait()
         send_probe_values()
 
     for s in range(2):
-        remote(er.at[s], hr.at[s], row_send.at[s], row_recv.at[s], nb, nl).wait_recv()
+        remote(
+            er.at[s, 0:FIELDS], hr.at[s, 0:FIELDS], row_send.at[s, 0], row_recv.at[s, 0], nb, nl
+        ).wait_recv()
         remote(cp.at[s], hcol.at[s], col_send.at[s], col_recv.at[s], b, west).wait_recv()
         for side in range(2):
             remote(
@@ -441,10 +494,12 @@
 
     @pl.when(polar)
     def _():
-        table_load.wait()
         own_rows(0)
 
     for s in range(2):
+        remote(
+            er.at[s, FIELDS:10], hr.at[s, FIELDS:10], row_send.at[s, 1], row_recv.at[s, 1], nb, nl
+        ).wait_recv()
         centers = edge_probe[s]
         half = jnp.concatenate([hm[edge_row[s] : edge_row[s] + 1, :]] * 4, axis=1)
         turn = jnp.where(over_pole[s], -inward[s], inward[s])
@@ -466,6 +521,7 @@
     @pl.when(polar)
     def _():
         own_rows(1)
+        edge_sends(start_copy)
         project(0, proj_p)
         project(1, proj_t)
 
@@ -504,22 +560,21 @@
     for s, wanted in enumerate((above_polar, below_polar)):
         @pl.when(wanted)
         def _():
-            for q in range(2):
-                remote(eb.at[s, q], bz.at[s, q], b_send.at[s, q], b_recv.at[s, q], nb, nl).wait_recv()
-            edge_proj[s] = evaluate(bz[s].reshape(2 * PAIRS, RANK), q3).reshape(2, PAIRS, WIDE)
+            for f in range(FIELDS):
+                remote(eb.at[f], bz.at[s, f], b_send.at[f], b_recv.at[s, f], nb, nl).wait_recv()
+            edge_proj[s] = from_modes(bz[s].reshape(2 * PAIRS, RANK), qe).reshape(FIELDS, 2 * LEV, WIDE)
 
         @pl.when(jnp.logical_not(wanted))
         def _():
-            edge_proj[s] = jnp.zeros((2, PAIRS, WIDE), F32)
+            edge_proj[s] = jnp.zeros((FIELDS, 2 * LEV, WIDE), F32)
 
     for s in range(2):
         a = []
         for f in range(FIELDS):
-            rows = slice(f * LEV, (f + 1) * LEV)
             a.append(
                 edge_probe[s][f]
-                + time_step * (edge_t[s, f] - edge_proj[s, 1, rows, :])
-                - edge_proj[s, 0, rows, :]
+                + time_step * (edge_t[s, f] - edge_proj[s, f, LEV : 2 * LEV, :])
+                - edge_proj[s, f, 0:LEV, :]
             )
         for f, weight in enumerate(row_weights(a, hr[s, 9])):
             flip = jnp.where(over_pole[s], -flips[f], 1.0)
@@ -563,9 +618,7 @@
                 y_copy(q, j).wait_send()
                 z_copy(q, j).wait_send()
 
-        for q in range(2):
-            for s in range(2):
-                edge_send(q, s).wait_send()
+        edge_sends(end_copy)
 
     tan_copy.wait()
     diag_copy.wait()
@@ -598,7 +651,7 @@
     results = pl.pallas_call(
         functools.partial(kernel, bands),
         out_shape=(out, out),
-        in_specs=[any_spec] * 9,
+        in_specs=[any_spec] * 11,
         out_specs=(any_spec, any_spec),
         scratch_shapes=[
             vmem((FIELDS, LEV, ROWS, COLS), F32),
@@ -608,8 +661,10 @@
             vmem((FIELDS, LEV, COLS), jnp.int32),
             pltpu.SMEM((ROWS,), jnp.int32),
             vmem((32, 128), F32),
+            vmem((WIDE, 2 * RANK), BF16),
             vmem((3 * RANK, WIDE), BF16),
             vmem((4, 2 * RANK, 4 * 64), BF16),
+            vmem((4, 6 * 64, 2 * RANK), BF16),
             vmem((PAIRS + 2 * LEV, 32, WIDE), F32),
             vmem((2, 10, LEV, WIDE), F32),
             vmem((2, 10, LEV, WIDE), F32),
@@ -620,20 +675,20 @@
             vmem((2, LANES, LEV, 8, RANK), F32),
             vmem((2, LANES, LEV, 8, RANK), F32),
             vmem((2, LANES, LEV, 8, RANK), F32),
-            vmem((2, 2, PAIRS, RANK), F32),
-            vmem((2, 2, PAIRS, RANK), F32),
+            vmem((LANES, 2 * LEV, RANK), F32),
+            vmem((2, FIELDS, 2 * LEV, RANK), F32),
             vmem((PAIRS, ROWS, WIDE), F32),
             vmem((PAIRS, ROWS, WIDE), F32),
             vmem((PAIRS, ROWS, WIDE), F32),
             vmem((2, FIELDS, LEV, WIDE), F32),
-            vmem((2, 2, PAIRS, WIDE), F32),
+            vmem((2, FIELDS, 2 * LEV, WIDE), F32),
             vmem((PAIRS, ROWS, WIDE), F32),
             vmem((PAIRS, 32, WIDE), F32),
             vmem((FIELDS, LEV, ROWS, COLS), F32),
             vmem((FIELDS, LEV, ROWS, COLS), F32),
-            dma((9,)),
-            dma((2,)),
-            dma((2,)),
+            dma((11,)),
+            dma((2, 2)),
+            dma((2, 2)),
             dma((2, 2)),
             dma((2, 2)),
             dma((2,)),
@@ -642,8 +697,8 @@
             dma((2, LANES)),
             dma((2, LANES)),
             dma((2, LANES)),
-            dma((2, 2)),
-            dma((2, 2)),
+            dma((LANES,)),
+            dma((2, FIELDS)),
             dma((2,)),
         ],
         compiler_params=pltpu.CompilerParams(

time: 30.3 us -> 27.3 us (0.901)
  the two profiles are of different devices: /device:TPU:225 before, /device:TPU:1 now
where the time goes in v5:
time: 27.3 us; the launch traced here: 27.2 us
  Pallas kernels  26.6 us (97%)
  between operations  0.64 us (2%)
    pallas_call x1, Pallas kernels, per_device(): pl.pallas_call(functools.partial(kernel, bands), out_shape=(out, out), in...  24.5 us
    pallas_call x1, Pallas kernels, per_device(): pl.pallas_call(hand_out, out_shape=(out, out), in_specs=[any_spec] * 2, o...  2.09 us

profile of v5, /device:TPU:1, one launch (start us, length us, event | category | flops | bytes accessed | tf_op | source)
XLA Modules:
  0.0 27.2 jit_solution(16572602155207964043)
XLA Ops:
  0.6 24.5 %shard_map.122 = (f32[4,4,16,450]{3,2,1,0:T(8,128)}, f32[4,4,16,450]{3,2,1,0:T(8,128)}) custom-call(f32[4,4,16,450]{3,2,1,0:T(8,128)} %spread.1, f32[4,16,450]{2,1,0:T(8,128)} %east.1, f32[4,16,450]{2,1,0:T(8,128)} %north.1, s32[4,4,16]{2,1,0:T(4,128)} %rs.1, s32[4,4,450]{2,1,0:T(4,128)} %cs.1, s32[16]{0:T(128)} %cut.1, ...), custom_call_target="tpu_custom_call" | custom-call | flops 1000000000 | bytes 4000000 | tf_op jit(solution)/shard_map/pallas_call | solution.py:651
  25.1 2.1 %shard_map.123 = (f32[4,4,16,450]{3,2,1,0:T(8,128)}, f32[4,4,16,450]{3,2,1,0:T(8,128)}) custom-call(f32[4,4,16,450]{3,2,1,0:T(8,128)} %get-tuple-element.4.tan_in, f32[4,4,16,450]{3,2,1,0:T(8,128)} %get-tuple-element.5.diag_in), custom_call_target="tpu_custom_call" | custom-call | tf_op jit(solution)/shard_map/pallas_call | solution.py:709

commit v6 on v5

--- a/solution.py
+++ b/solution.py
@@ -114,7 +114,11 @@
     total = bands * ROWS
     rows = np.clip(np.arange(bands)[:, None] * ROWS - 8 + np.arange(32)[None, :], 0, total - 1)
     metric = np.minimum(1.0 / np.cos(np.pi * ((rows + 0.5) / total - 0.5)), metric_cap)
-    return np.broadcast_to((0.5 * metric).astype(np.float32)[:, :, None], (bands, 32, 128)).copy()
+    table = np.broadcast_to((0.5 * metric).astype(np.float32)[:, :, None], (bands, 32, 128)).copy()
+    forward = mode_factors()[0].astype(np.float32)
+    for row, col in enumerate((0, COLS - 1)):
+        table[:, row] = forward[col, :RANK] + forward[col, RANK:]
+    return table
 
 
 def dot_cols(a, b):
@@ -156,10 +160,10 @@
 def kernel(
     bands, spread, east, north, rs, cs, cut, metric, qf_in, qe_in, wf_in, wb_in, tan_out, diag_out,
     spread_v, east_v, north_v, rs_v, cs_v, cut_s, hm, qf, qe, wf, wb,
-    grid, er, hr, hc, cp, hcol, ybuf, yr, zbuf, zr, eb, bz,
+    grid, er, hr, hc, cp, hcol, ybuf, yr, zbuf, zr, xb, cb, yc, eb, bz,
     tend, proj_p, proj_t, edge_t, edge_proj, adj, gy, tan_v, diag_v,
     in_sem, row_send, row_recv, cor_send, cor_recv, col_send, col_recv,
-    y_send, y_recv, z_send, z_recv, b_send, b_recv, out_sem,
+    y_send, y_recv, c_send, c_recv, z_send, z_recv, b_send, b_recv, out_sem,
 ):
     b = lax.axis_index("lat")
     i = lax.axis_index("lon")
@@ -205,6 +209,16 @@
         for load in table_loads:
             load.start()
 
+    def values(q, x):
+        y = to_modes(x.reshape(PAIRS * ROWS, WIDE), qf).reshape(FIELDS, LEV, 2, 8, RANK)
+        for f in range(FIELDS):
+            for h in range(2):
+                for l in range(LEV):
+                    ybuf[q, 2 * f + h, l] = y[f, l, h]
+
+    def probe_values():
+        values(0, grid[0:PAIRS, 8:24, :])
+
     barrier = pltpu.get_barrier_semaphore()
 
     def greet(lat, lon):
@@ -214,26 +228,12 @@
     greet(sb, sl)
     greet(b, west)
     greet(b, east_lane)
-    greet(nb, plus(nl, 1))
-    greet(nb, plus(nl, LANES - 1))
-    greet(sb, plus(sl, 1))
-    greet(sb, plus(sl, LANES - 1))
 
     @pl.when(polar)
     def _():
-        @pl.loop(1, LANES)
+        @pl.loop(2, LANES - 1)
         def _(d):
             greet(b, plus(i, d))
-
-    @pl.when(jnp.logical_and(above_polar, jnp.logical_not(is_north)))
-    def _():
-        for f in range(FIELDS):
-            greet(nb, 2 * f + 1)
-
-    @pl.when(jnp.logical_and(below_polar, jnp.logical_not(is_south)))
-    def _():
-        for f in range(FIELDS):
-            greet(sb, 2 * f)
 
     for load in loads[:5]:
         load.wait()
@@ -263,12 +263,14 @@
 
     own_half = lax.rem(i, 2)
     edge_over = jnp.where(own_half == 0, is_north, is_south)
-    pl.semaphore_wait(
-        barrier,
-        8
-        + jnp.where(polar, LANES - 1, 0)
-        + jnp.where(jnp.logical_and(polar, jnp.logical_not(edge_over)), LANES, 0),
-    )
+
+    @pl.when(polar)
+    def _():
+        for load in table_loads:
+            load.wait()
+        probe_values()
+
+    pl.semaphore_wait(barrier, 4 + jnp.where(polar, LANES - 3, 0))
 
     def remote(src, dst, send, recv, lat, lon):
         return pltpu.make_async_remote_copy(
@@ -285,19 +287,6 @@
         remote(cp.at[0], hcol.at[1], col_send.at[0], col_recv.at[1], b, west),
         remote(cp.at[1], hcol.at[0], col_send.at[1], col_recv.at[0], b, east_lane),
     ]
-    for s, (slot, lat, lon) in enumerate(((slot_n, nb, nl), (slot_s, sb, sl))):
-        halo_sends.append(
-            remote(
-                er.at[s, 0:FIELDS, :, 384:512], hc.at[slot, 0], cor_send.at[s, 0], cor_recv.at[slot, 0],
-                lat, plus(lon, 1),
-            )
-        )
-        halo_sends.append(
-            remote(
-                er.at[s, 0:FIELDS, :, 0:128], hc.at[slot, 1], cor_send.at[s, 1], cor_recv.at[slot, 1],
-                lat, plus(lon, LANES - 1),
-            )
-        )
     halo_sends += [
         remote(er.at[0, FIELDS:10], hr.at[slot_n, FIELDS:10], row_send.at[0, 1], row_recv.at[slot_n, 1], nb, nl),
         remote(er.at[1, FIELDS:10], hr.at[slot_s, FIELDS:10], row_send.at[1, 1], row_recv.at[slot_s, 1], sb, sl),
@@ -305,41 +294,33 @@
     for send in halo_sends:
         send.start()
 
+    corner_sends = [
+        remote(
+            hr.at[s, 0:FIELDS, :, start : start + 128], hc.at[s, side], cor_send.at[s, side], cor_recv.at[s, side],
+            b, lon,
+        )
+        for s in range(2)
+        for side, start, lon in ((0, 384, east_lane), (1, 0, west))
+    ]
+
     def y_copy(q, o):
         return remote(ybuf.at[q, o], yr.at[q, i], y_send.at[q, o], y_recv.at[q, i], b, o)
 
     def y_arrival(q, j):
         return remote(ybuf.at[q, j], yr.at[q, j], y_send.at[q, j], y_recv.at[q, j], b, j)
 
-    def send_probe_values():
-        y = to_modes(grid[0:PAIRS, 8:24, :].reshape(PAIRS * ROWS, WIDE), qf).reshape(FIELDS, LEV, 2, 8, RANK)
-        for f in range(FIELDS):
-            for h in range(2):
-                for l in range(LEV):
-                    ybuf[0, 2 * f + h, l] = y[f, l, h]
-
+    def send_values(q):
         @pl.loop(1, LANES)
         def _(d):
-            y_copy(0, plus(i, d)).start()
-
-        yr[0, i] = ybuf[0, i]
-
-    def send_tendency_values(h):
-        y = to_modes(tend[:, 8 * h : 8 * h + 8, :].reshape(PAIRS * 8, WIDE), qf).reshape(FIELDS, LEV, 8, RANK)
-        for f in range(FIELDS):
-            ybuf[1, 2 * f + h] = y[f]
-
-        @pl.loop(0, FIELDS)
-        def _(d):
-            o = 2 * lax.rem(i // 2 + d, FIELDS) + h
-
-            @pl.when(o != i)
-            def _():
-                y_copy(1, o).start()
-
-            @pl.when(o == i)
-            def _():
-                yr[1, i] = ybuf[1, i]
+            y_copy(q, plus(i, d)).start()
+
+        yr[q, i] = ybuf[q, i]
+
+    def c_copy(o):
+        return remote(cb.at[o], yc.at[i], c_send.at[o], c_recv.at[i], b, o)
+
+    def c_arrival(j):
+        return remote(cb.at[j], yc.at[j], c_send.at[j], c_recv.at[j], b, j)
 
     def z_copy(q, j):
         return remote(zbuf.at[q, j], zr.at[q, i], z_send.at[q, j], z_recv.at[q, i], b, j)
@@ -357,8 +338,30 @@
         def _(d):
             y_arrival(q, plus(i, d)).wait_recv()
 
+        if q == 1:
+            @pl.loop(1, LANES)
+            def _(d):
+                c_arrival(plus(i, d)).wait_recv()
+
+        lanes = []
+        for j in range(LANES):
+            y = yr[q, j]
+            if q == 1:
+                ends = pltpu.roll(yc[j, 8:16, :], lax.rem(128 - 2 * LEV * (i // 2), 128), 1)
+                edge = jnp.where(row == 7 * own_half, 1.0, 0.0)
+                y = jnp.concatenate(
+                    [
+                        y[l]
+                        + ends[:, 2 * l : 2 * l + 1] * hm[0:1, :]
+                        + ends[:, 2 * l + 1 : 2 * l + 2] * hm[1:2, :]
+                        + edge * yc[j, l : l + 1, :]
+                        for l in range(LEV)
+                    ],
+                    axis=0,
+                )
+            lanes.append(y.reshape(LEV * 8, RANK))
         pairs = []
-        over = over_lanes([yr[q, j].reshape(LEV * 8, RANK) for j in range(LANES)])
+        over = over_lanes(lanes)
         for group, pair in enumerate(over):
             coef = to_modes(jnp.concatenate(pair, axis=1), wf.at[group])
             wave = waves_of(group, lax.broadcasted_iota(jnp.int32, (8, 128), 1))
@@ -414,54 +417,6 @@
             [zr[q, 2 * f + h, l] for f in range(FIELDS) for l in range(LEV) for h in range(2)], axis=0
         )
         out[...] = from_modes(z, qe).reshape(PAIRS, ROWS, WIDE)
-
-    for load in loads[5:]:
-        load.wait()
-
-    @pl.when(polar)
-    def _():
-        for load in table_loads:
-            load.wait()
-        send_probe_values()
-
-    for s in range(2):
-        remote(
-            er.at[s, 0:FIELDS], hr.at[s, 0:FIELDS], row_send.at[s, 0], row_recv.at[s, 0], nb, nl
-        ).wait_recv()
-        remote(cp.at[s], hcol.at[s], col_send.at[s], col_recv.at[s], b, west).wait_recv()
-        for side in range(2):
-            remote(
-                er.at[s, 0:FIELDS, :, 0:128], hc.at[s, side], cor_send.at[s, side], cor_recv.at[s, side], nb, nl
-            ).wait_recv()
-
-    from_west = roll(hcol[0], 126, 1)
-    from_east = roll(hcol[1], COLS - 384, 1)
-    lane2 = lax.broadcasted_iota(jnp.int32, (1, 128), 1)
-    both = jnp.where(jnp.logical_and(lane2 >= 66, lane2 < 114), from_east, from_west)[None]
-    for width in (2, 4, 8):
-        both = jnp.concatenate([both, roll_blocks(both, -width)], axis=0)
-    both = jnp.concatenate([both, roll_blocks(both, -16), roll_blocks(both, -32)], axis=0)
-    in_halo = jnp.logical_or(
-        jnp.logical_and(lane128 >= 66, lane128 < 68), lane128 >= 126
-    )
-    grid[:, 8:24, 384:512] = jnp.where(in_halo, both, grid[:, 8:24, 384:512])
-
-    flips = (-1.0, -1.0, 1.0, 1.0)
-    over_pole = (is_north, is_south)
-    edge_row = (7, 24)
-    inward = (1.0, -1.0)
-
-    def edge_center(s, f):
-        tile = hr[s, f][:, 384:512]
-        tile = jnp.where(lane2 == 66, roll(hc[s, 1, f], 66, 1), tile)
-        tile = jnp.where(lane2 == 127, roll(hc[s, 0, f], 62, 1), tile)
-        return jnp.concatenate([hr[s, f][:, 0:384], tile], axis=1)
-
-    edge_probe = [[edge_center(s, f) for f in range(FIELDS)] for s in range(2)]
-    for s in range(2):
-        for f in range(FIELDS):
-            flip = jnp.where(over_pole[s], flips[f], 1.0)
-            grid[f * LEV : (f + 1) * LEV, edge_row[s], :] = flip * edge_probe[s][f]
 
     def tendency_rows(h):
         @pl.loop(0, LEV)
@@ -485,16 +440,107 @@
                     t = t - coupling * linked[f]
                 tend[f * LEV + l, h - 8 : h, :] = t
 
+    for load in loads[5:]:
+        load.wait()
+
+    @pl.when(polar)
+    def _():
+        send_values(0)
+        grid[0:PAIRS, 7:8, :] = jnp.zeros((PAIRS, 1, WIDE), F32)
+        grid[0:PAIRS, 24:25, :] = jnp.zeros((PAIRS, 1, WIDE), F32)
+        for part in range(2):
+            tendency_rows(8 + 8 * part)
+        values(1, tend[...])
+        send_values(1)
+
+    for s in range(2):
+        remote(
+            er.at[s, 0:FIELDS], hr.at[s, 0:FIELDS], row_send.at[s, 0], row_recv.at[s, 0], nb, nl
+        ).wait_recv()
+        remote(cp.at[s], hcol.at[s], col_send.at[s], col_recv.at[s], b, west).wait_recv()
+    for send in corner_sends:
+        send.start()
+
+    flips = (-1.0, -1.0, 1.0, 1.0)
+    over_pole = (is_north, is_south)
+    lane2 = lax.broadcasted_iota(jnp.int32, (1, 128), 1)
+
+    @pl.when(polar)
+    def _():
+        for s, sign in ((0, 1.0), (1, -1.0)):
+            ghosts = [jnp.where(over_pole[s], flips[f], 1.0) * hr[s, f] for f in range(FIELDS)]
+            for f, other in enumerate((None, 2, 1, None)):
+                added = (0.5 * sign) * (er[s, 9] * ghosts[f])
+                if other is not None:
+                    added = added + (0.5 * sign * coupling) * ghosts[other]
+                xb[(s * FIELDS + f) * LEV : (s * FIELDS + f + 1) * LEV, :] = added
+        y = to_modes(xb[...], qf)
+        for s in range(2):
+            for f in range(FIELDS):
+                cb[2 * f + s, 0:LEV, :] = y[(s * FIELDS + f) * LEV : (s * FIELDS + f + 1) * LEV, :]
+        ends = []
+        for side, sign in ((0, -1.0), (1, 1.0)):
+            along_x = (sign * hm[8:24, :]) * (roll(hcol[0], -1, 1) if side == 0 else hcol[1])
+            mine = jnp.where(
+                jnp.logical_and(lane2 >= 2 * PAIRS, lane2 < 2 * (PAIRS + LEV)), cp[side], 0.0
+            )
+            ew = sum(roll(mine, 2 * LEV * f - 2 * PAIRS - side, 1) for f in range(FIELDS))
+            linked = jnp.where(
+                lane2 < 2 * LEV,
+                roll(along_x, -4 * LEV, 1),
+                jnp.where(
+                    jnp.logical_and(lane2 >= 4 * LEV, lane2 < 6 * LEV), roll(along_x, 4 * LEV, 1), 0.0
+                ),
+            )
+            ends.append(-ew * along_x - coupling * linked)
+        ends = jnp.where(lax.rem(lane2, 2) == 0, ends[0], roll(ends[1], 1, 1))
+        for f in range(FIELDS):
+            for h in range(2):
+                cb[2 * f + h, 8:16, :] = ends[8 * h : 8 * h + 8, :]
+
+        @pl.loop(1, LANES)
+        def _(d):
+            c_copy(plus(i, d)).start()
+
+        yc[i] = cb[i]
+
+    @pl.when(polar)
+    def _():
+        own_rows(0)
+
+    from_west = roll(hcol[0], 126, 1)
+    from_east = roll(hcol[1], COLS - 384, 1)
+    both = jnp.where(jnp.logical_and(lane2 >= 66, lane2 < 114), from_east, from_west)[None]
+    for width in (2, 4, 8):
+        both = jnp.concatenate([both, roll_blocks(both, -width)], axis=0)
+    both = jnp.concatenate([both, roll_blocks(both, -16), roll_blocks(both, -32)], axis=0)
+    in_halo = jnp.logical_or(
+        jnp.logical_and(lane128 >= 66, lane128 < 68), lane128 >= 126
+    )
+    grid[:, 8:24, 384:512] = jnp.where(in_halo, both, grid[:, 8:24, 384:512])
+
+    edge_row = (7, 24)
+    inward = (1.0, -1.0)
+
+    def edge_center(s, f):
+        tile = hr[s, f][:, 384:512]
+        tile = jnp.where(lane2 == 66, roll(hc[s, 1, f], 66, 1), tile)
+        tile = jnp.where(lane2 == 127, roll(hc[s, 0, f], 62, 1), tile)
+        return jnp.concatenate([hr[s, f][:, 0:384], tile], axis=1)
+
+    for s in range(2):
+        for side in range(2):
+            remote(
+                hr.at[s, 0:FIELDS, :, 0:128], hc.at[s, side], cor_send.at[s, side], cor_recv.at[s, side], b, west
+            ).wait_recv()
+    edge_probe = [[edge_center(s, f) for f in range(FIELDS)] for s in range(2)]
+    for s in range(2):
+        for f in range(FIELDS):
+            flip = jnp.where(over_pole[s], flips[f], 1.0)
+            grid[f * LEV : (f + 1) * LEV, edge_row[s], :] = flip * edge_probe[s][f]
+
     for part in range(2):
         tendency_rows(8 + 8 * part)
-
-        @pl.when(polar)
-        def _():
-            send_tendency_values(part)
-
-    @pl.when(polar)
-    def _():
-        own_rows(0)
 
     for s in range(2):
         remote(
@@ -606,7 +652,7 @@
     diag_copy = pltpu.make_async_copy(diag_v, diag_out, out_sem.at[1])
     diag_copy.start()
 
-    for send in halo_sends:
+    for send in halo_sends + corner_sends:
         send.wait_send()
 
     @pl.when(polar)
@@ -617,6 +663,7 @@
             for q in range(2):
                 y_copy(q, j).wait_send()
                 z_copy(q, j).wait_send()
+            c_copy(j).wait_send()
 
         edge_sends(end_copy)
 
@@ -675,6 +722,9 @@
             vmem((2, LANES, LEV, 8, RANK), F32),
             vmem((2, LANES, LEV, 8, RANK), F32),
             vmem((2, LANES, LEV, 8, RANK), F32),
+            vmem((2 * PAIRS, WIDE), F32),
+            vmem((LANES, 16, RANK), F32),
+            vmem((LANES, 16, RANK), F32),
             vmem((LANES, 2 * LEV, RANK), F32),
             vmem((2, FIELDS, 2 * LEV, RANK), F32),
             vmem((PAIRS, ROWS, WIDE), F32),
@@ -695,6 +745,8 @@
             dma((2,)),
             dma((2, LANES)),
             dma((2, LANES)),
+            dma((LANES,)),
+            dma((LANES,)),
             dma((2, LANES)),
             dma((2, LANES)),
             dma((LANES,)),

time: 27.3 us -> 26.6 us (0.974)
  the two profiles are of different devices: /device:TPU:1 before, /device:TPU:225 now
where the time goes in v6:
time: 26.6 us; the launch traced here: 26.5 us
  Pallas kernels  25.8 us (97%)
  between operations  0.64 us (2%)
    pallas_call x1, Pallas kernels, per_device(): pl.pallas_call(functools.partial(kernel, bands), out_shape=(out, out), in...  23.7 us
    pallas_call x1, Pallas kernels, per_device(): pl.pallas_call(hand_out, out_shape=(out, out), in_specs=[any_spec] * 2, o...  2.09 us

profile of v6, /device:TPU:225, one launch (start us, length us, event | category | flops | bytes accessed | tf_op | source)
XLA Modules:
  0.0 26.5 jit_solution(7153994365402377936)
XLA Ops:
  0.6 23.7 %shard_map.122 = (f32[4,4,16,450]{3,2,1,0:T(8,128)}, f32[4,4,16,450]{3,2,1,0:T(8,128)}) custom-call(f32[4,4,16,450]{3,2,1,0:T(8,128)} %spread.1, f32[4,16,450]{2,1,0:T(8,128)} %east.1, f32[4,16,450]{2,1,0:T(8,128)} %north.1, s32[4,4,16]{2,1,0:T(4,128)} %rs.1, s32[4,4,450]{2,1,0:T(4,128)} %cs.1, s32[16]{0:T(128)} %cut.1, ...), custom_call_target="tpu_custom_call" | custom-call | flops 1000000000 | bytes 4000000 | tf_op jit(solution)/shard_map/pallas_call | solution.py:698
  24.4 2.1 %shard_map.123 = (f32[4,4,16,450]{3,2,1,0:T(8,128)}, f32[4,4,16,450]{3,2,1,0:T(8,128)}) custom-call(f32[4,4,16,450]{3,2,1,0:T(8,128)} %get-tuple-element.4.tan_in, f32[4,4,16,450]{3,2,1,0:T(8,128)} %get-tuple-element.5.diag_in), custom_call_target="tpu_custom_call" | custom-call | tf_op jit(solution)/shard_map/pallas_call | solution.py:761

commit v7 on v6

--- a/solution.py
+++ b/solution.py
@@ -214,7 +214,7 @@
         for f in range(FIELDS):
             for h in range(2):
                 for l in range(LEV):
-                    ybuf[q, 2 * f + h, l] = y[f, l, h]
+                    ybuf[2 * f + h, q, l] = y[f, l, h]
 
     def probe_values():
         values(0, grid[0:PAIRS, 8:24, :])
@@ -296,37 +296,38 @@
 
     corner_sends = [
         remote(
-            hr.at[s, 0:FIELDS, :, start : start + 128], hc.at[s, side], cor_send.at[s, side], cor_recv.at[s, side],
-            b, lon,
+            hr.at[s, 0:FIELDS, :, start : start + 128], hc.at[s, side], cor_send, cor_recv, b, lon,
         )
         for s in range(2)
         for side, start, lon in ((0, 384, east_lane), (1, 0, west))
     ]
 
-    def y_copy(q, o):
-        return remote(ybuf.at[q, o], yr.at[q, i], y_send.at[q, o], y_recv.at[q, i], b, o)
-
-    def y_arrival(q, j):
-        return remote(ybuf.at[q, j], yr.at[q, j], y_send.at[q, j], y_recv.at[q, j], b, j)
-
-    def send_values(q):
+    def y_copy(o):
+        return remote(ybuf.at[o], yr.at[i], y_send, y_recv, b, o)
+
+    others = pl.ds(0, LANES - 1)
+
+    def all_y():
+        return remote(ybuf.at[others], yr.at[others], y_send, y_recv, b, west)
+
+    def send_values():
         @pl.loop(1, LANES)
         def _(d):
-            y_copy(q, plus(i, d)).start()
-
-        yr[q, i] = ybuf[q, i]
+            y_copy(plus(i, d)).start()
+
+        yr[i] = ybuf[i]
 
     def c_copy(o):
-        return remote(cb.at[o], yc.at[i], c_send.at[o], c_recv.at[i], b, o)
-
-    def c_arrival(j):
-        return remote(cb.at[j], yc.at[j], c_send.at[j], c_recv.at[j], b, j)
+        return remote(cb.at[o], yc.at[i], c_send, c_recv, b, o)
+
+    def all_c():
+        return remote(cb.at[others], yc.at[others], c_send, c_recv, b, west)
 
     def z_copy(q, j):
-        return remote(zbuf.at[q, j], zr.at[q, i], z_send.at[q, j], z_recv.at[q, i], b, j)
-
-    def z_arrival(q, j):
-        return remote(zbuf.at[q, j], zr.at[q, j], z_send.at[q, j], z_recv.at[q, j], b, j)
+        return remote(zbuf.at[q, j], zr.at[q, i], z_send.at[q], z_recv.at[q], b, j)
+
+    def all_z(q):
+        return remote(zbuf.at[q, others], zr.at[q, others], z_send.at[q], z_recv.at[q], b, west)
 
     def own_rows(q):
         row = lax.broadcasted_iota(jnp.int32, (8, 128), 0)
@@ -334,18 +335,14 @@
         for r in range(8):
             cutoff = jnp.where(row == r, cut_s[8 * own_half + r], cutoff)
 
-        @pl.loop(1, LANES)
-        def _(d):
-            y_arrival(q, plus(i, d)).wait_recv()
-
-        if q == 1:
-            @pl.loop(1, LANES)
-            def _(d):
-                c_arrival(plus(i, d)).wait_recv()
+        if q == 0:
+            all_y().wait_recv()
+        else:
+            all_c().wait_recv()
 
         lanes = []
         for j in range(LANES):
-            y = yr[q, j]
+            y = yr[j, q]
             if q == 1:
                 ends = pltpu.roll(yc[j, 8:16, :], lax.rem(128 - 2 * LEV * (i // 2), 128), 1)
                 edge = jnp.where(row == 7 * own_half, 1.0, 0.0)
@@ -379,7 +376,7 @@
 
         zr[q, i] = zbuf[q, i]
 
-    def edge_sends(act):
+    def edge_sends():
         slot = jnp.where(own_half == 0, slot_n, slot_s)
         lat = jnp.where(own_half == 0, nb, sb)
 
@@ -391,28 +388,14 @@
 
             @pl.when(jnp.logical_not(here))
             def _():
-                act(
-                    remote(
-                        eb.at[j], bz.at[slot, i // 2], b_send.at[j], b_recv.at[slot, i // 2], lat, lon
-                    )
-                )
-
-            if act is start_copy:
-                @pl.when(here)
-                def _():
-                    pltpu.make_async_copy(eb.at[j], bz.at[slot, i // 2], b_recv.at[slot, i // 2]).start()
-
-    def start_copy(copy):
-        copy.start()
-
-    def end_copy(copy):
-        copy.wait_send()
+                remote(eb.at[j], bz.at[slot, i // 2], b_send, b_recv.at[slot], lat, lon).start()
+
+            @pl.when(here)
+            def _():
+                pltpu.make_async_copy(eb.at[j], bz.at[slot, i // 2], b_recv.at[slot]).start()
 
     def project(q, out):
-        @pl.loop(1, LANES)
-        def _(d):
-            z_arrival(q, plus(i, d)).wait_recv()
-
+        all_z(q).wait_recv()
         z = jnp.concatenate(
             [zr[q, 2 * f + h, l] for f in range(FIELDS) for l in range(LEV) for h in range(2)], axis=0
         )
@@ -445,13 +428,12 @@
 
     @pl.when(polar)
     def _():
-        send_values(0)
         grid[0:PAIRS, 7:8, :] = jnp.zeros((PAIRS, 1, WIDE), F32)
         grid[0:PAIRS, 24:25, :] = jnp.zeros((PAIRS, 1, WIDE), F32)
         for part in range(2):
             tendency_rows(8 + 8 * part)
         values(1, tend[...])
-        send_values(1)
+        send_values()
 
     for s in range(2):
         remote(
@@ -507,6 +489,8 @@
     @pl.when(polar)
     def _():
         own_rows(0)
+        own_rows(1)
+        edge_sends()
 
     from_west = roll(hcol[0], 126, 1)
     from_east = roll(hcol[1], COLS - 384, 1)
@@ -528,11 +512,7 @@
         tile = jnp.where(lane2 == 127, roll(hc[s, 0, f], 62, 1), tile)
         return jnp.concatenate([hr[s, f][:, 0:384], tile], axis=1)
 
-    for s in range(2):
-        for side in range(2):
-            remote(
-                hr.at[s, 0:FIELDS, :, 0:128], hc.at[s, side], cor_send.at[s, side], cor_recv.at[s, side], b, west
-            ).wait_recv()
+    remote(hc, hc, cor_send, cor_recv, b, west).wait_recv()
     edge_probe = [[edge_center(s, f) for f in range(FIELDS)] for s in range(2)]
     for s in range(2):
         for f in range(FIELDS):
@@ -566,8 +546,6 @@
 
     @pl.when(polar)
     def _():
-        own_rows(1)
-        edge_sends(start_copy)
         project(0, proj_p)
         project(1, proj_t)
 
@@ -606,8 +584,7 @@
     for s, wanted in enumerate((above_polar, below_polar)):
         @pl.when(wanted)
         def _():
-            for f in range(FIELDS):
-                remote(eb.at[f], bz.at[s, f], b_send.at[f], b_recv.at[s, f], nb, nl).wait_recv()
+            remote(bz.at[s], bz.at[s], b_send, b_recv.at[s], nb, nl).wait_recv()
             edge_proj[s] = from_modes(bz[s].reshape(2 * PAIRS, RANK), qe).reshape(FIELDS, 2 * LEV, WIDE)
 
         @pl.when(jnp.logical_not(wanted))
@@ -652,20 +629,24 @@
     diag_copy = pltpu.make_async_copy(diag_v, diag_out, out_sem.at[1])
     diag_copy.start()
 
-    for send in halo_sends + corner_sends:
+    for send in halo_sends:
         send.wait_send()
+    remote(hc, hc, cor_send, cor_recv, b, west).wait_send()
 
     @pl.when(polar)
     def _():
-        @pl.loop(1, LANES)
-        def _(d):
-            j = plus(i, d)
-            for q in range(2):
-                y_copy(q, j).wait_send()
-                z_copy(q, j).wait_send()
-            c_copy(j).wait_send()
-
-        edge_sends(end_copy)
+        all_y().wait_send()
+        all_c().wait_send()
+        for q in range(2):
+            all_z(q).wait_send()
+
+        @pl.when(edge_over)
+        def _():
+            remote(eb.at[others], eb.at[others], b_send, b_recv.at[0], b, west).wait_send()
+
+        @pl.when(jnp.logical_not(edge_over))
+        def _():
+            remote(eb, eb, b_send, b_recv.at[0], b, west).wait_send()
 
     tan_copy.wait()
     diag_copy.wait()
@@ -718,8 +699,8 @@
             vmem((2, 2, FIELDS, LEV, 128), F32),
             vmem((2, ROWS, 128), F32),
             vmem((2, ROWS, 128), F32),
-            vmem((2, LANES, LEV, 8, RANK), F32),
-            vmem((2, LANES, LEV, 8, RANK), F32),
+            vmem((LANES, 2, LEV, 8, RANK), F32),
+            vmem((LANES, 2, LEV, 8, RANK), F32),
             vmem((2, LANES, LEV, 8, RANK), F32),
             vmem((2, LANES, LEV, 8, RANK), F32),
             vmem((2 * PAIRS, WIDE), F32),
@@ -739,18 +720,18 @@
             dma((11,)),
             dma((2, 2)),
             dma((2, 2)),
-            dma((2, 2)),
-            dma((2, 2)),
+            dma,
+            dma,
             dma((2,)),
             dma((2,)),
-            dma((2, LANES)),
-            dma((2, LANES)),
-            dma((LANES,)),
-            dma((LANES,)),
-            dma((2, LANES)),
-            dma((2, LANES)),
-            dma((LANES,)),
-            dma((2, FIELDS)),
+            dma,
+            dma,
+            dma,
+            dma,
+            dma((2,)),
+            dma((2,)),
+            dma,
+            dma((2,)),
             dma((2,)),
         ],
         compiler_params=pltpu.CompilerParams(

time: 26.6 us -> 25.3 us (0.951)
  the two profiles are of different devices: /device:TPU:225 before, /device:TPU:1 now
where the time goes in v7:
time: 25.3 us; the launch traced here: 24.8 us
  Pallas kernels  24.2 us (96%)
  between operations  0.64 us (3%)
    pallas_call x1, Pallas kernels, per_device(): pl.pallas_call(functools.partial(kernel, bands), out_shape=(out, out), in...  22.1 us
    pallas_call x1, Pallas kernels, per_device(): pl.pallas_call(hand_out, out_shape=(out, out), in_specs=[any_spec] * 2, o...  2.09 us

profile of v7, /device:TPU:1, one launch (start us, length us, event | category | flops | bytes accessed | tf_op | source)
XLA Modules:
  0.0 24.8 jit_solution(17600036484350083276)
XLA Ops:
  0.6 22.1 %shard_map.122 = (f32[4,4,16,450]{3,2,1,0:T(8,128)}, f32[4,4,16,450]{3,2,1,0:T(8,128)}) custom-call(f32[4,4,16,450]{3,2,1,0:T(8,128)} %spread.1, f32[4,16,450]{2,1,0:T(8,128)} %east.1, f32[4,16,450]{2,1,0:T(8,128)} %north.1, s32[4,4,16]{2,1,0:T(4,128)} %rs.1, s32[4,4,450]{2,1,0:T(4,128)} %cs.1, s32[16]{0:T(128)} %cut.1, ...), custom_call_target="tpu_custom_call" | custom-call | flops 1000000000 | bytes 4000000 | tf_op jit(solution)/shard_map/pallas_call | solution.py:679
  22.7 2.1 %shard_map.123 = (f32[4,4,16,450]{3,2,1,0:T(8,128)}, f32[4,4,16,450]{3,2,1,0:T(8,128)}) custom-call(f32[4,4,16,450]{3,2,1,0:T(8,128)} %get-tuple-element.4.tan_in, f32[4,4,16,450]{3,2,1,0:T(8,128)} %get-tuple-element.5.diag_in), custom_call_target="tpu_custom_call" | custom-call | tf_op jit(solution)/shard_map/pallas_call | solution.py:742

commit v8 on v7

--- a/solution.py
+++ b/solution.py
@@ -24,6 +24,9 @@
 coupling = 0.5
 mixing = 0.2
 metric_cap = 4.0
+
+EVALUATE, FORWARD, TO_COEFS, FROM_COEFS, TABLE_ROWS = 0, 768, 1280, 2304, 3840
+NEAR, SIDES, REST, BLOCKS = 0, 8, 10, 24
 
 MESH = pl.DeviceIdType.MESH
 F32 = jnp.float32
@@ -75,12 +78,17 @@
     wide_h, wide_l = split_table(wide)
     own = np.where(np.arange(WIDE)[:, None] < COLS, 1, 0).astype(ml_dtypes.bfloat16)
     high, low = split_table(weights)
-    back = [np.swapaxes(part, 1, 2) for part in (high, low, high)]
-    return (
-        np.concatenate([wide_h.T * own, wide_l.T * own], axis=1),
-        np.concatenate([wide_h, wide_l, wide_h], axis=0),
-        np.concatenate([high, low], axis=2),
-        np.concatenate(back, axis=1),
+    back = np.concatenate([np.swapaxes(part, 1, 2) for part in (high, low, high)], axis=1)
+    evaluate = np.concatenate([wide_h, wide_l, wide_h], axis=0)
+    return np.concatenate(
+        [
+            evaluate[:, : WIDE // 2],
+            evaluate[:, WIDE // 2 :],
+            np.concatenate([wide_h.T * own, wide_l.T * own], axis=1),
+            np.concatenate([high, low], axis=2).reshape(-1, 2 * RANK),
+            back.reshape(-1, 2 * RANK),
+        ],
+        axis=0,
     )
 
 
@@ -115,7 +123,7 @@
     rows = np.clip(np.arange(bands)[:, None] * ROWS - 8 + np.arange(32)[None, :], 0, total - 1)
     metric = np.minimum(1.0 / np.cos(np.pi * ((rows + 0.5) / total - 0.5)), metric_cap)
     table = np.broadcast_to((0.5 * metric).astype(np.float32)[:, :, None], (bands, 32, 128)).copy()
-    forward = mode_factors()[0].astype(np.float32)
+    forward = mode_factors()[FORWARD : FORWARD + WIDE].astype(np.float32)
     for row, col in enumerate((0, COLS - 1)):
         table[:, row] = forward[col, :RANK] + forward[col, RANK:]
     return table
@@ -137,9 +145,10 @@
     return wide[:, :half] + wide[:, half:] + dot_cols(xl, table[:, 0:half])
 
 
-def from_modes(z, table):
+def from_modes(z, *tables):
     zh, zl = split(z)
-    return dot_cols(jnp.concatenate([zh, zh, zl], axis=1), table[...])
+    three = jnp.concatenate([zh, zh, zl], axis=1)
+    return jnp.concatenate([dot_cols(three, table[...]) for table in tables], axis=1)
 
 
 def roll(x, shift, axis):
@@ -158,12 +167,11 @@
 
 
 def kernel(
-    bands, spread, east, north, rs, cs, cut, metric, qf_in, qe_in, wf_in, wb_in, tan_out, diag_out,
-    spread_v, east_v, north_v, rs_v, cs_v, cut_s, hm, qf, qe, wf, wb,
-    grid, er, hr, hc, cp, hcol, ybuf, yr, zbuf, zr, xb, cb, yc, eb, bz,
+    bands, spread, east, north, rs, cs, cut, metric, table_in, tan_out, diag_out,
+    spread_v, winds_v, rs_v, cs_v, cut_s, hm, table,
+    grid, halo_out, halo_in, ybuf, yr, cb, yc, zbuf, zr, eb, bz,
     tend, proj_p, proj_t, edge_t, edge_proj, adj, gy, tan_v, diag_v,
-    in_sem, row_send, row_recv, cor_send, cor_recv, col_send, col_recv,
-    y_send, y_recv, c_send, c_recv, z_send, z_recv, b_send, b_recv, out_sem,
+    in_sem, halo_send, halo_recv, y_send, y_recv, c_send, c_recv, z_send, z_recv, b_send, b_recv, out_sem,
 ):
     b = lax.axis_index("lat")
     i = lax.axis_index("lon")
@@ -173,6 +181,7 @@
     polar = jnp.logical_or(b < caps, b >= bands - caps)
     above_polar = jnp.logical_or(b <= caps, is_south)
     below_polar = jnp.logical_or(b >= bands - caps - 1, is_north)
+    near_polar = jnp.logical_or(above_polar, below_polar)
     across = lax.rem(i + LANES // 2, LANES)
     west = lax.rem(i + LANES - 1, LANES)
     east_lane = lax.rem(i + 1, LANES)
@@ -182,42 +191,28 @@
     sl = jnp.where(is_south, across, i)
     slot_n = jnp.where(is_north, 0, 1)
     slot_s = jnp.where(is_south, 1, 0)
+    own_half = lax.rem(i, 2)
+    edge_over = jnp.where(own_half == 0, is_north, is_south)
+    over_pole = (is_north, is_south)
 
     def plus(lane, d):
         return lax.rem(lane + d, LANES)
 
-    loads = [
-        pltpu.make_async_copy(spread, spread_v, in_sem.at[0]),
-        pltpu.make_async_copy(rs, rs_v, in_sem.at[1]),
-        pltpu.make_async_copy(cs, cs_v, in_sem.at[2]),
-        pltpu.make_async_copy(east, east_v, in_sem.at[3]),
-        pltpu.make_async_copy(north, north_v, in_sem.at[4]),
-        pltpu.make_async_copy(metric.at[b], hm, in_sem.at[5]),
-        pltpu.make_async_copy(cut, cut_s, in_sem.at[6]),
-        pltpu.make_async_copy(qe_in, qe, in_sem.at[7]),
-    ]
-    table_loads = [
-        pltpu.make_async_copy(qf_in, qf, in_sem.at[8]),
-        pltpu.make_async_copy(wf_in, wf, in_sem.at[9]),
-        pltpu.make_async_copy(wb_in, wb, in_sem.at[10]),
-    ]
-    for load in loads:
-        load.start()
-
-    @pl.when(polar)
-    def _():
-        for load in table_loads:
-            load.start()
-
-    def values(q, x):
-        y = to_modes(x.reshape(PAIRS * ROWS, WIDE), qf).reshape(FIELDS, LEV, 2, 8, RANK)
-        for f in range(FIELDS):
-            for h in range(2):
-                for l in range(LEV):
-                    ybuf[2 * f + h, q, l] = y[f, l, h]
-
-    def probe_values():
-        values(0, grid[0:PAIRS, 8:24, :])
+    load_spread = pltpu.make_async_copy(spread, spread_v, in_sem.at[0])
+    load_rows = pltpu.make_async_copy(rs, rs_v, in_sem.at[1])
+    load_cols = pltpu.make_async_copy(cs, cs_v, in_sem.at[2])
+    load_metric = pltpu.make_async_copy(metric.at[b], hm, in_sem.at[4])
+    load_cut = pltpu.make_async_copy(cut, cut_s, in_sem.at[5])
+    load_table = pltpu.make_async_copy(table_in, table, in_sem.at[6])
+    load_part = pltpu.make_async_copy(
+        table_in.at[EVALUATE:FORWARD], table.at[EVALUATE:FORWARD], in_sem.at[6]
+    )
+    load_spread.start()
+    load_rows.start()
+    load_cols.start()
+    pltpu.make_async_copy(east, winds_v.at[0], in_sem.at[3]).start()
+    pltpu.make_async_copy(north, winds_v.at[1], in_sem.at[3]).start()
+    load_metric.start()
 
     barrier = pltpu.get_barrier_semaphore()
 
@@ -235,8 +230,16 @@
         def _(d):
             greet(b, plus(i, d))
 
-    for load in loads[:5]:
-        load.wait()
+        load_table.start()
+        load_cut.start()
+
+    @pl.when(jnp.logical_and(near_polar, jnp.logical_not(polar)))
+    def _():
+        load_part.start()
+
+    load_rows.wait()
+    load_cols.wait()
+    load_spread.wait()
     grid[:, 8:24, 384:512] = jnp.zeros((PAIRS + 2 * LEV, ROWS, 128), F32)
     row_part = jnp.concatenate([rs_v[f] for f in range(FIELDS)], axis=0)
     row_part = (2 * row_part - 1).astype(F32).T
@@ -245,30 +248,38 @@
         for l in range(LEV):
             n = f * LEV + l
             grid[n, 8:24, 0:COLS] = spread_v[f, l] * (row_part[:, n : n + 1] * col_part[l : l + 1, :])
-    for l in range(LEV):
-        grid[PAIRS + l, 8:24, 0:COLS] = east_v[l]
-        grid[PAIRS + LEV + l, 8:24, 0:COLS] = north_v[l]
+    pltpu.make_async_copy(winds_v, winds_v, in_sem.at[3]).wait()
+    for w in range(2):
+        for l in range(LEV):
+            grid[PAIRS + w * LEV + l, 8:24, 0:COLS] = winds_v[w, l]
 
     for s, (near, far) in enumerate(((8, 9), (23, 22))):
-        for f in range(FIELDS + 2):
-            er[s, f if f < FIELDS else f + FIELDS] = grid[f * LEV : (f + 1) * LEV, near, :]
-        for f in range(FIELDS):
-            er[s, FIELDS + f] = grid[f * LEV : (f + 1) * LEV, far, :]
+        for t in range(4):
+            lanes = slice(128 * t, 128 * t + 128)
+            halo_out[NEAR + 4 * s + t] = grid[0:PAIRS, near, lanes]
+            halo_out[REST + 7 * s + t] = grid[0:PAIRS, far, lanes]
+            halo_out[REST + 7 * s + 4 + t // 2, 8 * (t % 2) : 8 * (t % 2) + 8, :] = grid[
+                PAIRS : PAIRS + 2 * LEV, near, lanes
+            ]
     lane128 = lax.broadcasted_iota(jnp.int32, (1, 1, 128), 2)
     for s, (start, shift) in enumerate(((0, 0), (384, COLS - 2 - 384))):
         tile = grid[:, 8:24, start : start + 128]
         tile = jnp.where(jnp.logical_and(lane128 >= shift, lane128 < shift + 2), tile, 0.0)
         packed = fold(tile[:PAIRS]) + roll_blocks(fold(tile[PAIRS:]), 2 * PAIRS)
-        cp[s] = roll_blocks(packed, -shift)[0]
-
-    own_half = lax.rem(i, 2)
-    edge_over = jnp.where(own_half == 0, is_north, is_south)
+        halo_out[SIDES + s] = roll_blocks(packed, -shift)[0]
+
+    def values(q, x):
+        y = to_modes(x.reshape(PAIRS * ROWS, WIDE), table.at[FORWARD:TO_COEFS])
+        y = y.reshape(FIELDS, LEV, 2, 8, RANK)
+        for f in range(FIELDS):
+            for h in range(2):
+                for l in range(LEV):
+                    ybuf[2 * f + h, q, l] = y[f, l, h]
 
     @pl.when(polar)
     def _():
-        for load in table_loads:
-            load.wait()
-        probe_values()
+        load_table.wait()
+        values(0, grid[0:PAIRS, 8:24, :])
 
     pl.semaphore_wait(barrier, 4 + jnp.where(polar, LANES - 3, 0))
 
@@ -277,30 +288,20 @@
             src_ref=src, dst_ref=dst, send_sem=send, recv_sem=recv, device_id=(lat, lon), device_id_type=MESH
         )
 
-    halo_sends = [
-        remote(
-            er.at[0, 0:FIELDS], hr.at[slot_n, 0:FIELDS], row_send.at[0, 0], row_recv.at[slot_n, 0], nb, nl
-        ),
-        remote(
-            er.at[1, 0:FIELDS], hr.at[slot_s, 0:FIELDS], row_send.at[1, 0], row_recv.at[slot_s, 0], sb, sl
-        ),
-        remote(cp.at[0], hcol.at[1], col_send.at[0], col_recv.at[1], b, west),
-        remote(cp.at[1], hcol.at[0], col_send.at[1], col_recv.at[0], b, east_lane),
-    ]
-    halo_sends += [
-        remote(er.at[0, FIELDS:10], hr.at[slot_n, FIELDS:10], row_send.at[0, 1], row_recv.at[slot_n, 1], nb, nl),
-        remote(er.at[1, FIELDS:10], hr.at[slot_s, FIELDS:10], row_send.at[1, 1], row_recv.at[slot_s, 1], sb, sl),
-    ]
-    for send in halo_sends:
-        send.start()
-
-    corner_sends = [
-        remote(
-            hr.at[s, 0:FIELDS, :, start : start + 128], hc.at[s, side], cor_send, cor_recv, b, lon,
+    def halo_copy(start, count, to, which, lat, lon):
+        return remote(
+            halo_out.at[start : start + count], halo_in.at[pl.ds(to, count)], halo_send, halo_recv.at[which], lat, lon
         )
-        for s in range(2)
-        for side, start, lon in ((0, 384, east_lane), (1, 0, west))
-    ]
+
+    def halo_arrival(start, stop, which):
+        return remote(
+            halo_out.at[start:stop], halo_in.at[start:stop], halo_send, halo_recv.at[which], b, west
+        )
+
+    halo_copy(NEAR, 4, NEAR + 4 * slot_n, 0, nb, nl).start()
+    halo_copy(NEAR + 4, 4, NEAR + 4 * slot_s, 0, sb, sl).start()
+    halo_copy(SIDES, 1, SIDES + 1, 0, b, west).start()
+    halo_copy(SIDES + 1, 1, SIDES, 0, b, east_lane).start()
 
     def y_copy(o):
         return remote(ybuf.at[o], yr.at[i], y_send, y_recv, b, o)
@@ -360,10 +361,15 @@
         pairs = []
         over = over_lanes(lanes)
         for group, pair in enumerate(over):
-            coef = to_modes(jnp.concatenate(pair, axis=1), wf.at[group])
+            coef = to_modes(
+                jnp.concatenate(pair, axis=1), table.at[TO_COEFS + 256 * group : TO_COEFS + 256 * (group + 1)]
+            )
             wave = waves_of(group, lax.broadcasted_iota(jnp.int32, (8, 128), 1))
             keep = jnp.where(wave > cutoff, 2.0 / (COLS * LANES), 0.0)
-            back = from_modes(coef * jnp.concatenate([keep] * LEV, axis=0), wb.at[group])
+            back = from_modes(
+                coef * jnp.concatenate([keep] * LEV, axis=0),
+                table.at[FROM_COEFS + 384 * group : FROM_COEFS + 384 * (group + 1)],
+            )
             pairs.append((back[:, :RANK], back[:, RANK:]))
         for j, z in enumerate(to_lanes(pairs)):
             z = z.reshape(LEV, 8, RANK)
@@ -394,12 +400,15 @@
             def _():
                 pltpu.make_async_copy(eb.at[j], bz.at[slot, i // 2], b_recv.at[slot]).start()
 
+    def evaluate(z):
+        return from_modes(z, table.at[0:384], table.at[384:768])
+
     def project(q, out):
         all_z(q).wait_recv()
         z = jnp.concatenate(
             [zr[q, 2 * f + h, l] for f in range(FIELDS) for l in range(LEV) for h in range(2)], axis=0
         )
-        out[...] = from_modes(z, qe).reshape(PAIRS, ROWS, WIDE)
+        out[...] = evaluate(z).reshape(PAIRS, ROWS, WIDE)
 
     def tendency_rows(h):
         @pl.loop(0, LEV)
@@ -423,8 +432,7 @@
                     t = t - coupling * linked[f]
                 tend[f * LEV + l, h - 8 : h, :] = t
 
-    for load in loads[5:]:
-        load.wait()
+    load_metric.wait()
 
     @pl.when(polar)
     def _():
@@ -435,36 +443,43 @@
         values(1, tend[...])
         send_values()
 
-    for s in range(2):
-        remote(
-            er.at[s, 0:FIELDS], hr.at[s, 0:FIELDS], row_send.at[s, 0], row_recv.at[s, 0], nb, nl
-        ).wait_recv()
-        remote(cp.at[s], hcol.at[s], col_send.at[s], col_recv.at[s], b, west).wait_recv()
-    for send in corner_sends:
-        send.start()
-
-    flips = (-1.0, -1.0, 1.0, 1.0)
-    over_pole = (is_north, is_south)
+    halo_arrival(NEAR, REST, 0).wait_recv()
     lane2 = lax.broadcasted_iota(jnp.int32, (1, 128), 1)
+    row16 = lax.broadcasted_iota(jnp.int32, (PAIRS, 1), 0)
+    is_v = jnp.logical_and(row16 >= LEV, row16 < 2 * LEV)
+    is_temp = jnp.logical_and(row16 >= 2 * LEV, row16 < 3 * LEV)
+
+    def flip(s, minus):
+        sign = jnp.where(row16 < 2 * LEV, -1.0, 1.0) * minus
+        return jnp.where(over_pole[s], sign, 1.0)
+
+    def row_link(x):
+        return jnp.where(is_v, roll(x, -LEV, 0), jnp.where(is_temp, roll(x, LEV, 0), 0.0))
+
+    def wind(buffer, s, w):
+        base = REST + 7 * s + 4
+        rows = [buffer[base + t // 2, 8 * (t % 2) + LEV * w : 8 * (t % 2) + LEV * (w + 1), :] for t in range(4)]
+        return jnp.concatenate([jnp.concatenate(rows, axis=1)] * FIELDS, axis=0)
+
+    def row_of(buffer, start):
+        return jnp.concatenate([buffer[start + t] for t in range(4)], axis=1)
 
     @pl.when(polar)
     def _():
-        for s, sign in ((0, 1.0), (1, -1.0)):
-            ghosts = [jnp.where(over_pole[s], flips[f], 1.0) * hr[s, f] for f in range(FIELDS)]
-            for f, other in enumerate((None, 2, 1, None)):
-                added = (0.5 * sign) * (er[s, 9] * ghosts[f])
-                if other is not None:
-                    added = added + (0.5 * sign * coupling) * ghosts[other]
-                xb[(s * FIELDS + f) * LEV : (s * FIELDS + f + 1) * LEV, :] = added
-        y = to_modes(xb[...], qf)
+        added = []
+        for s, sign in ((0, 0.5), (1, -0.5)):
+            ghost = flip(s, 1.0) * row_of(halo_in, NEAR + 4 * s)
+            added.append(sign * (wind(halo_out, s, 1) * ghost + coupling * row_link(ghost)))
+        y = to_modes(jnp.concatenate(added, axis=0), table.at[FORWARD:TO_COEFS])
         for s in range(2):
             for f in range(FIELDS):
                 cb[2 * f + s, 0:LEV, :] = y[(s * FIELDS + f) * LEV : (s * FIELDS + f + 1) * LEV, :]
         ends = []
         for side, sign in ((0, -1.0), (1, 1.0)):
-            along_x = (sign * hm[8:24, :]) * (roll(hcol[0], -1, 1) if side == 0 else hcol[1])
+            came = halo_in[SIDES + side]
+            along_x = (sign * hm[8:24, :]) * (roll(came, -1, 1) if side == 0 else came)
             mine = jnp.where(
-                jnp.logical_and(lane2 >= 2 * PAIRS, lane2 < 2 * (PAIRS + LEV)), cp[side], 0.0
+                jnp.logical_and(lane2 >= 2 * PAIRS, lane2 < 2 * (PAIRS + LEV)), halo_out[SIDES + side], 0.0
             )
             ew = sum(roll(mine, 2 * LEV * f - 2 * PAIRS - side, 1) for f in range(FIELDS))
             linked = jnp.where(
@@ -486,63 +501,50 @@
 
         yc[i] = cb[i]
 
-    @pl.when(polar)
-    def _():
-        own_rows(0)
-        own_rows(1)
-        edge_sends()
-
-    from_west = roll(hcol[0], 126, 1)
-    from_east = roll(hcol[1], COLS - 384, 1)
+    from_west = roll(halo_in[SIDES], 126, 1)
+    from_east = roll(halo_in[SIDES + 1], COLS - 384, 1)
     both = jnp.where(jnp.logical_and(lane2 >= 66, lane2 < 114), from_east, from_west)[None]
     for width in (2, 4, 8):
         both = jnp.concatenate([both, roll_blocks(both, -width)], axis=0)
     both = jnp.concatenate([both, roll_blocks(both, -16), roll_blocks(both, -32)], axis=0)
-    in_halo = jnp.logical_or(
-        jnp.logical_and(lane128 >= 66, lane128 < 68), lane128 >= 126
-    )
+    in_halo = jnp.logical_or(jnp.logical_and(lane128 >= 66, lane128 < 68), lane128 >= 126)
     grid[:, 8:24, 384:512] = jnp.where(in_halo, both, grid[:, 8:24, 384:512])
-
+    for s, near in enumerate((8, 23)):
+        halo_out[REST + 7 * s + 6] = grid[0:PAIRS, near, 384:512]
+    halo_copy(REST, 7, REST + 7 * slot_n, 1, nb, nl).start()
+    halo_copy(REST + 7, 7, REST + 7 * slot_s, 1, sb, sl).start()
+
+    @pl.when(polar)
+    def _():
+        load_cut.wait()
+        own_rows(0)
+        own_rows(1)
+        edge_sends()
+
+    halo_arrival(REST, BLOCKS, 1).wait_recv()
     edge_row = (7, 24)
-    inward = (1.0, -1.0)
-
-    def edge_center(s, f):
-        tile = hr[s, f][:, 384:512]
-        tile = jnp.where(lane2 == 66, roll(hc[s, 1, f], 66, 1), tile)
-        tile = jnp.where(lane2 == 127, roll(hc[s, 0, f], 62, 1), tile)
-        return jnp.concatenate([hr[s, f][:, 0:384], tile], axis=1)
-
-    remote(hc, hc, cor_send, cor_recv, b, west).wait_recv()
-    edge_probe = [[edge_center(s, f) for f in range(FIELDS)] for s in range(2)]
+    edge_probe = []
     for s in range(2):
-        for f in range(FIELDS):
-            flip = jnp.where(over_pole[s], flips[f], 1.0)
-            grid[f * LEV : (f + 1) * LEV, edge_row[s], :] = flip * edge_probe[s][f]
+        edge_probe.append(
+            jnp.concatenate([halo_in[NEAR + 4 * s + t] for t in range(3)] + [halo_in[REST + 7 * s + 6]], axis=1)
+        )
+        grid[0:PAIRS, edge_row[s], :] = flip(s, 1.0) * edge_probe[s]
 
     for part in range(2):
         tendency_rows(8 + 8 * part)
 
-    for s in range(2):
-        remote(
-            er.at[s, FIELDS:10], hr.at[s, FIELDS:10], row_send.at[s, 1], row_recv.at[s, 1], nb, nl
-        ).wait_recv()
-        centers = edge_probe[s]
+    for s, inward in ((0, 1.0), (1, -1.0)):
+        mid = edge_probe[s]
         half = jnp.concatenate([hm[edge_row[s] : edge_row[s] + 1, :]] * 4, axis=1)
-        turn = jnp.where(over_pole[s], -inward[s], inward[s])
-        along_x, along_y = [], []
-        for f in range(FIELDS):
-            flip = jnp.where(over_pole[s], flips[f], 1.0)
-            along_x.append(half * (roll(centers[f], -1, 1) - roll(centers[f], 1, 1)))
-            along_y.append((0.5 * turn) * (flip * er[s, f] - hr[s, FIELDS + f]))
-        linked = (along_x[2], along_y[2], along_x[0] + along_y[1], None)
-        for f in range(FIELDS):
-            mid = centers[f]
-            up = jnp.concatenate([mid[0:1], mid[0:3]], axis=0)
-            down = jnp.concatenate([mid[1:4], mid[3:4]], axis=0)
-            t = -(hr[s, 8] * along_x[f] + hr[s, 9] * along_y[f]) + mixing * (up + down - 2.0 * mid)
-            if linked[f] is not None:
-                t = t - coupling * linked[f]
-            edge_t[s, f] = t
+        along_x = half * (roll(mid, -1, 1) - roll(mid, 1, 1))
+        turn = jnp.where(over_pole[s], -0.5 * inward, 0.5 * inward)
+        along_y = turn * (flip(s, 1.0) * row_of(halo_out, NEAR + 4 * s) - row_of(halo_in, REST + 7 * s))
+        linked = jnp.where(row16 < LEV, roll(along_x, -2 * LEV, 0), row_link(along_y))
+        linked = linked + jnp.where(is_temp, roll(along_x, 2 * LEV, 0), 0.0)
+        up = jnp.where(lax.rem(row16, LEV) == 0, mid, roll(mid, 1, 0))
+        down = jnp.where(lax.rem(row16, LEV) == LEV - 1, mid, roll(mid, -1, 0))
+        t = -(wind(halo_in, s, 0) * along_x + wind(halo_in, s, 1) * along_y) - coupling * linked
+        edge_t[s] = t + mixing * (up + down - 2.0 * mid)
 
     @pl.when(polar)
     def _():
@@ -585,23 +587,35 @@
         @pl.when(wanted)
         def _():
             remote(bz.at[s], bz.at[s], b_send, b_recv.at[s], nb, nl).wait_recv()
-            edge_proj[s] = from_modes(bz[s].reshape(2 * PAIRS, RANK), qe).reshape(FIELDS, 2 * LEV, WIDE)
 
         @pl.when(jnp.logical_not(wanted))
         def _():
-            edge_proj[s] = jnp.zeros((FIELDS, 2 * LEV, WIDE), F32)
+            bz[s] = jnp.zeros((FIELDS, 2 * LEV, RANK), F32)
+
+    @pl.when(jnp.logical_and(near_polar, jnp.logical_not(polar)))
+    def _():
+        load_part.wait()
+
+    @pl.when(near_polar)
+    def _():
+        parts = [
+            bz[s, f, LEV * q : LEV * (q + 1), :] for s in range(2) for q in range(2) for f in range(FIELDS)
+        ]
+        edge_proj[...] = evaluate(jnp.concatenate(parts, axis=0))
+
+    @pl.when(jnp.logical_not(near_polar))
+    def _():
+        edge_proj[...] = jnp.zeros(edge_proj.shape, F32)
 
     for s in range(2):
-        a = []
-        for f in range(FIELDS):
-            a.append(
-                edge_probe[s][f]
-                + time_step * (edge_t[s, f] - edge_proj[s, f, LEV : 2 * LEV, :])
-                - edge_proj[s, f, 0:LEV, :]
-            )
-        for f, weight in enumerate(row_weights(a, hr[s, 9])):
-            flip = jnp.where(over_pole[s], -flips[f], 1.0)
-            gy[f * LEV : (f + 1) * LEV, edge_row[s], :] = flip * weight
+        base = 2 * PAIRS * s
+        a = (
+            edge_probe[s]
+            + time_step * (edge_t[s] - edge_proj[base + PAIRS : base + 2 * PAIRS, :])
+            - edge_proj[base : base + PAIRS, :]
+        )
+        weight = -wind(halo_in, s, 1) * a - coupling * row_link(a)
+        gy[0:PAIRS, edge_row[s], :] = flip(s, -1.0) * weight
 
     @pl.loop(0, LEV)
     def _(l):
@@ -629,9 +643,7 @@
     diag_copy = pltpu.make_async_copy(diag_v, diag_out, out_sem.at[1])
     diag_copy.start()
 
-    for send in halo_sends:
-        send.wait_send()
-    remote(hc, hc, cor_send, cor_recv, b, west).wait_send()
+    halo_arrival(0, BLOCKS, 0).wait_send()
 
     @pl.when(polar)
     def _():
@@ -653,76 +665,58 @@
 
 
 def hand_out(tan_in, diag_in, tan_out, diag_out, held, in_sem, out_sem):
-    ways = [
-        (
-            pltpu.make_async_copy(src.at[f], held.at[n, f], in_sem.at[n, f]),
-            pltpu.make_async_copy(held.at[n, f], dst.at[f], out_sem.at[n, f]),
-        )
-        for n, (src, dst) in enumerate(((tan_in, tan_out), (diag_in, diag_out)))
-        for f in range(FIELDS)
-    ]
-    for arrive, leave in ways:
-        arrive.start()
-    for arrive, leave in ways:
-        arrive.wait()
-        leave.start()
-    for arrive, leave in ways:
-        leave.wait()
+    arrive = [pltpu.make_async_copy(src, held.at[n], in_sem.at[n]) for n, src in enumerate((tan_in, diag_in))]
+    leave = [pltpu.make_async_copy(held.at[n], dst, out_sem.at[n]) for n, dst in enumerate((tan_out, diag_out))]
+    for copy in arrive:
+        copy.start()
+    for copy, onward in zip(arrive, leave):
+        copy.wait()
+        onward.start()
+    for onward in leave:
+        onward.wait()
 
 
 def per_device(bands, row_signs, col_signs, spread, east_wind, north_wind, cutoffs):
     any_spec = pl.BlockSpec(memory_space=pl.ANY)
     out = jax.ShapeDtypeStruct((FIELDS, LEV, ROWS, COLS), F32)
-    tables = [jnp.asarray(table) for table in (half_metric(bands),) + mode_factors()]
+    tables = [jnp.asarray(half_metric(bands)), jnp.asarray(mode_factors())]
     vmem = pltpu.VMEM
     dma = pltpu.SemaphoreType.DMA
     results = pl.pallas_call(
         functools.partial(kernel, bands),
         out_shape=(out, out),
-        in_specs=[any_spec] * 11,
+        in_specs=[any_spec] * 8,
         out_specs=(any_spec, any_spec),
         scratch_shapes=[
             vmem((FIELDS, LEV, ROWS, COLS), F32),
-            vmem((LEV, ROWS, COLS), F32),
-            vmem((LEV, ROWS, COLS), F32),
+            vmem((2, LEV, ROWS, COLS), F32),
             vmem((FIELDS, LEV, ROWS), jnp.int32),
             vmem((FIELDS, LEV, COLS), jnp.int32),
             pltpu.SMEM((ROWS,), jnp.int32),
             vmem((32, 128), F32),
-            vmem((WIDE, 2 * RANK), BF16),
-            vmem((3 * RANK, WIDE), BF16),
-            vmem((4, 2 * RANK, 4 * 64), BF16),
-            vmem((4, 6 * 64, 2 * RANK), BF16),
+            vmem((TABLE_ROWS, 2 * RANK), BF16),
             vmem((PAIRS + 2 * LEV, 32, WIDE), F32),
-            vmem((2, 10, LEV, WIDE), F32),
-            vmem((2, 10, LEV, WIDE), F32),
-            vmem((2, 2, FIELDS, LEV, 128), F32),
-            vmem((2, ROWS, 128), F32),
-            vmem((2, ROWS, 128), F32),
+            vmem((BLOCKS, 16, 128), F32),
+            vmem((BLOCKS, 16, 128), F32),
             vmem((LANES, 2, LEV, 8, RANK), F32),
             vmem((LANES, 2, LEV, 8, RANK), F32),
+            vmem((LANES, 16, RANK), F32),
+            vmem((LANES, 16, RANK), F32),
             vmem((2, LANES, LEV, 8, RANK), F32),
             vmem((2, LANES, LEV, 8, RANK), F32),
-            vmem((2 * PAIRS, WIDE), F32),
-            vmem((LANES, 16, RANK), F32),
-            vmem((LANES, 16, RANK), F32),
             vmem((LANES, 2 * LEV, RANK), F32),
             vmem((2, FIELDS, 2 * LEV, RANK), F32),
             vmem((PAIRS, ROWS, WIDE), F32),
             vmem((PAIRS, ROWS, WIDE), F32),
             vmem((PAIRS, ROWS, WIDE), F32),
-            vmem((2, FIELDS, LEV, WIDE), F32),
-            vmem((2, FIELDS, 2 * LEV, WIDE), F32),
+            vmem((2, PAIRS, WIDE), F32),
+            vmem((4 * PAIRS, WIDE), F32),
             vmem((PAIRS, ROWS, WIDE), F32),
             vmem((PAIRS, 32, WIDE), F32),
             vmem((FIELDS, LEV, ROWS, COLS), F32),
             vmem((FIELDS, LEV, ROWS, COLS), F32),
-            dma((11,)),
-            dma((2, 2)),
-            dma((2, 2)),
+            dma((7,)),
             dma,
-            dma,
-            dma((2,)),
             dma((2,)),
             dma,
             dma,
@@ -744,7 +738,7 @@
         out_shape=(out, out),
         in_specs=[any_spec] * 2,
         out_specs=(any_spec, any_spec),
-        scratch_shapes=[vmem((2, FIELDS, LEV, ROWS, COLS), F32), dma((2, FIELDS)), dma((2, FIELDS))],
+        scratch_shapes=[vmem((2, FIELDS, LEV, ROWS, COLS), F32), dma((2,)), dma((2,))],
         compiler_params=pltpu.CompilerParams(vmem_limit_bytes=64 * 2**20),
     )(*results)
 

time: 25.3 us -> 24.7 us (0.976)
  the two profiles are of different devices: /device:TPU:1 before, /device:TPU:225 now
where the time goes in v8:
time: 24.7 us; the launch traced here: 24.5 us
  Pallas kernels  23.9 us (97%)
  between operations  0.64 us (3%)
    pallas_call x1, Pallas kernels, per_device(): pl.pallas_call(functools.partial(kernel, bands), out_shape=(out, out), in...  21.8 us
    pallas_call x1, Pallas kernels, per_device(): pl.pallas_call(hand_out, out_shape=(out, out), in_specs=[any_spec] * 2, o...  2.04 us

profile of v8, /device:TPU:225, one launch (start us, length us, event | category | flops | bytes accessed | tf_op | source)
XLA Modules:
  0.0 24.5 jit_solution(11538693623785151173)
XLA Ops:
  0.6 21.8 %shard_map.95 = (f32[4,4,16,450]{3,2,1,0:T(8,128)}, f32[4,4,16,450]{3,2,1,0:T(8,128)}) custom-call(f32[4,4,16,450]{3,2,1,0:T(8,128)} %spread.1, f32[4,16,450]{2,1,0:T(8,128)} %east.1, f32[4,16,450]{2,1,0:T(8,128)} %north.1, s32[4,4,16]{2,1,0:T(4,128)} %rs.1, s32[4,4,450]{2,1,0:T(4,128)} %cs.1, s32[16]{0:T(128)} %cut.1, f32[32,32,128]{2,1,0:T(8,128)} %constant.4.clone.metric, ...), custom_call_target="tpu_custom_call" | custom-call | flops 1000000000 | bytes 4000000 | tf_op jit(solution)/shard_map/pallas_call | solution.py:685
  22.5 2.0 %shard_map.96 = (f32[4,4,16,450]{3,2,1,0:T(8,128)}, f32[4,4,16,450]{3,2,1,0:T(8,128)}) custom-call(f32[4,4,16,450]{3,2,1,0:T(8,128)} %get-tuple-element.4.tan_in, f32[4,4,16,450]{3,2,1,0:T(8,128)} %get-tuple-element.5.diag_in), custom_call_target="tpu_custom_call" | custom-call | tf_op jit(solution)/shard_map/pallas_call | solution.py:736

commit v9 on v8

--- a/solution.py
+++ b/solution.py
@@ -25,7 +25,7 @@
 mixing = 0.2
 metric_cap = 4.0
 
-EVALUATE, FORWARD, TO_COEFS, FROM_COEFS, TABLE_ROWS = 0, 768, 1280, 2304, 3840
+FORWARD, EVALUATE, TO_COEFS, FROM_COEFS, TABLE_ROWS = 0, 512, 1280, 2304, 3840
 NEAR, SIDES, REST, BLOCKS = 0, 8, 10, 24
 
 MESH = pl.DeviceIdType.MESH
@@ -82,9 +82,9 @@
     evaluate = np.concatenate([wide_h, wide_l, wide_h], axis=0)
     return np.concatenate(
         [
+            np.concatenate([wide_h.T * own, wide_l.T * own], axis=1),
             evaluate[:, : WIDE // 2],
             evaluate[:, WIDE // 2 :],
-            np.concatenate([wide_h.T * own, wide_l.T * own], axis=1),
             np.concatenate([high, low], axis=2).reshape(-1, 2 * RANK),
             back.reshape(-1, 2 * RANK),
         ],
@@ -170,8 +170,8 @@
     bands, spread, east, north, rs, cs, cut, metric, table_in, tan_out, diag_out,
     spread_v, winds_v, rs_v, cs_v, cut_s, hm, table,
     grid, halo_out, halo_in, ybuf, yr, cb, yc, zbuf, zr, eb, bz,
-    tend, proj_p, proj_t, edge_t, edge_proj, adj, gy, tan_v, diag_v,
-    in_sem, halo_send, halo_recv, y_send, y_recv, c_send, c_recv, z_send, z_recv, b_send, b_recv, out_sem,
+    tend, proj_p, proj_t, edge_t, edge_proj, adj, gy,
+    in_sem, halo_send, halo_recv, y_send, y_recv, c_send, c_recv, z_send, z_recv, b_send, b_recv,
 ):
     b = lax.axis_index("lat")
     i = lax.axis_index("lon")
@@ -203,10 +203,13 @@
     load_cols = pltpu.make_async_copy(cs, cs_v, in_sem.at[2])
     load_metric = pltpu.make_async_copy(metric.at[b], hm, in_sem.at[4])
     load_cut = pltpu.make_async_copy(cut, cut_s, in_sem.at[5])
-    load_table = pltpu.make_async_copy(table_in, table, in_sem.at[6])
-    load_part = pltpu.make_async_copy(
-        table_in.at[EVALUATE:FORWARD], table.at[EVALUATE:FORWARD], in_sem.at[6]
-    )
+
+    def load_table(start, stop, sem):
+        return pltpu.make_async_copy(table_in.at[start:stop], table.at[start:stop], in_sem.at[sem])
+
+    load_forward = load_table(FORWARD, EVALUATE, 6)
+    load_others = load_table(EVALUATE, TABLE_ROWS, 7)
+    load_part = load_table(EVALUATE, TO_COEFS, 7)
     load_spread.start()
     load_rows.start()
     load_cols.start()
@@ -230,8 +233,9 @@
         def _(d):
             greet(b, plus(i, d))
 
-        load_table.start()
+        load_forward.start()
         load_cut.start()
+        load_others.start()
 
     @pl.when(jnp.logical_and(near_polar, jnp.logical_not(polar)))
     def _():
@@ -269,7 +273,7 @@
         halo_out[SIDES + s] = roll_blocks(packed, -shift)[0]
 
     def values(q, x):
-        y = to_modes(x.reshape(PAIRS * ROWS, WIDE), table.at[FORWARD:TO_COEFS])
+        y = to_modes(x.reshape(PAIRS * ROWS, WIDE), table.at[FORWARD:EVALUATE])
         y = y.reshape(FIELDS, LEV, 2, 8, RANK)
         for f in range(FIELDS):
             for h in range(2):
@@ -278,7 +282,7 @@
 
     @pl.when(polar)
     def _():
-        load_table.wait()
+        load_forward.wait()
         values(0, grid[0:PAIRS, 8:24, :])
 
     pl.semaphore_wait(barrier, 4 + jnp.where(polar, LANES - 3, 0))
@@ -401,7 +405,7 @@
                 pltpu.make_async_copy(eb.at[j], bz.at[slot, i // 2], b_recv.at[slot]).start()
 
     def evaluate(z):
-        return from_modes(z, table.at[0:384], table.at[384:768])
+        return from_modes(z, table.at[EVALUATE : EVALUATE + 384], table.at[EVALUATE + 384 : TO_COEFS])
 
     def project(q, out):
         all_z(q).wait_recv()
@@ -470,7 +474,7 @@
         for s, sign in ((0, 0.5), (1, -0.5)):
             ghost = flip(s, 1.0) * row_of(halo_in, NEAR + 4 * s)
             added.append(sign * (wind(halo_out, s, 1) * ghost + coupling * row_link(ghost)))
-        y = to_modes(jnp.concatenate(added, axis=0), table.at[FORWARD:TO_COEFS])
+        y = to_modes(jnp.concatenate(added, axis=0), table.at[FORWARD:EVALUATE])
         for s in range(2):
             for f in range(FIELDS):
                 cb[2 * f + s, 0:LEV, :] = y[(s * FIELDS + f) * LEV : (s * FIELDS + f + 1) * LEV, :]
@@ -517,6 +521,7 @@
     @pl.when(polar)
     def _():
         load_cut.wait()
+        load_others.wait()
         own_rows(0)
         own_rows(1)
         edge_sends()
@@ -574,14 +579,11 @@
                 change = time_step * (tend[n, h - 8 : h, :] - proj_t[n, h - 8 : h, :])
                 tend[n, h - 8 : h, :] = change
                 tangent = grid[n, h : h + 8, :] + change
-                tan_v[f, l, h - 8 : h, :] = tangent[:, :COLS]
+                tan_out[f, l, h - 8 : h, :] = tangent[:, :COLS]
                 a.append(tangent - proj_p[n, h - 8 : h, :])
                 adj[n, h - 8 : h, :] = a[f]
             for f, weight in enumerate(row_weights(a, nw)):
                 gy[f * LEV + l, h : h + 8, :] = weight
-
-    tan_copy = pltpu.make_async_copy(tan_v, tan_out, out_sem.at[0])
-    tan_copy.start()
 
     for s, wanted in enumerate((above_polar, below_polar)):
         @pl.when(wanted)
@@ -638,10 +640,7 @@
                 back = back + 0.5 * (gy[n, h - 1 : h + 7, :] - gy[n, h + 1 : h + 9, :])
                 back = back + mixing * (adj[f * LEV + lo, rows, :] + adj[f * LEV + hi, rows, :] - 2.0 * a[f])
                 diag = grid[n, h : h + 8, :] * (tend[n, rows, :] + time_step * back)
-                diag_v[f, l, rows, :] = diag[:, :COLS]
-
-    diag_copy = pltpu.make_async_copy(diag_v, diag_out, out_sem.at[1])
-    diag_copy.start()
+                diag_out[f, l, rows, :] = diag[:, :COLS]
 
     halo_arrival(0, BLOCKS, 0).wait_send()
 
@@ -660,33 +659,31 @@
         def _():
             remote(eb, eb, b_send, b_recv.at[0], b, west).wait_send()
 
-    tan_copy.wait()
-    diag_copy.wait()
-
-
-def hand_out(tan_in, diag_in, tan_out, diag_out, held, in_sem, out_sem):
-    arrive = [pltpu.make_async_copy(src, held.at[n], in_sem.at[n]) for n, src in enumerate((tan_in, diag_in))]
-    leave = [pltpu.make_async_copy(held.at[n], dst, out_sem.at[n]) for n, dst in enumerate((tan_out, diag_out))]
-    for copy in arrive:
+
+def hand_out(tan_in, diag_in, tan_out, diag_out, sem):
+    copies = [
+        pltpu.make_async_copy(src, dst, sem.at[n])
+        for n, (src, dst) in enumerate(((tan_in, tan_out), (diag_in, diag_out)))
+    ]
+    for copy in copies:
         copy.start()
-    for copy, onward in zip(arrive, leave):
+    for copy in copies:
         copy.wait()
-        onward.start()
-    for onward in leave:
-        onward.wait()
 
 
 def per_device(bands, row_signs, col_signs, spread, east_wind, north_wind, cutoffs):
     any_spec = pl.BlockSpec(memory_space=pl.ANY)
     out = jax.ShapeDtypeStruct((FIELDS, LEV, ROWS, COLS), F32)
     tables = [jnp.asarray(half_metric(bands)), jnp.asarray(mode_factors())]
+    operands = (spread, east_wind, north_wind, row_signs, col_signs, cutoffs, *tables)
     vmem = pltpu.VMEM
     dma = pltpu.SemaphoreType.DMA
+    held = pltpu.VMEM(out.shape, F32)
     results = pl.pallas_call(
         functools.partial(kernel, bands),
-        out_shape=(out, out),
+        out_shape=(held, held),
         in_specs=[any_spec] * 8,
-        out_specs=(any_spec, any_spec),
+        out_specs=(pl.BlockSpec(memory_space=pltpu.VMEM),) * 2,
         scratch_shapes=[
             vmem((FIELDS, LEV, ROWS, COLS), F32),
             vmem((2, LEV, ROWS, COLS), F32),
@@ -713,9 +710,7 @@
             vmem((4 * PAIRS, WIDE), F32),
             vmem((PAIRS, ROWS, WIDE), F32),
             vmem((PAIRS, 32, WIDE), F32),
-            vmem((FIELDS, LEV, ROWS, COLS), F32),
-            vmem((FIELDS, LEV, ROWS, COLS), F32),
-            dma((7,)),
+            dma((8,)),
             dma,
             dma((2,)),
             dma,
@@ -726,20 +721,18 @@
             dma((2,)),
             dma,
             dma((2,)),
-            dma((2,)),
         ],
         compiler_params=pltpu.CompilerParams(
-            collective_id=0, has_side_effects=True, vmem_limit_bytes=64 * 2**20
+            collective_id=0, has_side_effects=True, vmem_limit_bytes=32 * 2**20
         ),
         cost_estimate=pl.CostEstimate(flops=10**9, bytes_accessed=4 * 10**6, transcendentals=0),
-    )(spread, east_wind, north_wind, row_signs, col_signs, cutoffs, *tables)
+    )(*(pltpu.with_memory_space_constraint(x, pltpu.HBM) for x in operands))
     return pl.pallas_call(
         hand_out,
         out_shape=(out, out),
         in_specs=[any_spec] * 2,
         out_specs=(any_spec, any_spec),
-        scratch_shapes=[vmem((2, FIELDS, LEV, ROWS, COLS), F32), dma((2,)), dma((2,))],
-        compiler_params=pltpu.CompilerParams(vmem_limit_bytes=64 * 2**20),
+        scratch_shapes=[dma((2,))],
     )(*results)
 
 

time: 24.7 us -> 56.3 us (2.28)
  the two profiles are of different devices: /device:TPU:225 before, /device:TPU:1 now
where the time goes in v9:
time: 56.3 us; the launch traced here: 55.4 us
  Pallas kernels  53.1 us (94%)
  local copies, waits for them, and re-layouts  1.58 us (3%)
  between operations  0.65 us (1%)
    pallas_call x1, Pallas kernels, per_device(): pl.pallas_call(hand_out, out_shape=(out, out), in_specs=[any_spec] * 2, o...  32.9 us
    pallas_call x1, Pallas kernels, per_device(): pl.pallas_call(functools.partial(kernel, bands), out_shape=(held, held),...  20.3 us
    unnamed x4, local copies, waits for them, and re-layouts  1.58 us

profile of v9, /device:TPU:1, one launch (start us, length us, event | category | flops | bytes accessed | tf_op | source)
XLA Modules:
  0.0 55.4 jit_solution(16308452763902907300)
XLA Ops:
  0.6 20.3 %shard_map.95 = (f32[4,4,16,450]{3,2,1,0:T(8,128)S(1)}, f32[4,4,16,450]{3,2,1,0:T(8,128)S(1)}) custom-call(f32[4,4,16,450]{3,2,1,0:T(8,128)} %spread.1, f32[4,16,450]{2,1,0:T(8,128)} %east.1, f32[4,16,450]{2,1,0:T(8,128)} %north.1, s32[4,4,16]{2,1,0:T(4,128)} %rs.1, s32[4,4,450]{2,1,0:T(4,128)} %cs.1, s32[16]{0:T(128)} %cut.1, ...), custom_call_target="tpu_custom_call" | custom-call | flops 1000000000 | bytes 4000000 | tf_op jit(solution)/shard_map/pallas_call | solution.py:682
  20.9 0.0 copy-start
  20.9 0.8 %copy-done = f32[4,4,16,450]{3,2,1,0:T(8,128)} copy-done((f32[4,4,16,450]{3,2,1,0:T(8,128)}, f32[4,4,16,450]{3,2,1,0:T(8,128)S(1)}, u32[]{:S(2)}) %copy-start) | copy-done | bytes 460824
  21.7 0.0 copy-start.1
  21.7 0.8 %copy-done.1 = f32[4,4,16,450]{3,2,1,0:T(8,128)} copy-done((f32[4,4,16,450]{3,2,1,0:T(8,128)}, f32[4,4,16,450]{3,2,1,0:T(8,128)S(1)}, u32[]{:S(2)}) %copy-start.1) | copy-done | bytes 460824
  22.5 32.9 %shard_map.96 = (f32[4,4,16,450]{3,2,1,0:T(8,128)}, f32[4,4,16,450]{3,2,1,0:T(8,128)}) custom-call(f32[4,4,16,450]{3,2,1,0:T(8,128)} %copy-done, f32[4,4,16,450]{3,2,1,0:T(8,128)} %copy-done.1), custom_call_target="tpu_custom_call" | custom-call | tf_op jit(solution)/shard_map/pallas_call | solution.py:730
Async XLA Ops:
  20.9 0.8 %copy-start = (f32[4,4,16,450]{3,2,1,0:T(8,128)}, f32[4,4,16,450]{3,2,1,0:T(8,128)S(1)}, u32[]{:S(2)}) copy-start(f32[4,4,16,450]{3,2,1,0:T(8,128)S(1)} %get-tuple-element.4.tan_in) | copy-start | bytes 1382404
  21.7 0.8 %copy-start.1 = (f32[4,4,16,450]{3,2,1,0:T(8,128)}, f32[4,4,16,450]{3,2,1,0:T(8,128)S(1)}, u32[]{:S(2)}) copy-start(f32[4,4,16,450]{3,2,1,0:T(8,128)S(1)} %get-tuple-element.5.diag_in) | copy-start | bytes 1382404

commit v10 on v9

--- a/solution.py
+++ b/solution.py
@@ -733,7 +733,8 @@
         in_specs=[any_spec] * 2,
         out_specs=(any_spec, any_spec),
         scratch_shapes=[dma((2,))],
-    )(*results)
+        compiler_params=pltpu.CompilerParams(vmem_limit_bytes=2**20),
+    )(*(pltpu.with_memory_space_constraint(x, pltpu.VMEM) for x in results))
 
 
 def solution(mesh):

time: 56.3 us -> 22.8 us (0.40)
  the two profiles are of different devices: /device:TPU:1 before, /device:TPU:225 now
where the time goes in v10:
time: 22.8 us; the launch traced here: 22.7 us
  Pallas kernels  22.1 us (97%)
  between operations  0.64 us (3%)
    pallas_call x1, Pallas kernels, per_device(): pl.pallas_call(functools.partial(kernel, bands), out_shape=(held, held),...  21.1 us
    pallas_call x1, Pallas kernels, per_device(): pl.pallas_call(hand_out, out_shape=(out, out), in_specs=[any_spec] * 2, o...  0.99 us

profile of v10, /device:TPU:225, one launch (start us, length us, event | category | flops | bytes accessed | tf_op | source)
XLA Modules:
  0.0 22.7 jit_solution(11649783911549700334)
XLA Ops:
  0.6 21.1 %shard_map.95 = (f32[4,4,16,450]{3,2,1,0:T(8,128)S(1)}, f32[4,4,16,450]{3,2,1,0:T(8,128)S(1)}) custom-call(f32[4,4,16,450]{3,2,1,0:T(8,128)} %spread.1, f32[4,16,450]{2,1,0:T(8,128)} %east.1, f32[4,16,450]{2,1,0:T(8,128)} %north.1, s32[4,4,16]{2,1,0:T(4,128)} %rs.1, s32[4,4,450]{2,1,0:T(4,128)} %cs.1, s32[16]{0:T(128)} %cut.1, ...), custom_call_target="tpu_custom_call" | custom-call | flops 1000000000 | bytes 4000000 | tf_op jit(solution)/shard_map/pallas_call | solution.py:682
  21.8 1.0 %shard_map.96 = (f32[4,4,16,450]{3,2,1,0:T(8,128)}, f32[4,4,16,450]{3,2,1,0:T(8,128)}) custom-call(f32[4,4,16,450]{3,2,1,0:T(8,128)S(1)} %get-tuple-element.4.tan_in, f32[4,4,16,450]{3,2,1,0:T(8,128)S(1)} %get-tuple-element.5.diag_in), custom_call_target="tpu_custom_call" | custom-call | tf_op jit(solution)/shard_map/pallas_call | solution.py:730

commit v11 on v10

--- a/solution.py
+++ b/solution.py
@@ -170,7 +170,7 @@
     bands, spread, east, north, rs, cs, cut, metric, table_in, tan_out, diag_out,
     spread_v, winds_v, rs_v, cs_v, cut_s, hm, table,
     grid, halo_out, halo_in, ybuf, yr, cb, yc, zbuf, zr, eb, bz,
-    tend, proj_p, proj_t, edge_t, edge_proj, adj, gy,
+    tend, adj, gy,
     in_sem, halo_send, halo_recv, y_send, y_recv, c_send, c_recv, z_send, z_recv, b_send, b_recv,
 ):
     b = lax.axis_index("lat")
@@ -350,13 +350,13 @@
             y = yr[j, q]
             if q == 1:
                 ends = pltpu.roll(yc[j, 8:16, :], lax.rem(128 - 2 * LEV * (i // 2), 128), 1)
-                edge = jnp.where(row == 7 * own_half, 1.0, 0.0)
+                edge_rows = jnp.where(row == 7 * own_half, 1.0, 0.0)
                 y = jnp.concatenate(
                     [
                         y[l]
                         + ends[:, 2 * l : 2 * l + 1] * hm[0:1, :]
                         + ends[:, 2 * l + 1 : 2 * l + 2] * hm[1:2, :]
-                        + edge * yc[j, l : l + 1, :]
+                        + edge_rows * yc[j, l : l + 1, :]
                         for l in range(LEV)
                     ],
                     axis=0,
@@ -378,7 +378,8 @@
         for j, z in enumerate(to_lanes(pairs)):
             z = z.reshape(LEV, 8, RANK)
             zbuf[q, j] = z
-            eb[j, LEV * q : LEV * (q + 1), :] = jnp.where(own_half == 0, z[:, 0, :], z[:, 7, :])
+            edge = jnp.where(own_half == 0, z[:, 0, :], z[:, 7, :])
+            eb[j] = edge if q == 0 else eb[j] + edge
 
         @pl.loop(1, LANES)
         def _(d):
@@ -407,12 +408,10 @@
     def evaluate(z):
         return from_modes(z, table.at[EVALUATE : EVALUATE + 384], table.at[EVALUATE + 384 : TO_COEFS])
 
-    def project(q, out):
-        all_z(q).wait_recv()
-        z = jnp.concatenate(
-            [zr[q, 2 * f + h, l] for f in range(FIELDS) for l in range(LEV) for h in range(2)], axis=0
-        )
-        out[...] = evaluate(z).reshape(PAIRS, ROWS, WIDE)
+    def project(q, h):
+        z = jnp.concatenate([zr[q, 2 * f + h, l] for f in range(FIELDS) for l in range(LEV)], axis=0)
+        out = evaluate(z)
+        return [[out[8 * (LEV * f + l) : 8 * (LEV * f + l + 1), :] for l in range(LEV)] for f in range(FIELDS)]
 
     def tendency_rows(h):
         @pl.loop(0, LEV)
@@ -434,7 +433,7 @@
                 t = -(ew * along_x[f] + nw * along_y[f]) + mixing * mixed
                 if linked[f] is not None:
                     t = t - coupling * linked[f]
-                tend[f * LEV + l, h - 8 : h, :] = t
+                tend[f * LEV + l, h - 8 : h, :] = time_step * t
 
     load_metric.wait()
 
@@ -471,7 +470,7 @@
     @pl.when(polar)
     def _():
         added = []
-        for s, sign in ((0, 0.5), (1, -0.5)):
+        for s, sign in ((0, 0.5 * time_step), (1, -0.5 * time_step)):
             ghost = flip(s, 1.0) * row_of(halo_in, NEAR + 4 * s)
             added.append(sign * (wind(halo_out, s, 1) * ghost + coupling * row_link(ghost)))
         y = to_modes(jnp.concatenate(added, axis=0), table.at[FORWARD:EVALUATE])
@@ -493,7 +492,7 @@
                     jnp.logical_and(lane2 >= 4 * LEV, lane2 < 6 * LEV), roll(along_x, 4 * LEV, 1), 0.0
                 ),
             )
-            ends.append(-ew * along_x - coupling * linked)
+            ends.append(time_step * (-ew * along_x - coupling * linked))
         ends = jnp.where(lax.rem(lane2, 2) == 0, ends[0], roll(ends[1], 1, 1))
         for f in range(FIELDS):
             for h in range(2):
@@ -504,6 +503,12 @@
             c_copy(plus(i, d)).start()
 
         yc[i] = cb[i]
+
+    @pl.when(polar)
+    def _():
+        load_cut.wait()
+        load_others.wait()
+        own_rows(0)
 
     from_west = roll(halo_in[SIDES], 126, 1)
     from_east = roll(halo_in[SIDES + 1], COLS - 384, 1)
@@ -520,9 +525,6 @@
 
     @pl.when(polar)
     def _():
-        load_cut.wait()
-        load_others.wait()
-        own_rows(0)
         own_rows(1)
         edge_sends()
 
@@ -537,6 +539,9 @@
 
     for part in range(2):
         tendency_rows(8 + 8 * part)
+
+    def edge_weights(s, a):
+        return -wind(halo_in, s, 1) * a - coupling * row_link(a)
 
     for s, inward in ((0, 1.0), (1, -1.0)):
         mid = edge_probe[s]
@@ -549,17 +554,8 @@
         up = jnp.where(lax.rem(row16, LEV) == 0, mid, roll(mid, 1, 0))
         down = jnp.where(lax.rem(row16, LEV) == LEV - 1, mid, roll(mid, -1, 0))
         t = -(wind(halo_in, s, 0) * along_x + wind(halo_in, s, 1) * along_y) - coupling * linked
-        edge_t[s] = t + mixing * (up + down - 2.0 * mid)
-
-    @pl.when(polar)
-    def _():
-        project(0, proj_p)
-        project(1, proj_t)
-
-    @pl.when(jnp.logical_not(polar))
-    def _():
-        proj_p[...] = jnp.zeros(proj_p.shape, F32)
-        proj_t[...] = jnp.zeros(proj_t.shape, F32)
+        a = mid + time_step * (t + mixing * (up + down - 2.0 * mid))
+        gy[0:PAIRS, edge_row[s], :] = flip(s, -1.0) * edge_weights(s, a)
 
     def row_weights(a, nw):
         return (
@@ -569,55 +565,45 @@
             -nw * a[3],
         )
 
-    @pl.loop(0, LEV)
-    def _(l):
+    def put_weights(l, h, a):
+        for f, weight in enumerate(row_weights(a, grid[PAIRS + LEV + l, h : h + 8, :])):
+            gy[f * LEV + l, h : h + 8, :] = weight
+
+    @pl.when(polar)
+    def _():
+        all_z(0).wait_recv()
         for h in (8, 16):
-            nw = grid[PAIRS + LEV + l, h : h + 8, :]
-            a = []
-            for f in range(FIELDS):
-                n = f * LEV + l
-                change = time_step * (tend[n, h - 8 : h, :] - proj_t[n, h - 8 : h, :])
-                tend[n, h - 8 : h, :] = change
-                tangent = grid[n, h : h + 8, :] + change
-                tan_out[f, l, h - 8 : h, :] = tangent[:, :COLS]
-                a.append(tangent - proj_p[n, h - 8 : h, :])
-                adj[n, h - 8 : h, :] = a[f]
-            for f, weight in enumerate(row_weights(a, nw)):
-                gy[f * LEV + l, h : h + 8, :] = weight
-
-    for s, wanted in enumerate((above_polar, below_polar)):
-        @pl.when(wanted)
-        def _():
-            remote(bz.at[s], bz.at[s], b_send, b_recv.at[s], nb, nl).wait_recv()
-
-        @pl.when(jnp.logical_not(wanted))
-        def _():
-            bz[s] = jnp.zeros((FIELDS, 2 * LEV, RANK), F32)
-
-    @pl.when(jnp.logical_and(near_polar, jnp.logical_not(polar)))
-    def _():
-        load_part.wait()
-
-    @pl.when(near_polar)
-    def _():
-        parts = [
-            bz[s, f, LEV * q : LEV * (q + 1), :] for s in range(2) for q in range(2) for f in range(FIELDS)
-        ]
-        edge_proj[...] = evaluate(jnp.concatenate(parts, axis=0))
-
-    @pl.when(jnp.logical_not(near_polar))
-    def _():
-        edge_proj[...] = jnp.zeros(edge_proj.shape, F32)
-
-    for s in range(2):
-        base = 2 * PAIRS * s
-        a = (
-            edge_probe[s]
-            + time_step * (edge_t[s] - edge_proj[base + PAIRS : base + 2 * PAIRS, :])
-            - edge_proj[base : base + PAIRS, :]
-        )
-        weight = -wind(halo_in, s, 1) * a - coupling * row_link(a)
-        gy[0:PAIRS, edge_row[s], :] = flip(s, -1.0) * weight
+            taken = project(0, h // 8 - 1)
+            for l in range(LEV):
+                for f in range(FIELDS):
+                    n, rows = f * LEV + l, slice(h - 8, h)
+                    adj[n, rows, :] = grid[n, h : h + 8, :] + tend[n, rows, :] - taken[f][l]
+        all_z(1).wait_recv()
+        for h in (8, 16):
+            taken = project(1, h // 8 - 1)
+            for l in range(LEV):
+                a = []
+                for f in range(FIELDS):
+                    n, rows = f * LEV + l, slice(h - 8, h)
+                    change = tend[n, rows, :] - taken[f][l]
+                    tend[n, rows, :] = change
+                    tan_out[f, l, rows, :] = (grid[n, h : h + 8, :] + change)[:, :COLS]
+                    a.append(adj[n, rows, :] - taken[f][l])
+                    adj[n, rows, :] = a[f]
+                put_weights(l, h, a)
+
+    @pl.when(jnp.logical_not(polar))
+    def _():
+        @pl.loop(0, LEV)
+        def _(l):
+            for h in (8, 16):
+                a = []
+                for f in range(FIELDS):
+                    n, rows = f * LEV + l, slice(h - 8, h)
+                    a.append(grid[n, h : h + 8, :] + tend[n, rows, :])
+                    tan_out[f, l, rows, :] = a[f][:, :COLS]
+                    adj[n, rows, :] = a[f]
+                put_weights(l, h, a)
 
     @pl.loop(0, LEV)
     def _(l):
@@ -641,6 +627,21 @@
                 back = back + mixing * (adj[f * LEV + lo, rows, :] + adj[f * LEV + hi, rows, :] - 2.0 * a[f])
                 diag = grid[n, h : h + 8, :] * (tend[n, rows, :] + time_step * back)
                 diag_out[f, l, rows, :] = diag[:, :COLS]
+
+    @pl.when(jnp.logical_and(near_polar, jnp.logical_not(polar)))
+    def _():
+        load_part.wait()
+
+    for s, wanted in enumerate((above_polar, below_polar)):
+        @pl.when(wanted)
+        def _():
+            remote(bz.at[s], bz.at[s], b_send, b_recv.at[s], nb, nl).wait_recv()
+            taken = evaluate(jnp.concatenate([bz[s, f] for f in range(FIELDS)], axis=0))
+            weight = flip(s, -1.0) * edge_weights(s, taken)
+            row = 15 * s
+            less = ((0.5, -0.5)[s] * time_step) * grid[0:PAIRS, 8 + row, :] * weight
+            for f in range(FIELDS):
+                diag_out[f, :, row, :] = diag_out[f, :, row, :] - less[f * LEV : (f + 1) * LEV, :COLS]
 
     halo_arrival(0, BLOCKS, 0).wait_send()
 
@@ -701,13 +702,9 @@
             vmem((LANES, 16, RANK), F32),
             vmem((2, LANES, LEV, 8, RANK), F32),
             vmem((2, LANES, LEV, 8, RANK), F32),
-            vmem((LANES, 2 * LEV, RANK), F32),
-            vmem((2, FIELDS, 2 * LEV, RANK), F32),
+            vmem((LANES, LEV, RANK), F32),
+            vmem((2, FIELDS, LEV, RANK), F32),
             vmem((PAIRS, ROWS, WIDE), F32),
-            vmem((PAIRS, ROWS, WIDE), F32),
-            vmem((PAIRS, ROWS, WIDE), F32),
-            vmem((2, PAIRS, WIDE), F32),
-            vmem((4 * PAIRS, WIDE), F32),
             vmem((PAIRS, ROWS, WIDE), F32),
             vmem((PAIRS, 32, WIDE), F32),
             dma((8,)),

time: 22.8 us -> 22 us (0.965)
  the two profiles are of different devices: /device:TPU:225 before, /device:TPU:1 now
where the time goes in v11:
time: 22 us; the launch traced here: 21.7 us
  Pallas kernels  21 us (95%)
  between operations  0.64 us (3%)
    pallas_call x1, Pallas kernels, per_device(): pl.pallas_call(functools.partial(kernel, bands), out_shape=(held, held),...  20 us
    pallas_call x1, Pallas kernels, per_device(): pl.pallas_call(hand_out, out_shape=(out, out), in_specs=[any_spec] * 2, o...  0.99 us

profile of v11, /device:TPU:1, one launch (start us, length us, event | category | flops | bytes accessed | tf_op | source)
XLA Modules:
  0.0 21.7 jit_solution(14760996419030193595)
XLA Ops:
  0.6 20.0 %shard_map.95 = (f32[4,4,16,450]{3,2,1,0:T(8,128)S(1)}, f32[4,4,16,450]{3,2,1,0:T(8,128)S(1)}) custom-call(f32[4,4,16,450]{3,2,1,0:T(8,128)} %spread.1, f32[4,16,450]{2,1,0:T(8,128)} %east.1, f32[4,16,450]{2,1,0:T(8,128)} %north.1, s32[4,4,16]{2,1,0:T(4,128)} %rs.1, s32[4,4,450]{2,1,0:T(4,128)} %cs.1, s32[16]{0:T(128)} %cut.1, ...), custom_call_target="tpu_custom_call" | custom-call | flops 1000000000 | bytes 4000000 | tf_op jit(solution)/shard_map/pallas_call | solution.py:683
  20.7 1.0 %shard_map.96 = (f32[4,4,16,450]{3,2,1,0:T(8,128)}, f32[4,4,16,450]{3,2,1,0:T(8,128)}) custom-call(f32[4,4,16,450]{3,2,1,0:T(8,128)S(1)} %get-tuple-element.4.tan_in, f32[4,4,16,450]{3,2,1,0:T(8,128)S(1)} %get-tuple-element.5.diag_in), custom_call_target="tpu_custom_call" | custom-call | tf_op jit(solution)/shard_map/pallas_call | solution.py:727

commit v12 on v11

--- a/solution.py
+++ b/solution.py
@@ -198,7 +198,9 @@
     def plus(lane, d):
         return lax.rem(lane + d, LANES)
 
-    load_spread = pltpu.make_async_copy(spread, spread_v, in_sem.at[0])
+    load_spread = [
+        pltpu.make_async_copy(spread.at[f], spread_v.at[f], in_sem.at[8 + f]) for f in range(FIELDS)
+    ]
     load_rows = pltpu.make_async_copy(rs, rs_v, in_sem.at[1])
     load_cols = pltpu.make_async_copy(cs, cs_v, in_sem.at[2])
     load_metric = pltpu.make_async_copy(metric.at[b], hm, in_sem.at[4])
@@ -210,9 +212,10 @@
     load_forward = load_table(FORWARD, EVALUATE, 6)
     load_others = load_table(EVALUATE, TABLE_ROWS, 7)
     load_part = load_table(EVALUATE, TO_COEFS, 7)
-    load_spread.start()
     load_rows.start()
     load_cols.start()
+    for load in load_spread:
+        load.start()
     pltpu.make_async_copy(east, winds_v.at[0], in_sem.at[3]).start()
     pltpu.make_async_copy(north, winds_v.at[1], in_sem.at[3]).start()
     load_metric.start()
@@ -235,7 +238,6 @@
 
         load_forward.start()
         load_cut.start()
-        load_others.start()
 
     @pl.when(jnp.logical_and(near_polar, jnp.logical_not(polar)))
     def _():
@@ -243,15 +245,20 @@
 
     load_rows.wait()
     load_cols.wait()
-    load_spread.wait()
     grid[:, 8:24, 384:512] = jnp.zeros((PAIRS + 2 * LEV, ROWS, 128), F32)
     row_part = jnp.concatenate([rs_v[f] for f in range(FIELDS)], axis=0)
     row_part = (2 * row_part - 1).astype(F32).T
     for f in range(FIELDS):
         col_part = (2 * cs_v[f] - 1).astype(F32)
+        load_spread[f].wait()
         for l in range(LEV):
             n = f * LEV + l
             grid[n, 8:24, 0:COLS] = spread_v[f, l] * (row_part[:, n : n + 1] * col_part[l : l + 1, :])
+
+    @pl.when(polar)
+    def _():
+        load_others.start()
+
     pltpu.make_async_copy(winds_v, winds_v, in_sem.at[3]).wait()
     for w in range(2):
         for l in range(LEV):
@@ -271,19 +278,6 @@
         tile = jnp.where(jnp.logical_and(lane128 >= shift, lane128 < shift + 2), tile, 0.0)
         packed = fold(tile[:PAIRS]) + roll_blocks(fold(tile[PAIRS:]), 2 * PAIRS)
         halo_out[SIDES + s] = roll_blocks(packed, -shift)[0]
-
-    def values(q, x):
-        y = to_modes(x.reshape(PAIRS * ROWS, WIDE), table.at[FORWARD:EVALUATE])
-        y = y.reshape(FIELDS, LEV, 2, 8, RANK)
-        for f in range(FIELDS):
-            for h in range(2):
-                for l in range(LEV):
-                    ybuf[2 * f + h, q, l] = y[f, l, h]
-
-    @pl.when(polar)
-    def _():
-        load_forward.wait()
-        values(0, grid[0:PAIRS, 8:24, :])
 
     pl.semaphore_wait(barrier, 4 + jnp.where(polar, LANES - 3, 0))
 
@@ -362,19 +356,20 @@
                     axis=0,
                 )
             lanes.append(y.reshape(LEV * 8, RANK))
-        pairs = []
-        over = over_lanes(lanes)
-        for group, pair in enumerate(over):
-            coef = to_modes(
-                jnp.concatenate(pair, axis=1), table.at[TO_COEFS + 256 * group : TO_COEFS + 256 * (group + 1)]
-            )
+        coefs = [
+            to_modes(jnp.concatenate(pair, axis=1), table.at[TO_COEFS + 256 * group : TO_COEFS + 256 * (group + 1)])
+            for group, pair in enumerate(over_lanes(lanes))
+        ]
+        kept = []
+        for group, coef in enumerate(coefs):
             wave = waves_of(group, lax.broadcasted_iota(jnp.int32, (8, 128), 1))
             keep = jnp.where(wave > cutoff, 2.0 / (COLS * LANES), 0.0)
-            back = from_modes(
-                coef * jnp.concatenate([keep] * LEV, axis=0),
-                table.at[FROM_COEFS + 384 * group : FROM_COEFS + 384 * (group + 1)],
-            )
-            pairs.append((back[:, :RANK], back[:, RANK:]))
+            kept.append(coef * jnp.concatenate([keep] * LEV, axis=0))
+        backs = [
+            from_modes(coef, table.at[FROM_COEFS + 384 * group : FROM_COEFS + 384 * (group + 1)])
+            for group, coef in enumerate(kept)
+        ]
+        pairs = [(back[:, :RANK], back[:, RANK:]) for back in backs]
         for j, z in enumerate(to_lanes(pairs)):
             z = z.reshape(LEV, 8, RANK)
             zbuf[q, j] = z
@@ -443,7 +438,16 @@
         grid[0:PAIRS, 24:25, :] = jnp.zeros((PAIRS, 1, WIDE), F32)
         for part in range(2):
             tendency_rows(8 + 8 * part)
-        values(1, tend[...])
+        load_forward.wait()
+        probe = grid[0:PAIRS, 8:24, :].reshape(PAIRS * ROWS, WIDE)
+        change = tend[...].reshape(PAIRS * ROWS, WIDE)
+        y = to_modes(jnp.concatenate([probe, change], axis=0), table.at[FORWARD:EVALUATE])
+        y = y.reshape(2, FIELDS, LEV, 2, 8, RANK)
+        for q in range(2):
+            for f in range(FIELDS):
+                for h in range(2):
+                    for l in range(LEV):
+                        ybuf[2 * f + h, q, l] = y[q, f, l, h]
         send_values()
 
     halo_arrival(NEAR, REST, 0).wait_recv()
@@ -636,9 +640,16 @@
         @pl.when(wanted)
         def _():
             remote(bz.at[s], bz.at[s], b_send, b_recv.at[s], nb, nl).wait_recv()
-            taken = evaluate(jnp.concatenate([bz[s, f] for f in range(FIELDS)], axis=0))
-            weight = flip(s, -1.0) * edge_weights(s, taken)
-            row = 15 * s
+
+        @pl.when(jnp.logical_not(wanted))
+        def _():
+            bz[s] = jnp.zeros((FIELDS, LEV, RANK), F32)
+
+    @pl.when(near_polar)
+    def _():
+        taken = evaluate(jnp.concatenate([bz[s, f] for s in range(2) for f in range(FIELDS)], axis=0))
+        for s, row in ((0, 0), (1, 15)):
+            weight = flip(s, -1.0) * edge_weights(s, taken[PAIRS * s : PAIRS * (s + 1), :])
             less = ((0.5, -0.5)[s] * time_step) * grid[0:PAIRS, 8 + row, :] * weight
             for f in range(FIELDS):
                 diag_out[f, :, row, :] = diag_out[f, :, row, :] - less[f * LEV : (f + 1) * LEV, :COLS]
@@ -707,7 +718,7 @@
             vmem((PAIRS, ROWS, WIDE), F32),
             vmem((PAIRS, ROWS, WIDE), F32),
             vmem((PAIRS, 32, WIDE), F32),
-            dma((8,)),
+            dma((12,)),
             dma,
             dma((2,)),
             dma,

time: 22 us -> 22 us (level)
  no operation moved by 1% of the time
where the time goes in v12:
time: 22 us; the launch traced here: 21.7 us
  Pallas kernels  21.1 us (96%)
  between operations  0.64 us (3%)
    pallas_call x1, Pallas kernels, per_device(): pl.pallas_call(functools.partial(kernel, bands), out_shape=(held, held),...  20.1 us
    pallas_call x1, Pallas kernels, per_device(): pl.pallas_call(hand_out, out_shape=(out, out), in_specs=[any_spec] * 2, o...  0.99 us

profile of v12, /device:TPU:1, one launch (start us, length us, event | category | flops | bytes accessed | tf_op | source)
XLA Modules:
  0.0 21.7 jit_solution(10794066223265568740)
XLA Ops:
  0.6 20.1 %shard_map.95 = (f32[4,4,16,450]{3,2,1,0:T(8,128)S(1)}, f32[4,4,16,450]{3,2,1,0:T(8,128)S(1)}) custom-call(f32[4,4,16,450]{3,2,1,0:T(8,128)} %spread.1, f32[4,16,450]{2,1,0:T(8,128)} %east.1, f32[4,16,450]{2,1,0:T(8,128)} %north.1, s32[4,4,16]{2,1,0:T(4,128)} %rs.1, s32[4,4,450]{2,1,0:T(4,128)} %cs.1, s32[16]{0:T(128)} %cut.1, ...), custom_call_target="tpu_custom_call" | custom-call | flops 1000000000 | bytes 4000000 | tf_op jit(solution)/shard_map/pallas_call | solution.py:694
  20.8 1.0 %shard_map.96 = (f32[4,4,16,450]{3,2,1,0:T(8,128)}, f32[4,4,16,450]{3,2,1,0:T(8,128)}) custom-call(f32[4,4,16,450]{3,2,1,0:T(8,128)S(1)} %get-tuple-element.4.tan_in, f32[4,4,16,450]{3,2,1,0:T(8,128)S(1)} %get-tuple-element.5.diag_in), custom_call_target="tpu_custom_call" | custom-call | tf_op jit(solution)/shard_map/pallas_call | solution.py:738

commit v13 on v12

--- a/solution.py
+++ b/solution.py
@@ -12,6 +12,7 @@
 KTOP = 256
 POLAR = 32
 RANK = 128
+USED = 96
 ROWS = 16
 COLS = 450
 WIDE = 512
@@ -25,7 +26,7 @@
 mixing = 0.2
 metric_cap = 4.0
 
-FORWARD, EVALUATE, TO_COEFS, FROM_COEFS, TABLE_ROWS = 0, 512, 1280, 2304, 3840
+FORWARD, EVALUATE, TO_COEFS, FROM_COEFS, TABLE_ROWS = 0, 512, 1280, 2304, 3328
 NEAR, SIDES, REST, BLOCKS = 0, 8, 10, 24
 
 MESH = pl.DeviceIdType.MESH
@@ -56,7 +57,7 @@
     diag = ((size - 1 - 2 * place) / 2) ** 2 * np.cos(2 * np.pi * width)
     side = place[1:] * (size - place[1:]) / 2
     vectors = np.linalg.eigh(np.diag(diag) + np.diag(side, 1) + np.diag(side, -1))[1]
-    basis = vectors[:, ::-1][:, :RANK]
+    basis = np.concatenate([vectors[:, ::-1][:, :USED], np.zeros((size, RANK - USED))], axis=1)
     basis = basis * np.where(basis[size // 2] < 0, -1.0, 1.0)
     weights = []
     for group in range(4):
@@ -78,7 +79,7 @@
     wide_h, wide_l = split_table(wide)
     own = np.where(np.arange(WIDE)[:, None] < COLS, 1, 0).astype(ml_dtypes.bfloat16)
     high, low = split_table(weights)
-    back = np.concatenate([np.swapaxes(part, 1, 2) for part in (high, low, high)], axis=1)
+    back = np.concatenate([np.swapaxes(part, 1, 2) for part in (high, low)], axis=1)
     evaluate = np.concatenate([wide_h, wide_l, wide_h], axis=0)
     return np.concatenate(
         [
@@ -151,6 +152,31 @@
     return jnp.concatenate([dot_cols(three, table[...]) for table in tables], axis=1)
 
 
+def to_coefs(x, table):
+    rows = x.shape[0]
+    wide = dot_cols(jnp.concatenate(split(x), axis=0), table[...])
+    half = wide.shape[1] // 2
+    return wide[:rows, :half] + wide[:rows, half:] + wide[rows:, :half]
+
+
+def from_coefs(z, table):
+    zh, zl = split(z)
+    rows = jnp.concatenate([jnp.concatenate([zh, zh], axis=1), jnp.concatenate([zl, jnp.zeros_like(zl)], axis=1)], axis=0)
+    wide = dot_cols(rows, table[...])
+    return wide[: z.shape[0]] + wide[z.shape[0] :]
+
+
+def pack(levels):
+    lane = lax.broadcasted_iota(jnp.int32, (1, RANK), 1)
+    return [jnp.where(lane < USED, levels[l], roll(levels[3], 96 - 32 * l, 1)) for l in range(3)]
+
+
+def unpack(parts):
+    lane = lax.broadcasted_iota(jnp.int32, (1, RANK), 1)
+    last = jnp.where(lane < 64, roll(parts[1], 64, 1), roll(parts[2], 96, 1))
+    return parts + [jnp.where(lane < 32, roll(parts[0], 32, 1), last)]
+
+
 def roll(x, shift, axis):
     return pltpu.roll(x, shift % x.shape[axis], axis)
 
@@ -169,7 +195,7 @@
 def kernel(
     bands, spread, east, north, rs, cs, cut, metric, table_in, tan_out, diag_out,
     spread_v, winds_v, rs_v, cs_v, cut_s, hm, table,
-    grid, halo_out, halo_in, ybuf, yr, cb, yc, zbuf, zr, eb, bz,
+    grid, halo_out, halo_in, ybuf, yr, xb, cb, yc, zbuf, zr, eb, bz,
     tend, adj, gy,
     in_sem, halo_send, halo_recv, y_send, y_recv, c_send, c_recv, z_send, z_recv, b_send, b_recv,
 ):
@@ -339,25 +365,23 @@
         else:
             all_c().wait_recv()
 
+        levels = unpack([yr[:, q, l].reshape(LANES * 8, RANK) for l in range(LEV - 1)])
         lanes = []
         for j in range(LANES):
-            y = yr[j, q]
+            y = [levels[l][8 * j : 8 * j + 8, :] for l in range(LEV)]
             if q == 1:
                 ends = pltpu.roll(yc[j, 8:16, :], lax.rem(128 - 2 * LEV * (i // 2), 128), 1)
                 edge_rows = jnp.where(row == 7 * own_half, 1.0, 0.0)
-                y = jnp.concatenate(
-                    [
-                        y[l]
-                        + ends[:, 2 * l : 2 * l + 1] * hm[0:1, :]
-                        + ends[:, 2 * l + 1 : 2 * l + 2] * hm[1:2, :]
-                        + edge_rows * yc[j, l : l + 1, :]
-                        for l in range(LEV)
-                    ],
-                    axis=0,
-                )
-            lanes.append(y.reshape(LEV * 8, RANK))
+                y = [
+                    y[l]
+                    + ends[:, 2 * l : 2 * l + 1] * hm[0:1, :]
+                    + ends[:, 2 * l + 1 : 2 * l + 2] * hm[1:2, :]
+                    + edge_rows * yc[j, l : l + 1, :]
+                    for l in range(LEV)
+                ]
+            lanes.append(jnp.concatenate(y, axis=0))
         coefs = [
-            to_modes(jnp.concatenate(pair, axis=1), table.at[TO_COEFS + 256 * group : TO_COEFS + 256 * (group + 1)])
+            to_coefs(jnp.concatenate(pair, axis=1), table.at[TO_COEFS + 256 * group : TO_COEFS + 256 * (group + 1)])
             for group, pair in enumerate(over_lanes(lanes))
         ]
         kept = []
@@ -366,13 +390,14 @@
             keep = jnp.where(wave > cutoff, 2.0 / (COLS * LANES), 0.0)
             kept.append(coef * jnp.concatenate([keep] * LEV, axis=0))
         backs = [
-            from_modes(coef, table.at[FROM_COEFS + 384 * group : FROM_COEFS + 384 * (group + 1)])
+            from_coefs(coef, table.at[FROM_COEFS + 256 * group : FROM_COEFS + 256 * (group + 1)])
             for group, coef in enumerate(kept)
         ]
         pairs = [(back[:, :RANK], back[:, RANK:]) for back in backs]
-        for j, z in enumerate(to_lanes(pairs)):
-            z = z.reshape(LEV, 8, RANK)
-            zbuf[q, j] = z
+        zs = [z.reshape(LEV, 8, RANK) for z in to_lanes(pairs)]
+        for l, part in enumerate(pack([jnp.concatenate([z[l] for z in zs], axis=0) for l in range(LEV)])):
+            zbuf[q, :, l] = part.reshape(LANES, 8, RANK)
+        for j, z in enumerate(zs):
             edge = jnp.where(own_half == 0, z[:, 0, :], z[:, 7, :])
             eb[j] = edge if q == 0 else eb[j] + edge
 
@@ -404,31 +429,58 @@
         return from_modes(z, table.at[EVALUATE : EVALUATE + 384], table.at[EVALUATE + 384 : TO_COEFS])
 
     def project(q, h):
-        z = jnp.concatenate([zr[q, 2 * f + h, l] for f in range(FIELDS) for l in range(LEV)], axis=0)
+        levels = unpack(
+            [jnp.concatenate([zr[q, 2 * f + h, l] for f in range(FIELDS)], axis=0) for l in range(LEV - 1)]
+        )
+        z = jnp.concatenate(
+            [levels[l][8 * f : 8 * f + 8, :] for f in range(FIELDS) for l in range(LEV)], axis=0
+        )
         out = evaluate(z)
         return [[out[8 * (LEV * f + l) : 8 * (LEV * f + l + 1), :] for l in range(LEV)] for f in range(FIELDS)]
 
-    def tendency_rows(h):
+    def tendency_rows(h, l, at, half):
+        lo = jnp.maximum(l - 1, 0)
+        hi = jnp.minimum(l + 1, LEV - 1)
+        ew = at(PAIRS + l, h)
+        nw = at(PAIRS + LEV + l, h)
+        mids, along_x, along_y = [], [], []
+        for f in range(FIELDS):
+            mid = at(f * LEV + l, h)
+            mids.append(mid)
+            along_x.append(half * (roll(mid, -1, 1) - roll(mid, 1, 1)))
+            along_y.append(0.5 * (at(f * LEV + l, h + 1) - at(f * LEV + l, h - 1)))
+        linked = (along_x[2], along_y[2], along_x[0] + along_y[1], None)
+        out = []
+        for f in range(FIELDS):
+            mixed = at(f * LEV + lo, h) + at(f * LEV + hi, h) - 2.0 * mids[f]
+            t = -(ew * along_x[f] + nw * along_y[f]) + mixing * mixed
+            if linked[f] is not None:
+                t = t - coupling * linked[f]
+            out.append(time_step * t)
+        return out
+
+    def full_tendency():
         @pl.loop(0, LEV)
         def _(l):
-            lo = jnp.maximum(l - 1, 0)
-            hi = jnp.minimum(l + 1, LEV - 1)
-            half = jnp.concatenate([hm[h : h + 8, :]] * 4, axis=1)
-            ew = grid[PAIRS + l, h : h + 8, :]
-            nw = grid[PAIRS + LEV + l, h : h + 8, :]
-            along_x, along_y = [], []
-            for f in range(FIELDS):
-                mid = grid[f * LEV + l, h : h + 8, :]
-                along_x.append(half * (roll(mid, -1, 1) - roll(mid, 1, 1)))
-                along_y.append(0.5 * (grid[f * LEV + l, h + 1 : h + 9, :] - grid[f * LEV + l, h - 1 : h + 7, :]))
-            linked = (along_x[2], along_y[2], along_x[0] + along_y[1], None)
-            for f in range(FIELDS):
-                mid = grid[f * LEV + l, h : h + 8, :]
-                mixed = grid[f * LEV + lo, h : h + 8, :] + grid[f * LEV + hi, h : h + 8, :] - 2.0 * mid
-                t = -(ew * along_x[f] + nw * along_y[f]) + mixing * mixed
-                if linked[f] is not None:
-                    t = t - coupling * linked[f]
-                tend[f * LEV + l, h - 8 : h, :] = time_step * t
+            for h in (8, 16):
+                half = jnp.concatenate([hm[h : h + 8, :]] * 4, axis=1)
+                for f, t in enumerate(tendency_rows(h, l, lambda n, r: grid[n, r : r + 8, :], half)):
+                    tend[f * LEV + l, h - 8 : h, :] = t
+
+    def side_tendency():
+        lane = lax.broadcasted_iota(jnp.int32, (1, 128), 1)
+        late = jnp.logical_or(jnp.logical_or(lane == 65, lane == 66), lane == 127)
+
+        def at(n, r):
+            return jnp.where(lane < 2, grid[n, r : r + 8, 0:128], grid[n, r : r + 8, 384:512])
+
+        @pl.loop(0, LEV)
+        def _(l):
+            for h in (8, 16):
+                for f, t in enumerate(tendency_rows(h, l, at, hm[h : h + 8, :])):
+                    n, rows = f * LEV + l, slice(h - 8, h)
+                    tend[n, rows, 0:128] = jnp.where(lane == 0, t, tend[n, rows, 0:128])
+                    tend[n, rows, 384:512] = jnp.where(late, t, tend[n, rows, 384:512])
 
     load_metric.wait()
 
@@ -436,18 +488,19 @@
     def _():
         grid[0:PAIRS, 7:8, :] = jnp.zeros((PAIRS, 1, WIDE), F32)
         grid[0:PAIRS, 24:25, :] = jnp.zeros((PAIRS, 1, WIDE), F32)
-        for part in range(2):
-            tendency_rows(8 + 8 * part)
+        full_tendency()
         load_forward.wait()
         probe = grid[0:PAIRS, 8:24, :].reshape(PAIRS * ROWS, WIDE)
         change = tend[...].reshape(PAIRS * ROWS, WIDE)
         y = to_modes(jnp.concatenate([probe, change], axis=0), table.at[FORWARD:EVALUATE])
         y = y.reshape(2, FIELDS, LEV, 2, 8, RANK)
         for q in range(2):
-            for f in range(FIELDS):
-                for h in range(2):
-                    for l in range(LEV):
-                        ybuf[2 * f + h, q, l] = y[q, f, l, h]
+            blocks = [
+                jnp.concatenate([y[q, f, l, h] for f in range(FIELDS) for h in range(2)], axis=0)
+                for l in range(LEV)
+            ]
+            for l, part in enumerate(pack(blocks)):
+                ybuf[:, q, l] = part.reshape(LANES, 8, RANK)
         send_values()
 
     halo_arrival(NEAR, REST, 0).wait_recv()
@@ -477,6 +530,7 @@
         for s, sign in ((0, 0.5 * time_step), (1, -0.5 * time_step)):
             ghost = flip(s, 1.0) * row_of(halo_in, NEAR + 4 * s)
             added.append(sign * (wind(halo_out, s, 1) * ghost + coupling * row_link(ghost)))
+            xb[s] = added[s]
         y = to_modes(jnp.concatenate(added, axis=0), table.at[FORWARD:EVALUATE])
         for s in range(2):
             for f in range(FIELDS):
@@ -541,8 +595,15 @@
         )
         grid[0:PAIRS, edge_row[s], :] = flip(s, 1.0) * edge_probe[s]
 
-    for part in range(2):
-        tendency_rows(8 + 8 * part)
+    @pl.when(polar)
+    def _():
+        for s, row in ((0, 0), (1, 15)):
+            tend[:, row, :] = tend[:, row, :] + xb[s]
+        side_tendency()
+
+    @pl.when(jnp.logical_not(polar))
+    def _():
+        full_tendency()
 
     def edge_weights(s, a):
         return -wind(halo_in, s, 1) * a - coupling * row_link(a)
@@ -707,12 +768,13 @@
             vmem((PAIRS + 2 * LEV, 32, WIDE), F32),
             vmem((BLOCKS, 16, 128), F32),
             vmem((BLOCKS, 16, 128), F32),
-            vmem((LANES, 2, LEV, 8, RANK), F32),
-            vmem((LANES, 2, LEV, 8, RANK), F32),
+            vmem((LANES, 2, LEV - 1, 8, RANK), F32),
+            vmem((LANES, 2, LEV - 1, 8, RANK), F32),
+            vmem((2, PAIRS, WIDE), F32),
             vmem((LANES, 16, RANK), F32),
             vmem((LANES, 16, RANK), F32),
-            vmem((2, LANES, LEV, 8, RANK), F32),
-            vmem((2, LANES, LEV, 8, RANK), F32),
+            vmem((2, LANES, LEV - 1, 8, RANK), F32),
+            vmem((2, LANES, LEV - 1, 8, RANK), F32),
             vmem((LANES, LEV, RANK), F32),
             vmem((2, FIELDS, LEV, RANK), F32),
             vmem((PAIRS, ROWS, WIDE), F32),

time: 22 us -> 21.7 us (0.986)
  the two profiles are of different devices: /device:TPU:1 before, /device:TPU:225 now
where the time goes in v13:
time: 21.7 us; the launch traced here: 21.6 us
  Pallas kernels  20.9 us (96%)
  between operations  0.64 us (3%)
    pallas_call x1, Pallas kernels, per_device(): pl.pallas_call(functools.partial(kernel, bands), out_shape=(held, held),...  20 us
    pallas_call x1, Pallas kernels, per_device(): pl.pallas_call(hand_out, out_shape=(out, out), in_specs=[any_spec] * 2, o...  0.99 us

profile of v13, /device:TPU:225, one launch (start us, length us, event | category | flops | bytes accessed | tf_op | source)
XLA Modules:
  0.0 21.6 jit_solution(516530582199141729)
XLA Ops:
  0.6 20.0 %shard_map.95 = (f32[4,4,16,450]{3,2,1,0:T(8,128)S(1)}, f32[4,4,16,450]{3,2,1,0:T(8,128)S(1)}) custom-call(f32[4,4,16,450]{3,2,1,0:T(8,128)} %spread.1, f32[4,16,450]{2,1,0:T(8,128)} %east.1, f32[4,16,450]{2,1,0:T(8,128)} %north.1, s32[4,4,16]{2,1,0:T(4,128)} %rs.1, s32[4,4,450]{2,1,0:T(4,128)} %cs.1, s32[16]{0:T(128)} %cut.1, ...), custom_call_target="tpu_custom_call" | custom-call | flops 1000000000 | bytes 4000000 | tf_op jit(solution)/shard_map/pallas_call | solution.py:755
  20.6 1.0 %shard_map.96 = (f32[4,4,16,450]{3,2,1,0:T(8,128)}, f32[4,4,16,450]{3,2,1,0:T(8,128)}) custom-call(f32[4,4,16,450]{3,2,1,0:T(8,128)S(1)} %get-tuple-element.4.tan_in, f32[4,4,16,450]{3,2,1,0:T(8,128)S(1)} %get-tuple-element.5.diag_in), custom_call_target="tpu_custom_call" | custom-call | tf_op jit(solution)/shard_map/pallas_call | solution.py:800

commit v14 on v13

--- a/solution.py
+++ b/solution.py
@@ -220,13 +220,14 @@
     own_half = lax.rem(i, 2)
     edge_over = jnp.where(own_half == 0, is_north, is_south)
     over_pole = (is_north, is_south)
+    outward = jnp.logical_or(
+        jnp.logical_and(b == caps - 1, own_half == 1), jnp.logical_and(b == bands - caps, own_half == 0)
+    )
 
     def plus(lane, d):
         return lax.rem(lane + d, LANES)
 
-    load_spread = [
-        pltpu.make_async_copy(spread.at[f], spread_v.at[f], in_sem.at[8 + f]) for f in range(FIELDS)
-    ]
+    load_spread = pltpu.make_async_copy(spread, spread_v, in_sem.at[0])
     load_rows = pltpu.make_async_copy(rs, rs_v, in_sem.at[1])
     load_cols = pltpu.make_async_copy(cs, cs_v, in_sem.at[2])
     load_metric = pltpu.make_async_copy(metric.at[b], hm, in_sem.at[4])
@@ -238,13 +239,9 @@
     load_forward = load_table(FORWARD, EVALUATE, 6)
     load_others = load_table(EVALUATE, TABLE_ROWS, 7)
     load_part = load_table(EVALUATE, TO_COEFS, 7)
+    load_spread.start()
     load_rows.start()
     load_cols.start()
-    for load in load_spread:
-        load.start()
-    pltpu.make_async_copy(east, winds_v.at[0], in_sem.at[3]).start()
-    pltpu.make_async_copy(north, winds_v.at[1], in_sem.at[3]).start()
-    load_metric.start()
 
     barrier = pltpu.get_barrier_semaphore()
 
@@ -255,6 +252,9 @@
     greet(sb, sl)
     greet(b, west)
     greet(b, east_lane)
+    pltpu.make_async_copy(east, winds_v.at[0], in_sem.at[3]).start()
+    pltpu.make_async_copy(north, winds_v.at[1], in_sem.at[3]).start()
+    load_metric.start()
 
     @pl.when(polar)
     def _():
@@ -271,12 +271,12 @@
 
     load_rows.wait()
     load_cols.wait()
+    load_spread.wait()
     grid[:, 8:24, 384:512] = jnp.zeros((PAIRS + 2 * LEV, ROWS, 128), F32)
     row_part = jnp.concatenate([rs_v[f] for f in range(FIELDS)], axis=0)
     row_part = (2 * row_part - 1).astype(F32).T
     for f in range(FIELDS):
         col_part = (2 * cs_v[f] - 1).astype(F32)
-        load_spread[f].wait()
         for l in range(LEV):
             n = f * LEV + l
             grid[n, 8:24, 0:COLS] = spread_v[f, l] * (row_part[:, n : n + 1] * col_part[l : l + 1, :])
@@ -290,14 +290,16 @@
         for l in range(LEV):
             grid[PAIRS + w * LEV + l, 8:24, 0:COLS] = winds_v[w, l]
 
-    for s, (near, far) in enumerate(((8, 9), (23, 22))):
-        for t in range(4):
-            lanes = slice(128 * t, 128 * t + 128)
-            halo_out[NEAR + 4 * s + t] = grid[0:PAIRS, near, lanes]
-            halo_out[REST + 7 * s + t] = grid[0:PAIRS, far, lanes]
-            halo_out[REST + 7 * s + 4 + t // 2, 8 * (t % 2) : 8 * (t % 2) + 8, :] = grid[
-                PAIRS : PAIRS + 2 * LEV, near, lanes
-            ]
+    def edge_rows(start, entries, rows):
+        for s, row in enumerate(rows):
+            for t in range(4):
+                values = grid[entries, row, 128 * t : 128 * t + 128]
+                if entries == slice(0, PAIRS):
+                    halo_out[start[s] + t] = values
+                else:
+                    halo_out[start[s] + t // 2, 8 * (t % 2) : 8 * (t % 2) + 8, :] = values
+
+    edge_rows((NEAR, NEAR + 4), slice(0, PAIRS), (8, 23))
     lane128 = lax.broadcasted_iota(jnp.int32, (1, 1, 128), 2)
     for s, (start, shift) in enumerate(((0, 0), (384, COLS - 2 - 384))):
         tile = grid[:, 8:24, start : start + 128]
@@ -327,20 +329,26 @@
     halo_copy(SIDES, 1, SIDES + 1, 0, b, west).start()
     halo_copy(SIDES + 1, 1, SIDES, 0, b, east_lane).start()
 
-    def y_copy(o):
-        return remote(ybuf.at[o], yr.at[i], y_send, y_recv, b, o)
-
     others = pl.ds(0, LANES - 1)
 
-    def all_y():
-        return remote(ybuf.at[others], yr.at[others], y_send, y_recv, b, west)
-
-    def send_values():
+    def all_y(q):
+        return remote(ybuf.at[q, others], yr.at[q, others], y_send.at[q], y_recv.at[q], b, west)
+
+    def send_values(q, x):
+        y = to_modes(x.reshape(PAIRS * ROWS, WIDE), table.at[FORWARD:EVALUATE])
+        y = y.reshape(FIELDS, LEV, 2, 8, RANK)
+        blocks = [
+            jnp.concatenate([y[f, l, h] for f in range(FIELDS) for h in range(2)], axis=0) for l in range(LEV)
+        ]
+        for l, part in enumerate(pack(blocks)):
+            ybuf[q, :, l] = part.reshape(LANES, 8, RANK)
+
         @pl.loop(1, LANES)
         def _(d):
-            y_copy(plus(i, d)).start()
-
-        yr[i] = ybuf[i]
+            o = plus(i, d)
+            remote(ybuf.at[q, o], yr.at[q, i], y_send.at[q], y_recv.at[q], b, o).start()
+
+        yr[q, i] = ybuf[q, i]
 
     def c_copy(o):
         return remote(cb.at[o], yc.at[i], c_send, c_recv, b, o)
@@ -353,6 +361,24 @@
 
     def all_z(q):
         return remote(zbuf.at[q, others], zr.at[q, others], z_send.at[q], z_recv.at[q], b, west)
+
+    def edge_sends():
+        slot = jnp.where(own_half == 0, slot_n, slot_s)
+        lat = jnp.where(own_half == 0, nb, sb)
+
+        @pl.loop(0, LANES)
+        def _(d):
+            j = plus(i, d)
+            lon = jnp.where(edge_over, plus(j, LANES // 2), j)
+            here = jnp.logical_and(edge_over, lon == i)
+
+            @pl.when(jnp.logical_not(here))
+            def _():
+                remote(eb.at[j], bz.at[slot, i // 2], b_send, b_recv.at[slot], lat, lon).start()
+
+            @pl.when(here)
+            def _():
+                pltpu.make_async_copy(eb.at[j], bz.at[slot, i // 2], b_recv.at[slot]).start()
 
     def own_rows(q):
         row = lax.broadcasted_iota(jnp.int32, (8, 128), 0)
@@ -360,12 +386,11 @@
         for r in range(8):
             cutoff = jnp.where(row == r, cut_s[8 * own_half + r], cutoff)
 
-        if q == 0:
-            all_y().wait_recv()
-        else:
+        all_y(q).wait_recv()
+        if q == 1:
             all_c().wait_recv()
 
-        levels = unpack([yr[:, q, l].reshape(LANES * 8, RANK) for l in range(LEV - 1)])
+        levels = unpack([yr[q, :, l].reshape(LANES * 8, RANK) for l in range(LEV - 1)])
         lanes = []
         for j in range(LANES):
             y = [levels[l][8 * j : 8 * j + 8, :] for l in range(LEV)]
@@ -401,29 +426,16 @@
             edge = jnp.where(own_half == 0, z[:, 0, :], z[:, 7, :])
             eb[j] = edge if q == 0 else eb[j] + edge
 
+        if q == 1:
+            pl.when(outward)(edge_sends)
+
         @pl.loop(1, LANES)
         def _(d):
             z_copy(q, plus(i, d)).start()
 
         zr[q, i] = zbuf[q, i]
-
-    def edge_sends():
-        slot = jnp.where(own_half == 0, slot_n, slot_s)
-        lat = jnp.where(own_half == 0, nb, sb)
-
-        @pl.loop(0, LANES)
-        def _(d):
-            j = plus(i, d)
-            lon = jnp.where(edge_over, plus(j, LANES // 2), j)
-            here = jnp.logical_and(edge_over, lon == i)
-
-            @pl.when(jnp.logical_not(here))
-            def _():
-                remote(eb.at[j], bz.at[slot, i // 2], b_send, b_recv.at[slot], lat, lon).start()
-
-            @pl.when(here)
-            def _():
-                pltpu.make_async_copy(eb.at[j], bz.at[slot, i // 2], b_recv.at[slot]).start()
+        if q == 1:
+            pl.when(jnp.logical_not(outward))(edge_sends)
 
     def evaluate(z):
         return from_modes(z, table.at[EVALUATE : EVALUATE + 384], table.at[EVALUATE + 384 : TO_COEFS])
@@ -486,22 +498,14 @@
 
     @pl.when(polar)
     def _():
+        load_forward.wait()
+        send_values(0, grid[0:PAIRS, 8:24, :])
         grid[0:PAIRS, 7:8, :] = jnp.zeros((PAIRS, 1, WIDE), F32)
         grid[0:PAIRS, 24:25, :] = jnp.zeros((PAIRS, 1, WIDE), F32)
         full_tendency()
-        load_forward.wait()
-        probe = grid[0:PAIRS, 8:24, :].reshape(PAIRS * ROWS, WIDE)
-        change = tend[...].reshape(PAIRS * ROWS, WIDE)
-        y = to_modes(jnp.concatenate([probe, change], axis=0), table.at[FORWARD:EVALUATE])
-        y = y.reshape(2, FIELDS, LEV, 2, 8, RANK)
-        for q in range(2):
-            blocks = [
-                jnp.concatenate([y[q, f, l, h] for f in range(FIELDS) for h in range(2)], axis=0)
-                for l in range(LEV)
-            ]
-            for l, part in enumerate(pack(blocks)):
-                ybuf[:, q, l] = part.reshape(LANES, 8, RANK)
-        send_values()
+        send_values(1, tend[...])
+
+    edge_rows((REST + 4, REST + 11), slice(PAIRS, PAIRS + 2 * LEV), (8, 23))
 
     halo_arrival(NEAR, REST, 0).wait_recv()
     lane2 = lax.broadcasted_iota(jnp.int32, (1, 128), 1)
@@ -576,6 +580,7 @@
     both = jnp.concatenate([both, roll_blocks(both, -16), roll_blocks(both, -32)], axis=0)
     in_halo = jnp.logical_or(jnp.logical_and(lane128 >= 66, lane128 < 68), lane128 >= 126)
     grid[:, 8:24, 384:512] = jnp.where(in_halo, both, grid[:, 8:24, 384:512])
+    edge_rows((REST, REST + 7), slice(0, PAIRS), (9, 22))
     for s, near in enumerate((8, 23)):
         halo_out[REST + 7 * s + 6] = grid[0:PAIRS, near, 384:512]
     halo_copy(REST, 7, REST + 7 * slot_n, 1, nb, nl).start()
@@ -584,7 +589,6 @@
     @pl.when(polar)
     def _():
         own_rows(1)
-        edge_sends()
 
     halo_arrival(REST, BLOCKS, 1).wait_recv()
     edge_row = (7, 24)
@@ -709,19 +713,22 @@
     @pl.when(near_polar)
     def _():
         taken = evaluate(jnp.concatenate([bz[s, f] for s in range(2) for f in range(FIELDS)], axis=0))
-        for s, row in ((0, 0), (1, 15)):
-            weight = flip(s, -1.0) * edge_weights(s, taken[PAIRS * s : PAIRS * (s + 1), :])
-            less = ((0.5, -0.5)[s] * time_step) * grid[0:PAIRS, 8 + row, :] * weight
-            for f in range(FIELDS):
-                diag_out[f, :, row, :] = diag_out[f, :, row, :] - less[f * LEV : (f + 1) * LEV, :COLS]
+        for s, wanted in enumerate((above_polar, below_polar)):
+            @pl.when(wanted)
+            def _():
+                row = 15 * s
+                weight = flip(s, -1.0) * edge_weights(s, taken[PAIRS * s : PAIRS * (s + 1), :])
+                less = ((0.5, -0.5)[s] * time_step) * grid[0:PAIRS, 8 + row, :] * weight
+                for f in range(FIELDS):
+                    diag_out[f, :, row, :] = diag_out[f, :, row, :] - less[f * LEV : (f + 1) * LEV, :COLS]
 
     halo_arrival(0, BLOCKS, 0).wait_send()
 
     @pl.when(polar)
     def _():
-        all_y().wait_send()
         all_c().wait_send()
         for q in range(2):
+            all_y(q).wait_send()
             all_z(q).wait_send()
 
         @pl.when(edge_over)
@@ -735,8 +742,9 @@
 
 def hand_out(tan_in, diag_in, tan_out, diag_out, sem):
     copies = [
-        pltpu.make_async_copy(src, dst, sem.at[n])
+        pltpu.make_async_copy(src.at[f], dst.at[f], sem.at[n, f])
         for n, (src, dst) in enumerate(((tan_in, tan_out), (diag_in, diag_out)))
+        for f in range(FIELDS)
     ]
     for copy in copies:
         copy.start()
@@ -768,8 +776,8 @@
             vmem((PAIRS + 2 * LEV, 32, WIDE), F32),
             vmem((BLOCKS, 16, 128), F32),
             vmem((BLOCKS, 16, 128), F32),
-            vmem((LANES, 2, LEV - 1, 8, RANK), F32),
-            vmem((LANES, 2, LEV - 1, 8, RANK), F32),
+            vmem((2, LANES, LEV - 1, 8, RANK), F32),
+            vmem((2, LANES, LEV - 1, 8, RANK), F32),
             vmem((2, PAIRS, WIDE), F32),
             vmem((LANES, 16, RANK), F32),
             vmem((LANES, 16, RANK), F32),
@@ -780,11 +788,11 @@
             vmem((PAIRS, ROWS, WIDE), F32),
             vmem((PAIRS, ROWS, WIDE), F32),
             vmem((PAIRS, 32, WIDE), F32),
-            dma((12,)),
+            dma((8,)),
             dma,
             dma((2,)),
-            dma,
-            dma,
+            dma((2,)),
+            dma((2,)),
             dma,
             dma,
             dma((2,)),
@@ -802,7 +810,7 @@
         out_shape=(out, out),
         in_specs=[any_spec] * 2,
         out_specs=(any_spec, any_spec),
-        scratch_shapes=[dma((2,))],
+        scratch_shapes=[dma((2, FIELDS))],
         compiler_params=pltpu.CompilerParams(vmem_limit_bytes=2**20),
     )(*(pltpu.with_memory_space_constraint(x, pltpu.VMEM) for x in results))
 

time: 21.7 us -> 21.4 us (0.986)
    pallas_call x1, Pallas kernels: 20 us -> 19.7 us  [per_device(): pl.pallas_call(functools.partial(kernel, bands), out_shape=(held, held),...]
where the time goes in v14:
time: 21.4 us; the launch traced here: 21.3 us
  Pallas kernels  20.7 us (97%)
  between operations  0.64 us (3%)
    pallas_call x1, Pallas kernels, per_device(): pl.pallas_call(functools.partial(kernel, bands), out_shape=(held, held),...  19.7 us
    pallas_call x1, Pallas kernels, per_device(): pl.pallas_call(hand_out, out_shape=(out, out), in_specs=[any_spec] * 2, o...  1.03 us

profile of v14, /device:TPU:225, one launch (start us, length us, event | category | flops | bytes accessed | tf_op | source)
XLA Modules:
  0.0 21.3 jit_solution(13609187793276548952)
XLA Ops:
  0.6 19.7 %shard_map.95 = (f32[4,4,16,450]{3,2,1,0:T(8,128)S(1)}, f32[4,4,16,450]{3,2,1,0:T(8,128)S(1)}) custom-call(f32[4,4,16,450]{3,2,1,0:T(8,128)} %spread.1, f32[4,16,450]{2,1,0:T(8,128)} %east.1, f32[4,16,450]{2,1,0:T(8,128)} %north.1, s32[4,4,16]{2,1,0:T(4,128)} %rs.1, s32[4,4,450]{2,1,0:T(4,128)} %cs.1, s32[16]{0:T(128)} %cut.1, ...), custom_call_target="tpu_custom_call" | custom-call | flops 1000000000 | bytes 4000000 | tf_op jit(solution)/shard_map/pallas_call | solution.py:763
  20.3 1.0 %shard_map.96 = (f32[4,4,16,450]{3,2,1,0:T(8,128)}, f32[4,4,16,450]{3,2,1,0:T(8,128)}) custom-call(f32[4,4,16,450]{3,2,1,0:T(8,128)S(1)} %get-tuple-element.4.tan_in, f32[4,4,16,450]{3,2,1,0:T(8,128)S(1)} %get-tuple-element.5.diag_in), custom_call_target="tpu_custom_call" | custom-call | tf_op jit(solution)/shard_map/pallas_call | solution.py:808

commit v15 on v14

--- a/solution.py
+++ b/solution.py
@@ -28,6 +28,8 @@
 
 FORWARD, EVALUATE, TO_COEFS, FROM_COEFS, TABLE_ROWS = 0, 512, 1280, 2304, 3328
 NEAR, SIDES, REST, BLOCKS = 0, 8, 10, 24
+
+FAR_FIRST = (6, 2, 5, 3, 7, 1, 4)
 
 MESH = pl.DeviceIdType.MESH
 F32 = jnp.float32
@@ -239,29 +241,30 @@
     load_forward = load_table(FORWARD, EVALUATE, 6)
     load_others = load_table(EVALUATE, TABLE_ROWS, 7)
     load_part = load_table(EVALUATE, TO_COEFS, 7)
-    load_spread.start()
-    load_rows.start()
-    load_cols.start()
-
     barrier = pltpu.get_barrier_semaphore()
 
     def greet(lat, lon):
         pl.semaphore_signal(barrier, inc=1, device_id=(lat, lon), device_id_type=MESH)
+
+    @pl.when(polar)
+    def _():
+        for d in FAR_FIRST[:4]:
+            greet(b, plus(i, d))
 
     greet(nb, nl)
     greet(sb, sl)
     greet(b, west)
     greet(b, east_lane)
+    load_spread.start()
+    load_rows.start()
+    load_cols.start()
     pltpu.make_async_copy(east, winds_v.at[0], in_sem.at[3]).start()
     pltpu.make_async_copy(north, winds_v.at[1], in_sem.at[3]).start()
     load_metric.start()
 
     @pl.when(polar)
     def _():
-        @pl.loop(2, LANES - 1)
-        def _(d):
-            greet(b, plus(i, d))
-
+        greet(b, across)
         load_forward.start()
         load_cut.start()
 
@@ -343,8 +346,7 @@
         for l, part in enumerate(pack(blocks)):
             ybuf[q, :, l] = part.reshape(LANES, 8, RANK)
 
-        @pl.loop(1, LANES)
-        def _(d):
+        for d in FAR_FIRST:
             o = plus(i, d)
             remote(ybuf.at[q, o], yr.at[q, i], y_send.at[q], y_recv.at[q], b, o).start()
 
@@ -429,8 +431,7 @@
         if q == 1:
             pl.when(outward)(edge_sends)
 
-        @pl.loop(1, LANES)
-        def _(d):
+        for d in FAR_FIRST:
             z_copy(q, plus(i, d)).start()
 
         zr[q, i] = zbuf[q, i]
@@ -560,8 +561,7 @@
             for h in range(2):
                 cb[2 * f + h, 8:16, :] = ends[8 * h : 8 * h + 8, :]
 
-        @pl.loop(1, LANES)
-        def _(d):
+        for d in FAR_FIRST:
             c_copy(plus(i, d)).start()
 
         yc[i] = cb[i]
@@ -742,9 +742,8 @@
 
 def hand_out(tan_in, diag_in, tan_out, diag_out, sem):
     copies = [
-        pltpu.make_async_copy(src.at[f], dst.at[f], sem.at[n, f])
+        pltpu.make_async_copy(src, dst, sem.at[n])
         for n, (src, dst) in enumerate(((tan_in, tan_out), (diag_in, diag_out)))
-        for f in range(FIELDS)
     ]
     for copy in copies:
         copy.start()
@@ -810,7 +809,7 @@
         out_shape=(out, out),
         in_specs=[any_spec] * 2,
         out_specs=(any_spec, any_spec),
-        scratch_shapes=[dma((2, FIELDS))],
+        scratch_shapes=[dma((2,))],
         compiler_params=pltpu.CompilerParams(vmem_limit_bytes=2**20),
     )(*(pltpu.with_memory_space_constraint(x, pltpu.VMEM) for x in results))
 

time: 21.4 us -> 21.2 us (level)
  Pallas kernels: 20.7 us -> 20.4 us
    pallas_call x1, Pallas kernels: 19.7 us -> 19.4 us  [per_device(): pl.pallas_call(functools.partial(kernel, bands), out_shape=(held, held),...]
where the time goes in v15:
time: 21.2 us; the launch traced here: 21.1 us
  Pallas kernels  20.4 us (96%)
  between operations  0.64 us (3%)
    pallas_call x1, Pallas kernels, per_device(): pl.pallas_call(functools.partial(kernel, bands), out_shape=(held, held),...  19.4 us
    pallas_call x1, Pallas kernels, per_device(): pl.pallas_call(hand_out, out_shape=(out, out), in_specs=[any_spec] * 2, o...  0.99 us

profile of v15, /device:TPU:225, one launch (start us, length us, event | category | flops | bytes accessed | tf_op | source)
XLA Modules:
  0.0 21.1 jit_solution(8168595215787740633)
XLA Ops:
  0.6 19.4 %shard_map.95 = (f32[4,4,16,450]{3,2,1,0:T(8,128)S(1)}, f32[4,4,16,450]{3,2,1,0:T(8,128)S(1)}) custom-call(f32[4,4,16,450]{3,2,1,0:T(8,128)} %spread.1, f32[4,16,450]{2,1,0:T(8,128)} %east.1, f32[4,16,450]{2,1,0:T(8,128)} %north.1, s32[4,4,16]{2,1,0:T(4,128)} %rs.1, s32[4,4,450]{2,1,0:T(4,128)} %cs.1, s32[16]{0:T(128)} %cut.1, ...), custom_call_target="tpu_custom_call" | custom-call | flops 1000000000 | bytes 4000000 | tf_op jit(solution)/shard_map/pallas_call | solution.py:762
  20.1 1.0 %shard_map.96 = (f32[4,4,16,450]{3,2,1,0:T(8,128)}, f32[4,4,16,450]{3,2,1,0:T(8,128)}) custom-call(f32[4,4,16,450]{3,2,1,0:T(8,128)S(1)} %get-tuple-element.4.tan_in, f32[4,4,16,450]{3,2,1,0:T(8,128)S(1)} %get-tuple-element.5.diag_in), custom_call_target="tpu_custom_call" | custom-call | tf_op jit(solution)/shard_map/pallas_call | solution.py:807

commit v16 on v15

--- a/solution.py
+++ b/solution.py
@@ -387,35 +387,33 @@
         cutoff = jnp.zeros((8, 128), jnp.int32)
         for r in range(8):
             cutoff = jnp.where(row == r, cut_s[8 * own_half + r], cutoff)
-
+        keeps = []
+        for group in range(4):
+            wave = waves_of(group, lax.broadcasted_iota(jnp.int32, (8, 128), 1))
+            keep = jnp.where(wave > cutoff, 2.0 / (COLS * LANES), 0.0)
+            keeps.append(jnp.concatenate([keep] * LEV, axis=0))
         all_y(q).wait_recv()
+        levels = unpack([yr[q, :, l].reshape(LANES * 8, RANK) for l in range(LEV - 1)])
         if q == 1:
+            edge_row = jnp.where(row == 7 * own_half, 1.0, 0.0)
             all_c().wait_recv()
-
-        levels = unpack([yr[q, :, l].reshape(LANES * 8, RANK) for l in range(LEV - 1)])
-        lanes = []
-        for j in range(LANES):
-            y = [levels[l][8 * j : 8 * j + 8, :] for l in range(LEV)]
-            if q == 1:
-                ends = pltpu.roll(yc[j, 8:16, :], lax.rem(128 - 2 * LEV * (i // 2), 128), 1)
-                edge_rows = jnp.where(row == 7 * own_half, 1.0, 0.0)
-                y = [
-                    y[l]
-                    + ends[:, 2 * l : 2 * l + 1] * hm[0:1, :]
-                    + ends[:, 2 * l + 1 : 2 * l + 2] * hm[1:2, :]
-                    + edge_rows * yc[j, l : l + 1, :]
-                    for l in range(LEV)
-                ]
-            lanes.append(jnp.concatenate(y, axis=0))
+            ends = jnp.concatenate([yc[j, 8:16, :] for j in range(LANES)], axis=0)
+            ends = pltpu.roll(ends, lax.rem(128 - 2 * LEV * (i // 2), 128), 1)
+            levels = [
+                levels[l]
+                + ends[:, 2 * l : 2 * l + 1] * hm[0:1, :]
+                + ends[:, 2 * l + 1 : 2 * l + 2] * hm[1:2, :]
+                + jnp.concatenate([edge_row * yc[j, l : l + 1, :] for j in range(LANES)], axis=0)
+                for l in range(LEV)
+            ]
+        lanes = [
+            jnp.concatenate([levels[l][8 * j : 8 * j + 8, :] for l in range(LEV)], axis=0) for j in range(LANES)
+        ]
         coefs = [
             to_coefs(jnp.concatenate(pair, axis=1), table.at[TO_COEFS + 256 * group : TO_COEFS + 256 * (group + 1)])
             for group, pair in enumerate(over_lanes(lanes))
         ]
-        kept = []
-        for group, coef in enumerate(coefs):
-            wave = waves_of(group, lax.broadcasted_iota(jnp.int32, (8, 128), 1))
-            keep = jnp.where(wave > cutoff, 2.0 / (COLS * LANES), 0.0)
-            kept.append(coef * jnp.concatenate([keep] * LEV, axis=0))
+        kept = [coef * keep for coef, keep in zip(coefs, keeps)]
         backs = [
             from_coefs(coef, table.at[FROM_COEFS + 256 * group : FROM_COEFS + 256 * (group + 1)])
             for group, coef in enumerate(kept)
@@ -424,19 +422,23 @@
         zs = [z.reshape(LEV, 8, RANK) for z in to_lanes(pairs)]
         for l, part in enumerate(pack([jnp.concatenate([z[l] for z in zs], axis=0) for l in range(LEV)])):
             zbuf[q, :, l] = part.reshape(LANES, 8, RANK)
-        for j, z in enumerate(zs):
-            edge = jnp.where(own_half == 0, z[:, 0, :], z[:, 7, :])
-            eb[j] = edge if q == 0 else eb[j] + edge
+
+        def edges():
+            for j, z in enumerate(zs):
+                edge = jnp.where(own_half == 0, z[:, 0, :], z[:, 7, :])
+                eb[j] = edge if q == 0 else eb[j] + edge
+            if q == 1:
+                edge_sends()
 
         if q == 1:
-            pl.when(outward)(edge_sends)
-
+            pl.when(outward)(edges)
         for d in FAR_FIRST:
             z_copy(q, plus(i, d)).start()
-
+        if q == 1:
+            pl.when(jnp.logical_not(outward))(edges)
+        else:
+            edges()
         zr[q, i] = zbuf[q, i]
-        if q == 1:
-            pl.when(jnp.logical_not(outward))(edge_sends)
 
     def evaluate(z):
         return from_modes(z, table.at[EVALUATE : EVALUATE + 384], table.at[EVALUATE + 384 : TO_COEFS])
@@ -566,12 +568,6 @@
 
         yc[i] = cb[i]
 
-    @pl.when(polar)
-    def _():
-        load_cut.wait()
-        load_others.wait()
-        own_rows(0)
-
     from_west = roll(halo_in[SIDES], 126, 1)
     from_east = roll(halo_in[SIDES + 1], COLS - 384, 1)
     both = jnp.where(jnp.logical_and(lane2 >= 66, lane2 < 114), from_east, from_west)[None]
@@ -588,7 +584,9 @@
 
     @pl.when(polar)
     def _():
-        own_rows(1)
+        load_cut.wait()
+        load_others.wait()
+        own_rows(0)
 
     halo_arrival(REST, BLOCKS, 1).wait_recv()
     edge_row = (7, 24)
@@ -625,6 +623,10 @@
         t = -(wind(halo_in, s, 0) * along_x + wind(halo_in, s, 1) * along_y) - coupling * linked
         a = mid + time_step * (t + mixing * (up + down - 2.0 * mid))
         gy[0:PAIRS, edge_row[s], :] = flip(s, -1.0) * edge_weights(s, a)
+
+    @pl.when(polar)
+    def _():
+        own_rows(1)
 
     def row_weights(a, nw):
         return (

time: 21.2 us -> 22.1 us (1.042)
  the two profiles are of different devices: /device:TPU:225 before, /device:TPU:1 now
where the time goes in v16:
time: 22.1 us; the launch traced here: 22 us
  Pallas kernels  21.3 us (96%)
  between operations  0.64 us (3%)
    pallas_call x1, Pallas kernels, per_device(): pl.pallas_call(functools.partial(kernel, bands), out_shape=(held, held),...  20.3 us
    pallas_call x1, Pallas kernels, per_device(): pl.pallas_call(hand_out, out_shape=(out, out), in_specs=[any_spec] * 2, o...  0.99 us

profile of v16, /device:TPU:1, one launch (start us, length us, event | category | flops | bytes accessed | tf_op | source)
XLA Modules:
  0.0 22.0 jit_solution(11659696387428618743)
XLA Ops:
  0.6 20.3 %shard_map.95 = (f32[4,4,16,450]{3,2,1,0:T(8,128)S(1)}, f32[4,4,16,450]{3,2,1,0:T(8,128)S(1)}) custom-call(f32[4,4,16,450]{3,2,1,0:T(8,128)} %spread.1, f32[4,16,450]{2,1,0:T(8,128)} %east.1, f32[4,16,450]{2,1,0:T(8,128)} %north.1, s32[4,4,16]{2,1,0:T(4,128)} %rs.1, s32[4,4,450]{2,1,0:T(4,128)} %cs.1, s32[16]{0:T(128)} %cut.1, ...), custom_call_target="tpu_custom_call" | custom-call | flops 1000000000 | bytes 4000000 | tf_op jit(solution)/shard_map/pallas_call | solution.py:764
  21.0 1.0 %shard_map.96 = (f32[4,4,16,450]{3,2,1,0:T(8,128)}, f32[4,4,16,450]{3,2,1,0:T(8,128)}) custom-call(f32[4,4,16,450]{3,2,1,0:T(8,128)S(1)} %get-tuple-element.4.tan_in, f32[4,4,16,450]{3,2,1,0:T(8,128)S(1)} %get-tuple-element.5.diag_in), custom_call_target="tpu_custom_call" | custom-call | tf_op jit(solution)/shard_map/pallas_call | solution.py:809

commit v17 on v16

--- a/solution.py
+++ b/solution.py
@@ -588,6 +588,10 @@
         load_others.wait()
         own_rows(0)
 
+    @pl.when(jnp.logical_and(polar, b < bands // 2))
+    def _():
+        own_rows(1)
+
     halo_arrival(REST, BLOCKS, 1).wait_recv()
     edge_row = (7, 24)
     edge_probe = []
@@ -624,7 +628,7 @@
         a = mid + time_step * (t + mixing * (up + down - 2.0 * mid))
         gy[0:PAIRS, edge_row[s], :] = flip(s, -1.0) * edge_weights(s, a)
 
-    @pl.when(polar)
+    @pl.when(jnp.logical_and(polar, b >= bands // 2))
     def _():
         own_rows(1)
 

time: 22.1 us -> 21 us (0.950)
  Pallas kernels: 21.3 us -> 20.1 us
    pallas_call x1, Pallas kernels: 20.3 us -> 19.1 us  [per_device(): pl.pallas_call(functools.partial(kernel, bands), out_shape=(held, held),...]
where the time goes in v17:
time: 21 us; the launch traced here: 20.7 us
  Pallas kernels  20.1 us (96%)
  between operations  0.64 us (3%)
    pallas_call x1, Pallas kernels, per_device(): pl.pallas_call(functools.partial(kernel, bands), out_shape=(held, held),...  19.1 us
    pallas_call x1, Pallas kernels, per_device(): pl.pallas_call(hand_out, out_shape=(out, out), in_specs=[any_spec] * 2, o...  0.99 us

profile of v17, /device:TPU:1, one launch (start us, length us, event | category | flops | bytes accessed | tf_op | source)
XLA Modules:
  0.0 20.7 jit_solution(3400571717796134560)
XLA Ops:
  0.6 19.1 %shard_map.95 = (f32[4,4,16,450]{3,2,1,0:T(8,128)S(1)}, f32[4,4,16,450]{3,2,1,0:T(8,128)S(1)}) custom-call(f32[4,4,16,450]{3,2,1,0:T(8,128)} %spread.1, f32[4,16,450]{2,1,0:T(8,128)} %east.1, f32[4,16,450]{2,1,0:T(8,128)} %north.1, s32[4,4,16]{2,1,0:T(4,128)} %rs.1, s32[4,4,450]{2,1,0:T(4,128)} %cs.1, s32[16]{0:T(128)} %cut.1, ...), custom_call_target="tpu_custom_call" | custom-call | flops 1000000000 | bytes 4000000 | tf_op jit(solution)/shard_map/pallas_call | solution.py:768
  19.7 1.0 %shard_map.96 = (f32[4,4,16,450]{3,2,1,0:T(8,128)}, f32[4,4,16,450]{3,2,1,0:T(8,128)}) custom-call(f32[4,4,16,450]{3,2,1,0:T(8,128)S(1)} %get-tuple-element.4.tan_in, f32[4,4,16,450]{3,2,1,0:T(8,128)S(1)} %get-tuple-element.5.diag_in), custom_call_target="tpu_custom_call" | custom-call | tf_op jit(solution)/shard_map/pallas_call | solution.py:813

commit v18 on v17

--- a/solution.py
+++ b/solution.py
@@ -246,13 +246,14 @@
     def greet(lat, lon):
         pl.semaphore_signal(barrier, inc=1, device_id=(lat, lon), device_id_type=MESH)
 
+    greet(nb, nl)
+    greet(sb, sl)
+
     @pl.when(polar)
     def _():
         for d in FAR_FIRST[:4]:
             greet(b, plus(i, d))
 
-    greet(nb, nl)
-    greet(sb, sl)
     greet(b, west)
     greet(b, east_lane)
     load_spread.start()
@@ -327,8 +328,16 @@
             halo_out.at[start:stop], halo_in.at[start:stop], halo_send, halo_recv.at[which], b, west
         )
 
-    halo_copy(NEAR, 4, NEAR + 4 * slot_n, 0, nb, nl).start()
+    @pl.when(b < bands // 2)
+    def _():
+        halo_copy(NEAR, 4, NEAR + 4 * slot_n, 0, nb, nl).start()
+
     halo_copy(NEAR + 4, 4, NEAR + 4 * slot_s, 0, sb, sl).start()
+
+    @pl.when(b >= bands // 2)
+    def _():
+        halo_copy(NEAR, 4, NEAR + 4 * slot_n, 0, nb, nl).start()
+
     halo_copy(SIDES, 1, SIDES + 1, 0, b, west).start()
     halo_copy(SIDES + 1, 1, SIDES, 0, b, east_lane).start()
 
@@ -710,23 +719,15 @@
     for s, wanted in enumerate((above_polar, below_polar)):
         @pl.when(wanted)
         def _():
+            row = 15 * s
+            north_wind = wind(halo_in, s, 1)
+            factor = ((0.5, -0.5)[s] * time_step) * grid[0:PAIRS, 8 + row, :] * flip(s, -1.0)
+            before = [diag_out[f, :, row, :] for f in range(FIELDS)]
             remote(bz.at[s], bz.at[s], b_send, b_recv.at[s], nb, nl).wait_recv()
-
-        @pl.when(jnp.logical_not(wanted))
-        def _():
-            bz[s] = jnp.zeros((FIELDS, LEV, RANK), F32)
-
-    @pl.when(near_polar)
-    def _():
-        taken = evaluate(jnp.concatenate([bz[s, f] for s in range(2) for f in range(FIELDS)], axis=0))
-        for s, wanted in enumerate((above_polar, below_polar)):
-            @pl.when(wanted)
-            def _():
-                row = 15 * s
-                weight = flip(s, -1.0) * edge_weights(s, taken[PAIRS * s : PAIRS * (s + 1), :])
-                less = ((0.5, -0.5)[s] * time_step) * grid[0:PAIRS, 8 + row, :] * weight
-                for f in range(FIELDS):
-                    diag_out[f, :, row, :] = diag_out[f, :, row, :] - less[f * LEV : (f + 1) * LEV, :COLS]
+            taken = evaluate(jnp.concatenate([bz[s, f] for f in range(FIELDS)], axis=0))
+            more = factor * (north_wind * taken + coupling * row_link(taken))
+            for f in range(FIELDS):
+                diag_out[f, :, row, :] = before[f] + more[f * LEV : (f + 1) * LEV, :COLS]
 
     halo_arrival(0, BLOCKS, 0).wait_send()
 

time: 21 us -> 21 us (level)
  no operation moved by 1% of the time
where the time goes in v18:
time: 21 us; the launch traced here: 20.7 us
  Pallas kernels  20.1 us (96%)
  between operations  0.64 us (3%)
    pallas_call x1, Pallas kernels, per_device(): pl.pallas_call(functools.partial(kernel, bands), out_shape=(held, held),...  19.1 us
    pallas_call x1, Pallas kernels, per_device(): pl.pallas_call(hand_out, out_shape=(out, out), in_specs=[any_spec] * 2, o...  0.99 us

profile of v18, /device:TPU:1, one launch (start us, length us, event | category | flops | bytes accessed | tf_op | source)
XLA Modules:
  0.0 20.7 jit_solution(12055081174294340361)
XLA Ops:
  0.6 19.1 %shard_map.95 = (f32[4,4,16,450]{3,2,1,0:T(8,128)S(1)}, f32[4,4,16,450]{3,2,1,0:T(8,128)S(1)}) custom-call(f32[4,4,16,450]{3,2,1,0:T(8,128)} %spread.1, f32[4,16,450]{2,1,0:T(8,128)} %east.1, f32[4,16,450]{2,1,0:T(8,128)} %north.1, s32[4,4,16]{2,1,0:T(4,128)} %rs.1, s32[4,4,450]{2,1,0:T(4,128)} %cs.1, s32[16]{0:T(128)} %cut.1, ...), custom_call_target="tpu_custom_call" | custom-call | flops 1000000000 | bytes 4000000 | tf_op jit(solution)/shard_map/pallas_call | solution.py:769
  19.7 1.0 %shard_map.96 = (f32[4,4,16,450]{3,2,1,0:T(8,128)}, f32[4,4,16,450]{3,2,1,0:T(8,128)}) custom-call(f32[4,4,16,450]{3,2,1,0:T(8,128)S(1)} %get-tuple-element.4.tan_in, f32[4,4,16,450]{3,2,1,0:T(8,128)S(1)} %get-tuple-element.5.diag_in), custom_call_target="tpu_custom_call" | custom-call | tf_op jit(solution)/shard_map/pallas_call | solution.py:814

commit v19 on v18

--- a/solution.py
+++ b/solution.py
@@ -484,7 +484,7 @@
         return out
 
     def full_tendency():
-        @pl.loop(0, LEV)
+        @pl.loop(0, LEV, unroll=True)
         def _(l):
             for h in (8, 16):
                 half = jnp.concatenate([hm[h : h + 8, :]] * 4, axis=1)
@@ -498,7 +498,7 @@
         def at(n, r):
             return jnp.where(lane < 2, grid[n, r : r + 8, 0:128], grid[n, r : r + 8, 384:512])
 
-        @pl.loop(0, LEV)
+        @pl.loop(0, LEV, unroll=True)
         def _(l):
             for h in (8, 16):
                 for f, t in enumerate(tendency_rows(h, l, at, hm[h : h + 8, :])):
@@ -678,7 +678,7 @@
 
     @pl.when(jnp.logical_not(polar))
     def _():
-        @pl.loop(0, LEV)
+        @pl.loop(0, LEV, unroll=True)
         def _(l):
             for h in (8, 16):
                 a = []
@@ -689,7 +689,7 @@
                     adj[n, rows, :] = a[f]
                 put_weights(l, h, a)
 
-    @pl.loop(0, LEV)
+    @pl.loop(0, LEV, unroll=True)
     def _(l):
         lo = jnp.maximum(l - 1, 0)
         hi = jnp.minimum(l + 1, LEV - 1)

time: 21 us -> 21 us (level)
  no operation moved by 1% of the time
where the time goes in v19:
time: 21 us; the launch traced here: 20.8 us
  Pallas kernels  20.1 us (96%)
  between operations  0.64 us (3%)
    pallas_call x1, Pallas kernels, per_device(): pl.pallas_call(functools.partial(kernel, bands), out_shape=(held, held),...  19.1 us
    pallas_call x1, Pallas kernels, per_device(): pl.pallas_call(hand_out, out_shape=(out, out), in_specs=[any_spec] * 2, o...  0.99 us

profile of v19, /device:TPU:1, one launch (start us, length us, event | category | flops | bytes accessed | tf_op | source)
XLA Modules:
  0.0 20.8 jit_solution(2979362617640778611)
XLA Ops:
  0.6 19.1 %shard_map.95 = (f32[4,4,16,450]{3,2,1,0:T(8,128)S(1)}, f32[4,4,16,450]{3,2,1,0:T(8,128)S(1)}) custom-call(f32[4,4,16,450]{3,2,1,0:T(8,128)} %spread.1, f32[4,16,450]{2,1,0:T(8,128)} %east.1, f32[4,16,450]{2,1,0:T(8,128)} %north.1, s32[4,4,16]{2,1,0:T(4,128)} %rs.1, s32[4,4,450]{2,1,0:T(4,128)} %cs.1, s32[16]{0:T(128)} %cut.1, ...), custom_call_target="tpu_custom_call" | custom-call | flops 1000000000 | bytes 4000000 | tf_op jit(solution)/shard_map/pallas_call | solution.py:769
  19.8 1.0 %shard_map.96 = (f32[4,4,16,450]{3,2,1,0:T(8,128)}, f32[4,4,16,450]{3,2,1,0:T(8,128)}) custom-call(f32[4,4,16,450]{3,2,1,0:T(8,128)S(1)} %get-tuple-element.4.tan_in, f32[4,4,16,450]{3,2,1,0:T(8,128)S(1)} %get-tuple-element.5.diag_in), custom_call_target="tpu_custom_call" | custom-call | tf_op jit(solution)/shard_map/pallas_call | solution.py:814

commit v20 on v19

--- a/solution.py
+++ b/solution.py
@@ -30,6 +30,7 @@
 NEAR, SIDES, REST, BLOCKS = 0, 8, 10, 24
 
 FAR_FIRST = (6, 2, 5, 3, 7, 1, 4)
+ANSWERS = (0, 4, 1, 3, 2, 7, 5, 6)
 
 MESH = pl.DeviceIdType.MESH
 F32 = jnp.float32
@@ -222,9 +223,7 @@
     own_half = lax.rem(i, 2)
     edge_over = jnp.where(own_half == 0, is_north, is_south)
     over_pole = (is_north, is_south)
-    outward = jnp.logical_or(
-        jnp.logical_and(b == caps - 1, own_half == 1), jnp.logical_and(b == bands - caps, own_half == 0)
-    )
+    outward = jnp.logical_and(b == bands - caps, own_half == 0)
 
     def plus(lane, d):
         return lax.rem(lane + d, LANES)
@@ -377,19 +376,26 @@
         slot = jnp.where(own_half == 0, slot_n, slot_s)
         lat = jnp.where(own_half == 0, nb, sb)
 
-        @pl.loop(0, LANES)
-        def _(d):
-            j = plus(i, d)
-            lon = jnp.where(edge_over, plus(j, LANES // 2), j)
-            here = jnp.logical_and(edge_over, lon == i)
-
-            @pl.when(jnp.logical_not(here))
-            def _():
-                remote(eb.at[j], bz.at[slot, i // 2], b_send, b_recv.at[slot], lat, lon).start()
-
-            @pl.when(here)
-            def _():
-                pltpu.make_async_copy(eb.at[j], bz.at[slot, i // 2], b_recv.at[slot]).start()
+        def away(j, lon):
+            remote(eb.at[j], bz.at[slot, i // 2], b_send, b_recv.at[slot], lat, lon).start()
+
+        @pl.when(jnp.logical_not(edge_over))
+        def _():
+            for j in ANSWERS:
+                away(j, j)
+
+        @pl.when(edge_over)
+        def _():
+            for j in ANSWERS:
+                lon = (j + LANES // 2) % LANES
+
+                @pl.when(i != lon)
+                def _():
+                    away(j, lon)
+
+                @pl.when(i == lon)
+                def _():
+                    pltpu.make_async_copy(eb.at[j], bz.at[slot, i // 2], b_recv.at[slot]).start()
 
     def own_rows(q):
         row = lax.broadcasted_iota(jnp.int32, (8, 128), 0)
@@ -441,8 +447,11 @@
 
         if q == 1:
             pl.when(outward)(edges)
-        for d in FAR_FIRST:
-            z_copy(q, plus(i, d)).start()
+        for j in ANSWERS:
+            @pl.when(i != j)
+            def _():
+                z_copy(q, j).start()
+
         if q == 1:
             pl.when(jnp.logical_not(outward))(edges)
         else:

time: 21 us -> 20.8 us (level)
  no operation moved by 1% of the time
where the time goes in v20:
time: 20.8 us; the launch traced here: 20.7 us
  Pallas kernels  20.1 us (97%)
  between operations  0.64 us (3%)
    pallas_call x1, Pallas kernels, per_device(): pl.pallas_call(functools.partial(kernel, bands), out_shape=(held, held),...  19.1 us
    pallas_call x1, Pallas kernels, per_device(): pl.pallas_call(hand_out, out_shape=(out, out), in_specs=[any_spec] * 2, o...  0.99 us

profile of v20, /device:TPU:1, one launch (start us, length us, event | category | flops | bytes accessed | tf_op | source)
XLA Modules:
  0.0 20.7 jit_solution(10752325345730445742)
XLA Ops:
  0.6 19.1 %shard_map.95 = (f32[4,4,16,450]{3,2,1,0:T(8,128)S(1)}, f32[4,4,16,450]{3,2,1,0:T(8,128)S(1)}) custom-call(f32[4,4,16,450]{3,2,1,0:T(8,128)} %spread.1, f32[4,16,450]{2,1,0:T(8,128)} %east.1, f32[4,16,450]{2,1,0:T(8,128)} %north.1, s32[4,4,16]{2,1,0:T(4,128)} %rs.1, s32[4,4,450]{2,1,0:T(4,128)} %cs.1, s32[16]{0:T(128)} %cut.1, ...), custom_call_target="tpu_custom_call" | custom-call | flops 1000000000 | bytes 4000000 | tf_op jit(solution)/shard_map/pallas_call | solution.py:778
  19.7 1.0 %shard_map.96 = (f32[4,4,16,450]{3,2,1,0:T(8,128)}, f32[4,4,16,450]{3,2,1,0:T(8,128)}) custom-call(f32[4,4,16,450]{3,2,1,0:T(8,128)S(1)} %get-tuple-element.4.tan_in, f32[4,4,16,450]{3,2,1,0:T(8,128)S(1)} %get-tuple-element.5.diag_in), custom_call_target="tpu_custom_call" | custom-call | tf_op jit(solution)/shard_map/pallas_call | solution.py:823

commit v21 on v20

--- a/solution.py
+++ b/solution.py
@@ -184,17 +184,6 @@
     return pltpu.roll(x, shift % x.shape[axis], axis)
 
 
-def roll_blocks(x, shift):
-    return roll(x.reshape(x.shape[0] * x.shape[1], x.shape[2]), shift, 1).reshape(x.shape)
-
-
-def fold(x):
-    while x.shape[0] > 1:
-        half = x.shape[0] // 2
-        x = x[:half] + roll_blocks(x[half:], 2 * half)
-    return x
-
-
 def kernel(
     bands, spread, east, north, rs, cs, cut, metric, table_in, tan_out, diag_out,
     spread_v, winds_v, rs_v, cs_v, cut_s, hm, table,
@@ -303,12 +292,16 @@
                     halo_out[start[s] + t // 2, 8 * (t % 2) : 8 * (t % 2) + 8, :] = values
 
     edge_rows((NEAR, NEAR + 4), slice(0, PAIRS), (8, 23))
-    lane128 = lax.broadcasted_iota(jnp.int32, (1, 1, 128), 2)
+    lane2 = lax.broadcasted_iota(jnp.int32, (1, 128), 1)
     for s, (start, shift) in enumerate(((0, 0), (384, COLS - 2 - 384))):
-        tile = grid[:, 8:24, start : start + 128]
-        tile = jnp.where(jnp.logical_and(lane128 >= shift, lane128 < shift + 2), tile, 0.0)
-        packed = fold(tile[:PAIRS]) + roll_blocks(fold(tile[PAIRS:]), 2 * PAIRS)
-        halo_out[SIDES + s] = roll_blocks(packed, -shift)[0]
+        ends = jnp.logical_and(lane2 >= shift, lane2 < shift + 2)
+        parts = [
+            roll(jnp.where(ends, grid[e, 8:24, start : start + 128], 0.0), 2 * e - shift, 1)
+            for e in range(PAIRS + 2 * LEV)
+        ]
+        while len(parts) > 1:
+            parts = [sum(parts[k : k + 2]) for k in range(0, len(parts), 2)]
+        halo_out[SIDES + s] = parts[0]
 
     pl.semaphore_wait(barrier, 4 + jnp.where(polar, LANES - 3, 0))
 
@@ -529,7 +522,6 @@
     edge_rows((REST + 4, REST + 11), slice(PAIRS, PAIRS + 2 * LEV), (8, 23))
 
     halo_arrival(NEAR, REST, 0).wait_recv()
-    lane2 = lax.broadcasted_iota(jnp.int32, (1, 128), 1)
     row16 = lax.broadcasted_iota(jnp.int32, (PAIRS, 1), 0)
     is_v = jnp.logical_and(row16 >= LEV, row16 < 2 * LEV)
     is_temp = jnp.logical_and(row16 >= 2 * LEV, row16 < 3 * LEV)
@@ -588,12 +580,10 @@
 
     from_west = roll(halo_in[SIDES], 126, 1)
     from_east = roll(halo_in[SIDES + 1], COLS - 384, 1)
-    both = jnp.where(jnp.logical_and(lane2 >= 66, lane2 < 114), from_east, from_west)[None]
-    for width in (2, 4, 8):
-        both = jnp.concatenate([both, roll_blocks(both, -width)], axis=0)
-    both = jnp.concatenate([both, roll_blocks(both, -16), roll_blocks(both, -32)], axis=0)
-    in_halo = jnp.logical_or(jnp.logical_and(lane128 >= 66, lane128 < 68), lane128 >= 126)
-    grid[:, 8:24, 384:512] = jnp.where(in_halo, both, grid[:, 8:24, 384:512])
+    both = jnp.where(jnp.logical_and(lane2 >= 66, lane2 < 114), from_east, from_west)
+    in_halo = jnp.logical_or(jnp.logical_and(lane2 >= 66, lane2 < 68), lane2 >= 126)
+    for e in range(PAIRS + 2 * LEV):
+        grid[e, 8:24, 384:512] = jnp.where(in_halo, roll(both, -2 * e, 1), grid[e, 8:24, 384:512])
     edge_rows((REST, REST + 7), slice(0, PAIRS), (9, 22))
     for s, near in enumerate((8, 23)):
         halo_out[REST + 7 * s + 6] = grid[0:PAIRS, near, 384:512]

time: 20.8 us -> 21.2 us (1.019)
  Pallas kernels: 20.1 us -> 20.5 us
    pallas_call x1, Pallas kernels: 19.1 us -> 19.5 us  [per_device(): pl.pallas_call(functools.partial(kernel, bands), out_shape=(held, held),...]
where the time goes in v21:
time: 21.2 us; the launch traced here: 21.1 us
  Pallas kernels  20.5 us (97%)
  between operations  0.64 us (3%)
    pallas_call x1, Pallas kernels, per_device(): pl.pallas_call(functools.partial(kernel, bands), out_shape=(held, held),...  19.5 us
    pallas_call x1, Pallas kernels, per_device(): pl.pallas_call(hand_out, out_shape=(out, out), in_specs=[any_spec] * 2, o...  0.99 us

profile of v21, /device:TPU:1, one launch (start us, length us, event | category | flops | bytes accessed | tf_op | source)
XLA Modules:
  0.0 21.1 jit_solution(13389705974867552823)
XLA Ops:
  0.6 19.5 %shard_map.95 = (f32[4,4,16,450]{3,2,1,0:T(8,128)S(1)}, f32[4,4,16,450]{3,2,1,0:T(8,128)S(1)}) custom-call(f32[4,4,16,450]{3,2,1,0:T(8,128)} %spread.1, f32[4,16,450]{2,1,0:T(8,128)} %east.1, f32[4,16,450]{2,1,0:T(8,128)} %north.1, s32[4,4,16]{2,1,0:T(4,128)} %rs.1, s32[4,4,450]{2,1,0:T(4,128)} %cs.1, s32[16]{0:T(128)} %cut.1, ...), custom_call_target="tpu_custom_call" | custom-call | flops 1000000000 | bytes 4000000 | tf_op jit(solution)/shard_map/pallas_call | solution.py:768
  20.1 1.0 %shard_map.96 = (f32[4,4,16,450]{3,2,1,0:T(8,128)}, f32[4,4,16,450]{3,2,1,0:T(8,128)}) custom-call(f32[4,4,16,450]{3,2,1,0:T(8,128)S(1)} %get-tuple-element.4.tan_in, f32[4,4,16,450]{3,2,1,0:T(8,128)S(1)} %get-tuple-element.5.diag_in), custom_call_target="tpu_custom_call" | custom-call | tf_op jit(solution)/shard_map/pallas_call | solution.py:813

commit v22 on v21

--- a/solution.py
+++ b/solution.py
@@ -196,6 +196,7 @@
     caps = POLAR // ROWS
     is_north = b == 0
     is_south = b == bands - 1
+    northern = b < bands // 2
     polar = jnp.logical_or(b < caps, b >= bands - caps)
     above_polar = jnp.logical_or(b <= caps, is_south)
     below_polar = jnp.logical_or(b >= bands - caps - 1, is_north)
@@ -303,42 +304,51 @@
             parts = [sum(parts[k : k + 2]) for k in range(0, len(parts), 2)]
         halo_out[SIDES + s] = parts[0]
 
-    pl.semaphore_wait(barrier, 4 + jnp.where(polar, LANES - 3, 0))
-
-    def remote(src, dst, send, recv, lat, lon):
-        return pltpu.make_async_remote_copy(
-            src_ref=src, dst_ref=dst, send_sem=send, recv_sem=recv, device_id=(lat, lon), device_id_type=MESH
-        )
-
-    def halo_copy(start, count, to, which, lat, lon):
-        return remote(
-            halo_out.at[start : start + count], halo_in.at[pl.ds(to, count)], halo_send, halo_recv.at[which], lat, lon
-        )
-
-    def halo_arrival(start, stop, which):
-        return remote(
-            halo_out.at[start:stop], halo_in.at[start:stop], halo_send, halo_recv.at[which], b, west
-        )
-
-    @pl.when(b < bands // 2)
-    def _():
-        halo_copy(NEAR, 4, NEAR + 4 * slot_n, 0, nb, nl).start()
-
-    halo_copy(NEAR + 4, 4, NEAR + 4 * slot_s, 0, sb, sl).start()
-
-    @pl.when(b >= bands // 2)
-    def _():
-        halo_copy(NEAR, 4, NEAR + 4 * slot_n, 0, nb, nl).start()
-
-    halo_copy(SIDES, 1, SIDES + 1, 0, b, west).start()
-    halo_copy(SIDES + 1, 1, SIDES, 0, b, east_lane).start()
-
-    others = pl.ds(0, LANES - 1)
-
-    def all_y(q):
-        return remote(ybuf.at[q, others], yr.at[q, others], y_send.at[q], y_recv.at[q], b, west)
-
-    def send_values(q, x):
+    def tendency_rows(h, l, at, half):
+        lo = jnp.maximum(l - 1, 0)
+        hi = jnp.minimum(l + 1, LEV - 1)
+        ew = at(PAIRS + l, h)
+        nw = at(PAIRS + LEV + l, h)
+        mids, along_x, along_y = [], [], []
+        for f in range(FIELDS):
+            mid = at(f * LEV + l, h)
+            mids.append(mid)
+            along_x.append(half * (roll(mid, -1, 1) - roll(mid, 1, 1)))
+            along_y.append(0.5 * (at(f * LEV + l, h + 1) - at(f * LEV + l, h - 1)))
+        linked = (along_x[2], along_y[2], along_x[0] + along_y[1], None)
+        out = []
+        for f in range(FIELDS):
+            mixed = at(f * LEV + lo, h) + at(f * LEV + hi, h) - 2.0 * mids[f]
+            t = -(ew * along_x[f] + nw * along_y[f]) + mixing * mixed
+            if linked[f] is not None:
+                t = t - coupling * linked[f]
+            out.append(time_step * t)
+        return out
+
+    def full_tendency():
+        @pl.loop(0, LEV, unroll=True)
+        def _(l):
+            for h in (8, 16):
+                half = jnp.concatenate([hm[h : h + 8, :]] * 4, axis=1)
+                for f, t in enumerate(tendency_rows(h, l, lambda n, r: grid[n, r : r + 8, :], half)):
+                    tend[f * LEV + l, h - 8 : h, :] = t
+
+    def side_tendency():
+        lane = lax.broadcasted_iota(jnp.int32, (1, 128), 1)
+        late = jnp.logical_or(jnp.logical_or(lane == 65, lane == 66), lane == 127)
+
+        def at(n, r):
+            return jnp.where(lane < 2, grid[n, r : r + 8, 0:128], grid[n, r : r + 8, 384:512])
+
+        @pl.loop(0, LEV, unroll=True)
+        def _(l):
+            for h in (8, 16):
+                for f, t in enumerate(tendency_rows(h, l, at, hm[h : h + 8, :])):
+                    n, rows = f * LEV + l, slice(h - 8, h)
+                    tend[n, rows, 0:128] = jnp.where(lane == 0, t, tend[n, rows, 0:128])
+                    tend[n, rows, 384:512] = jnp.where(late, t, tend[n, rows, 384:512])
+
+    def values(q, x):
         y = to_modes(x.reshape(PAIRS * ROWS, WIDE), table.at[FORWARD:EVALUATE])
         y = y.reshape(FIELDS, LEV, 2, 8, RANK)
         blocks = [
@@ -347,6 +357,59 @@
         for l, part in enumerate(pack(blocks)):
             ybuf[q, :, l] = part.reshape(LANES, 8, RANK)
 
+    def probe_values():
+        values(0, grid[0:PAIRS, 8:24, :])
+
+    def local_tendency_values():
+        grid[0:PAIRS, 7:8, :] = jnp.zeros((PAIRS, 1, WIDE), F32)
+        grid[0:PAIRS, 24:25, :] = jnp.zeros((PAIRS, 1, WIDE), F32)
+        full_tendency()
+        values(1, tend[...])
+
+    load_metric.wait()
+
+    @pl.when(jnp.logical_and(polar, northern))
+    def _():
+        load_forward.wait()
+        probe_values()
+        local_tendency_values()
+
+    pl.semaphore_wait(barrier, 4 + jnp.where(polar, LANES - 3, 0))
+
+    def remote(src, dst, send, recv, lat, lon):
+        return pltpu.make_async_remote_copy(
+            src_ref=src, dst_ref=dst, send_sem=send, recv_sem=recv, device_id=(lat, lon), device_id_type=MESH
+        )
+
+    def halo_copy(start, count, to, which, lat, lon):
+        return remote(
+            halo_out.at[start : start + count], halo_in.at[pl.ds(to, count)], halo_send, halo_recv.at[which], lat, lon
+        )
+
+    def halo_arrival(start, stop, which):
+        return remote(
+            halo_out.at[start:stop], halo_in.at[start:stop], halo_send, halo_recv.at[which], b, west
+        )
+
+    @pl.when(northern)
+    def _():
+        halo_copy(NEAR, 4, NEAR + 4 * slot_n, 0, nb, nl).start()
+
+    halo_copy(NEAR + 4, 4, NEAR + 4 * slot_s, 0, sb, sl).start()
+
+    @pl.when(jnp.logical_not(northern))
+    def _():
+        halo_copy(NEAR, 4, NEAR + 4 * slot_n, 0, nb, nl).start()
+
+    halo_copy(SIDES, 1, SIDES + 1, 0, b, west).start()
+    halo_copy(SIDES + 1, 1, SIDES, 0, b, east_lane).start()
+
+    others = pl.ds(0, LANES - 1)
+
+    def all_y(q):
+        return remote(ybuf.at[q, others], yr.at[q, others], y_send.at[q], y_recv.at[q], b, west)
+
+    def send_values(q):
         for d in FAR_FIRST:
             o = plus(i, d)
             remote(ybuf.at[q, o], yr.at[q, i], y_send.at[q], y_recv.at[q], b, o).start()
@@ -464,60 +527,19 @@
         out = evaluate(z)
         return [[out[8 * (LEV * f + l) : 8 * (LEV * f + l + 1), :] for l in range(LEV)] for f in range(FIELDS)]
 
-    def tendency_rows(h, l, at, half):
-        lo = jnp.maximum(l - 1, 0)
-        hi = jnp.minimum(l + 1, LEV - 1)
-        ew = at(PAIRS + l, h)
-        nw = at(PAIRS + LEV + l, h)
-        mids, along_x, along_y = [], [], []
-        for f in range(FIELDS):
-            mid = at(f * LEV + l, h)
-            mids.append(mid)
-            along_x.append(half * (roll(mid, -1, 1) - roll(mid, 1, 1)))
-            along_y.append(0.5 * (at(f * LEV + l, h + 1) - at(f * LEV + l, h - 1)))
-        linked = (along_x[2], along_y[2], along_x[0] + along_y[1], None)
-        out = []
-        for f in range(FIELDS):
-            mixed = at(f * LEV + lo, h) + at(f * LEV + hi, h) - 2.0 * mids[f]
-            t = -(ew * along_x[f] + nw * along_y[f]) + mixing * mixed
-            if linked[f] is not None:
-                t = t - coupling * linked[f]
-            out.append(time_step * t)
-        return out
-
-    def full_tendency():
-        @pl.loop(0, LEV, unroll=True)
-        def _(l):
-            for h in (8, 16):
-                half = jnp.concatenate([hm[h : h + 8, :]] * 4, axis=1)
-                for f, t in enumerate(tendency_rows(h, l, lambda n, r: grid[n, r : r + 8, :], half)):
-                    tend[f * LEV + l, h - 8 : h, :] = t
-
-    def side_tendency():
-        lane = lax.broadcasted_iota(jnp.int32, (1, 128), 1)
-        late = jnp.logical_or(jnp.logical_or(lane == 65, lane == 66), lane == 127)
-
-        def at(n, r):
-            return jnp.where(lane < 2, grid[n, r : r + 8, 0:128], grid[n, r : r + 8, 384:512])
-
-        @pl.loop(0, LEV, unroll=True)
-        def _(l):
-            for h in (8, 16):
-                for f, t in enumerate(tendency_rows(h, l, at, hm[h : h + 8, :])):
-                    n, rows = f * LEV + l, slice(h - 8, h)
-                    tend[n, rows, 0:128] = jnp.where(lane == 0, t, tend[n, rows, 0:128])
-                    tend[n, rows, 384:512] = jnp.where(late, t, tend[n, rows, 384:512])
-
-    load_metric.wait()
-
-    @pl.when(polar)
+
+    @pl.when(jnp.logical_and(polar, northern))
+    def _():
+        send_values(0)
+        send_values(1)
+
+    @pl.when(jnp.logical_and(polar, jnp.logical_not(northern)))
     def _():
         load_forward.wait()
-        send_values(0, grid[0:PAIRS, 8:24, :])
-        grid[0:PAIRS, 7:8, :] = jnp.zeros((PAIRS, 1, WIDE), F32)
-        grid[0:PAIRS, 24:25, :] = jnp.zeros((PAIRS, 1, WIDE), F32)
-        full_tendency()
-        send_values(1, tend[...])
+        probe_values()
+        send_values(0)
+        local_tendency_values()
+        send_values(1)
 
     edge_rows((REST + 4, REST + 11), slice(PAIRS, PAIRS + 2 * LEV), (8, 23))
 
@@ -596,7 +618,7 @@
         load_others.wait()
         own_rows(0)
 
-    @pl.when(jnp.logical_and(polar, b < bands // 2))
+    @pl.when(jnp.logical_and(polar, northern))
     def _():
         own_rows(1)
 
@@ -636,7 +658,7 @@
         a = mid + time_step * (t + mixing * (up + down - 2.0 * mid))
         gy[0:PAIRS, edge_row[s], :] = flip(s, -1.0) * edge_weights(s, a)
 
-    @pl.when(jnp.logical_and(polar, b >= bands // 2))
+    @pl.when(jnp.logical_and(polar, jnp.logical_not(northern)))
     def _():
         own_rows(1)
 

time: 21.2 us -> 21.7 us (1.024)
  Pallas kernels: 20.5 us -> 21 us
    pallas_call x1, Pallas kernels: 19.5 us -> 20 us  [per_device(): pl.pallas_call(functools.partial(kernel, bands), out_shape=(held, held),...]
where the time goes in v22:
time: 21.7 us; the launch traced here: 21.6 us
  Pallas kernels  21 us (97%)
  between operations  0.64 us (3%)
    pallas_call x1, Pallas kernels, per_device(): pl.pallas_call(functools.partial(kernel, bands), out_shape=(held, held),...  20 us
    pallas_call x1, Pallas kernels, per_device(): pl.pallas_call(hand_out, out_shape=(out, out), in_specs=[any_spec] * 2, o...  0.99 us

profile of v22, /device:TPU:1, one launch (start us, length us, event | category | flops | bytes accessed | tf_op | source)
XLA Modules:
  0.0 21.6 jit_solution(5790505355260644585)
XLA Ops:
  0.6 20.0 %shard_map.95 = (f32[4,4,16,450]{3,2,1,0:T(8,128)S(1)}, f32[4,4,16,450]{3,2,1,0:T(8,128)S(1)}) custom-call(f32[4,4,16,450]{3,2,1,0:T(8,128)} %spread.1, f32[4,16,450]{2,1,0:T(8,128)} %east.1, f32[4,16,450]{2,1,0:T(8,128)} %north.1, s32[4,4,16]{2,1,0:T(4,128)} %rs.1, s32[4,4,450]{2,1,0:T(4,128)} %cs.1, s32[16]{0:T(128)} %cut.1, ...), custom_call_target="tpu_custom_call" | custom-call | flops 1000000000 | bytes 4000000 | tf_op jit(solution)/shard_map/pallas_call | solution.py:790
  20.6 1.0 %shard_map.96 = (f32[4,4,16,450]{3,2,1,0:T(8,128)}, f32[4,4,16,450]{3,2,1,0:T(8,128)}) custom-call(f32[4,4,16,450]{3,2,1,0:T(8,128)S(1)} %get-tuple-element.4.tan_in, f32[4,4,16,450]{3,2,1,0:T(8,128)S(1)} %get-tuple-element.5.diag_in), custom_call_target="tpu_custom_call" | custom-call | tf_op jit(solution)/shard_map/pallas_call | solution.py:835

commit v23 on v22

--- a/solution.py
+++ b/solution.py
@@ -531,7 +531,6 @@
     @pl.when(jnp.logical_and(polar, northern))
     def _():
         send_values(0)
-        send_values(1)
 
     @pl.when(jnp.logical_and(polar, jnp.logical_not(northern)))
     def _():
@@ -599,6 +598,10 @@
             c_copy(plus(i, d)).start()
 
         yc[i] = cb[i]
+
+    @pl.when(jnp.logical_and(polar, northern))
+    def _():
+        send_values(1)
 
     from_west = roll(halo_in[SIDES], 126, 1)
     from_east = roll(halo_in[SIDES + 1], COLS - 384, 1)

time: 21.7 us -> 22.5 us (1.037)
  Pallas kernels: 21 us -> 21.8 us
    pallas_call x1, Pallas kernels: 20 us -> 20.8 us  [per_device(): pl.pallas_call(functools.partial(kernel, bands), out_shape=(held, held),...]
where the time goes in v23:
time: 22.5 us; the launch traced here: 22.4 us
  Pallas kernels  21.8 us (97%)
  between operations  0.64 us (3%)
    pallas_call x1, Pallas kernels, per_device(): pl.pallas_call(functools.partial(kernel, bands), out_shape=(held, held),...  20.8 us
    pallas_call x1, Pallas kernels, per_device(): pl.pallas_call(hand_out, out_shape=(out, out), in_specs=[any_spec] * 2, o...  0.99 us

profile of v23, /device:TPU:1, one launch (start us, length us, event | category | flops | bytes accessed | tf_op | source)
XLA Modules:
  0.0 22.4 jit_solution(14000377008252739725)
XLA Ops:
  0.6 20.8 %shard_map.95 = (f32[4,4,16,450]{3,2,1,0:T(8,128)S(1)}, f32[4,4,16,450]{3,2,1,0:T(8,128)S(1)}) custom-call(f32[4,4,16,450]{3,2,1,0:T(8,128)} %spread.1, f32[4,16,450]{2,1,0:T(8,128)} %east.1, f32[4,16,450]{2,1,0:T(8,128)} %north.1, s32[4,4,16]{2,1,0:T(4,128)} %rs.1, s32[4,4,450]{2,1,0:T(4,128)} %cs.1, s32[16]{0:T(128)} %cut.1, ...), custom_call_target="tpu_custom_call" | custom-call | flops 1000000000 | bytes 4000000 | tf_op jit(solution)/shard_map/pallas_call | solution.py:793
  21.4 1.0 %shard_map.96 = (f32[4,4,16,450]{3,2,1,0:T(8,128)}, f32[4,4,16,450]{3,2,1,0:T(8,128)}) custom-call(f32[4,4,16,450]{3,2,1,0:T(8,128)S(1)} %get-tuple-element.4.tan_in, f32[4,4,16,450]{3,2,1,0:T(8,128)S(1)} %get-tuple-element.5.diag_in), custom_call_target="tpu_custom_call" | custom-call | tf_op jit(solution)/shard_map/pallas_call | solution.py:838

commit v24 on v22

--- a/solution.py
+++ b/solution.py
@@ -372,7 +372,6 @@
     def _():
         load_forward.wait()
         probe_values()
-        local_tendency_values()
 
     pl.semaphore_wait(barrier, 4 + jnp.where(polar, LANES - 3, 0))
 
@@ -528,15 +527,13 @@
         return [[out[8 * (LEV * f + l) : 8 * (LEV * f + l + 1), :] for l in range(LEV)] for f in range(FIELDS)]
 
 
-    @pl.when(jnp.logical_and(polar, northern))
-    def _():
-        send_values(0)
-        send_values(1)
-
     @pl.when(jnp.logical_and(polar, jnp.logical_not(northern)))
     def _():
         load_forward.wait()
         probe_values()
+
+    @pl.when(polar)
+    def _():
         send_values(0)
         local_tendency_values()
         send_values(1)

time: 21.7 us -> 21.2 us (0.977)
  Pallas kernels: 21 us -> 20.4 us
    pallas_call x1, Pallas kernels: 20 us -> 19.4 us  [per_device(): pl.pallas_call(functools.partial(kernel, bands), out_shape=(held, held),...]
where the time goes in v24:
time: 21.2 us; the launch traced here: 21.1 us
  Pallas kernels  20.4 us (96%)
  between operations  0.64 us (3%)
    pallas_call x1, Pallas kernels, per_device(): pl.pallas_call(functools.partial(kernel, bands), out_shape=(held, held),...  19.4 us
    pallas_call x1, Pallas kernels, per_device(): pl.pallas_call(hand_out, out_shape=(out, out), in_specs=[any_spec] * 2, o...  0.99 us

profile of v24, /device:TPU:1, one launch (start us, length us, event | category | flops | bytes accessed | tf_op | source)
XLA Modules:
  0.0 21.1 jit_solution(1615632514279013892)
XLA Ops:
  0.6 19.4 %shard_map.95 = (f32[4,4,16,450]{3,2,1,0:T(8,128)S(1)}, f32[4,4,16,450]{3,2,1,0:T(8,128)S(1)}) custom-call(f32[4,4,16,450]{3,2,1,0:T(8,128)} %spread.1, f32[4,16,450]{2,1,0:T(8,128)} %east.1, f32[4,16,450]{2,1,0:T(8,128)} %north.1, s32[4,4,16]{2,1,0:T(4,128)} %rs.1, s32[4,4,450]{2,1,0:T(4,128)} %cs.1, s32[16]{0:T(128)} %cut.1, ...), custom_call_target="tpu_custom_call" | custom-call | flops 1000000000 | bytes 4000000 | tf_op jit(solution)/shard_map/pallas_call | solution.py:787
  20.1 1.0 %shard_map.96 = (f32[4,4,16,450]{3,2,1,0:T(8,128)}, f32[4,4,16,450]{3,2,1,0:T(8,128)}) custom-call(f32[4,4,16,450]{3,2,1,0:T(8,128)S(1)} %get-tuple-element.4.tan_in, f32[4,4,16,450]{3,2,1,0:T(8,128)S(1)} %get-tuple-element.5.diag_in), custom_call_target="tpu_custom_call" | custom-call | tf_op jit(solution)/shard_map/pallas_call | solution.py:832

commit v25 on v24

--- a/solution.py
+++ b/solution.py
@@ -184,6 +184,17 @@
     return pltpu.roll(x, shift % x.shape[axis], axis)
 
 
+def roll_blocks(x, shift):
+    return roll(x.reshape(x.shape[0] * x.shape[1], x.shape[2]), shift, 1).reshape(x.shape)
+
+
+def fold(x):
+    while x.shape[0] > 1:
+        half = x.shape[0] // 2
+        x = x[:half] + roll_blocks(x[half:], 2 * half)
+    return x
+
+
 def kernel(
     bands, spread, east, north, rs, cs, cut, metric, table_in, tan_out, diag_out,
     spread_v, winds_v, rs_v, cs_v, cut_s, hm, table,
@@ -296,13 +307,9 @@
     lane2 = lax.broadcasted_iota(jnp.int32, (1, 128), 1)
     for s, (start, shift) in enumerate(((0, 0), (384, COLS - 2 - 384))):
         ends = jnp.logical_and(lane2 >= shift, lane2 < shift + 2)
-        parts = [
-            roll(jnp.where(ends, grid[e, 8:24, start : start + 128], 0.0), 2 * e - shift, 1)
-            for e in range(PAIRS + 2 * LEV)
-        ]
-        while len(parts) > 1:
-            parts = [sum(parts[k : k + 2]) for k in range(0, len(parts), 2)]
-        halo_out[SIDES + s] = parts[0]
+        tile = jnp.where(ends, grid[:, 8:24, start : start + 128], 0.0)
+        packed = fold(tile[:PAIRS]) + roll_blocks(fold(tile[PAIRS:]), 2 * PAIRS)
+        halo_out[SIDES + s] = roll_blocks(packed, -shift)[0]
 
     def tendency_rows(h, l, at, half):
         lo = jnp.maximum(l - 1, 0)

time: 21.2 us -> 21.2 us (level)
  no operation moved by 1% of the time
where the time goes in v25:
time: 21.2 us; the launch traced here: 21.1 us
  Pallas kernels  20.5 us (97%)
  between operations  0.64 us (3%)
    pallas_call x1, Pallas kernels, per_device(): pl.pallas_call(functools.partial(kernel, bands), out_shape=(held, held),...  19.5 us
    pallas_call x1, Pallas kernels, per_device(): pl.pallas_call(hand_out, out_shape=(out, out), in_specs=[any_spec] * 2, o...  0.99 us

profile of v25, /device:TPU:1, one launch (start us, length us, event | category | flops | bytes accessed | tf_op | source)
XLA Modules:
  0.0 21.1 jit_solution(13595154476841439058)
XLA Ops:
  0.6 19.5 %shard_map.95 = (f32[4,4,16,450]{3,2,1,0:T(8,128)S(1)}, f32[4,4,16,450]{3,2,1,0:T(8,128)S(1)}) custom-call(f32[4,4,16,450]{3,2,1,0:T(8,128)} %spread.1, f32[4,16,450]{2,1,0:T(8,128)} %east.1, f32[4,16,450]{2,1,0:T(8,128)} %north.1, s32[4,4,16]{2,1,0:T(4,128)} %rs.1, s32[4,4,450]{2,1,0:T(4,128)} %cs.1, s32[16]{0:T(128)} %cut.1, ...), custom_call_target="tpu_custom_call" | custom-call | flops 1000000000 | bytes 4000000 | tf_op jit(solution)/shard_map/pallas_call | solution.py:794
  20.1 1.0 %shard_map.96 = (f32[4,4,16,450]{3,2,1,0:T(8,128)}, f32[4,4,16,450]{3,2,1,0:T(8,128)}) custom-call(f32[4,4,16,450]{3,2,1,0:T(8,128)S(1)} %get-tuple-element.4.tan_in, f32[4,4,16,450]{3,2,1,0:T(8,128)S(1)} %get-tuple-element.5.diag_in), custom_call_target="tpu_custom_call" | custom-call | tf_op jit(solution)/shard_map/pallas_call | solution.py:839

commit v26 on v24

--- a/solution.py
+++ b/solution.py
@@ -597,6 +597,13 @@
 
         yc[i] = cb[i]
 
+    def first_owner_step():
+        load_cut.wait()
+        load_others.wait()
+        own_rows(0)
+
+    pl.when(jnp.logical_and(polar, northern))(first_owner_step)
+
     from_west = roll(halo_in[SIDES], 126, 1)
     from_east = roll(halo_in[SIDES + 1], COLS - 384, 1)
     both = jnp.where(jnp.logical_and(lane2 >= 66, lane2 < 114), from_east, from_west)
@@ -609,11 +616,7 @@
     halo_copy(REST, 7, REST + 7 * slot_n, 1, nb, nl).start()
     halo_copy(REST + 7, 7, REST + 7 * slot_s, 1, sb, sl).start()
 
-    @pl.when(polar)
-    def _():
-        load_cut.wait()
-        load_others.wait()
-        own_rows(0)
+    pl.when(jnp.logical_and(polar, jnp.logical_not(northern)))(first_owner_step)
 
     @pl.when(jnp.logical_and(polar, northern))
     def _():

time: 21.2 us -> 21.1 us (level)
  no operation moved by 1% of the time
where the time goes in v26:
time: 21.1 us; the launch traced here: 21 us
  Pallas kernels  20.4 us (97%)
  between operations  0.64 us (3%)
    pallas_call x1, Pallas kernels, per_device(): pl.pallas_call(functools.partial(kernel, bands), out_shape=(held, held),...  19.4 us
    pallas_call x1, Pallas kernels, per_device(): pl.pallas_call(hand_out, out_shape=(out, out), in_specs=[any_spec] * 2, o...  0.99 us

profile of v26, /device:TPU:1, one launch (start us, length us, event | category | flops | bytes accessed | tf_op | source)
XLA Modules:
  0.0 21.0 jit_solution(17230314191837136659)
XLA Ops:
  0.6 19.4 %shard_map.95 = (f32[4,4,16,450]{3,2,1,0:T(8,128)S(1)}, f32[4,4,16,450]{3,2,1,0:T(8,128)S(1)}) custom-call(f32[4,4,16,450]{3,2,1,0:T(8,128)} %spread.1, f32[4,16,450]{2,1,0:T(8,128)} %east.1, f32[4,16,450]{2,1,0:T(8,128)} %north.1, s32[4,4,16]{2,1,0:T(4,128)} %rs.1, s32[4,4,450]{2,1,0:T(4,128)} %cs.1, s32[16]{0:T(128)} %cut.1, ...), custom_call_target="tpu_custom_call" | custom-call | flops 1000000000 | bytes 4000000 | tf_op jit(solution)/shard_map/pallas_call | solution.py:790
  20.0 1.0 %shard_map.96 = (f32[4,4,16,450]{3,2,1,0:T(8,128)}, f32[4,4,16,450]{3,2,1,0:T(8,128)}) custom-call(f32[4,4,16,450]{3,2,1,0:T(8,128)S(1)} %get-tuple-element.4.tan_in, f32[4,4,16,450]{3,2,1,0:T(8,128)S(1)} %get-tuple-element.5.diag_in), custom_call_target="tpu_custom_call" | custom-call | tf_op jit(solution)/shard_map/pallas_call | solution.py:835
